TPU v7x, 32 devices: a whole 2x2x4 slice. The times are simulated.
32 devices in a mesh: dp: 8 (over y, x, core), expert: 4 (over z).
Axes of the slice: x: 2, y: 2, z: 4, core: 2. Of those that a mesh axis runs over, the one named last changes fastest.
Arguments:
- tokens: bfloat16 [2, 4, 1024, 2048], P(None, 'expert', 'dp'), may hold values from -6 to 6
- segment_ids: int32 [2, 4, 1024], P(None, 'expert'), may hold values from 0 to 2, as said below
- attn_routes: int32 [2, 4, 1024, 2], P(None, 'expert', 'dp'), may hold values from 0 to 3, all different within a row; in each aligned block of 128 rows (0 to 127, 128 to 255, ..., all dimensions but the last counted through in order) at most 64 rows name the same one
- mlp_routes: int32 [2, 4, 1024, 2], P(None, 'expert', 'dp'), may hold values from 0 to 3, all different within a row; in each aligned block of 128 rows (0 to 127, 128 to 255, ..., all dimensions but the last counted through in order) at most 64 rows name the same one
- cotangent: bfloat16 [2, 4, 1024, 2048], P(None, 'expert', 'dp'), may hold values from -6 to 6
- attn_gain: bfloat16 [2048], P(('dp', 'expert')), may hold values from 0.099609375 to 1.8984375
- kv_weights: bfloat16 [2048, 2, 2048], P(('dp', 'expert')), may hold values from -0.125 to 0.125
- attn_router: bfloat16 [2048, 4], P(('dp', 'expert')), may hold values from -0.09375 to 0.09375
- query_maps: bfloat16 [4, 2048, 2048], P('expert', 'dp'), may hold values from -0.125 to 0.125
- output_maps: bfloat16 [4, 2048, 2048], P('expert', 'dp'), may hold values from -0.5 to 0.5
- mlp_gain: bfloat16 [2048], P(('dp', 'expert')), may hold values from 0.099609375 to 1.8984375
- mlp_router: bfloat16 [2048, 4], P(('dp', 'expert')), may hold values from -0.09375 to 0.09375
- gate_up: bfloat16 [4, 5632, 2, 2048], P('expert', 'dp'), may hold values from -0.125 to 0.125
- down_maps: bfloat16 [4, 5632, 2048], P('expert', 'dp'), may hold values from -0.078125 to 0.078125
Outputs:
- mixed: bfloat16 [2, 4, 1024, 2048], P(None, 'expert', 'dp')
- input_grad: float32 [2, 4, 1024, 2048], P(None, 'expert', 'dp')
- attn_gain_grad: float32 [2048], P(('dp', 'expert'))
- kv_grad: float32 [2048, 2, 2048], P(('dp', 'expert'))
- attn_router_grad: float32 [2048, 4], P(('dp', 'expert'))
- query_grad: float32 [4, 2048, 2048], P('expert', 'dp')
- output_grad: float32 [4, 2048, 2048], P('expert', 'dp')
- mlp_gain_grad: float32 [2048], P(('dp', 'expert'))
- mlp_router_grad: float32 [2048, 4], P(('dp', 'expert'))
- gate_up_grad: float32 [4, 5632, 2, 2048], P('expert', 'dp')
- down_grad: float32 [4, 5632, 2048], P('expert', 'dp')
Inputs may be any that keep to these rules, and one draw needn't show every extreme that they name: `attn_routes`: A token's two experts differ. Within the 1024 // 8 consecutive positions of one sequence that one device holds, every expert is named exactly 64 times. `mlp_routes`: A token's two experts differ. Within the 1024 // 8 consecutive positions of one sequence that one device holds, every expert is named exactly 64 times. `segment_ids`: each sequence holds three documents numbered 0, 1, 2 in order: 0 ends at a position from 32 to 64, 2 begins at a position from 960 to 992.
All inputs are finite; a program needn't handle non-finite values.
Results may differ from a plain program's by a relative error of at most 0.02.
Values may be sent and summed in bfloat16 or wider, within the bound.
No kernel may reach another device: no remote copies, remote signals or barrier semaphores. Data moves between devices by JAX's collectives and lax.ppermute only.
A program may use at most 640 MiB of HBM per device.

v0:
```python
import jax
import jax.numpy as jnp
from jax import lax
from jax.sharding import PartitionSpec as P

HEAD_WIDTH = 128


EPSILON = 1e-05
THETA_BASE = 10000.0
NEGATIVE = -1000000000.0
PRECISION_TOP = lax.Precision.HIGHEST


def rope_tables(positions, half_dim):
    frequency = THETA_BASE ** (-jnp.arange(half_dim, dtype=jnp.float32) / half_dim)
    angles = positions.astype(jnp.float32)[:, None] * frequency[None, :]
    return (jnp.cos(angles), jnp.sin(angles))


def rotate(values, cosine, sine_table):
    half_dim = values.shape[-1] // 2
    first_half = values[..., :half_dim]
    second_half = values[..., half_dim:]
    return jnp.concatenate(
        [
            first_half * cosine - second_half * sine_table,
            second_half * cosine + first_half * sine_table,
        ],
        axis=-1,
    )


def rotate_back(gradients, cosine, sine_table):
    half_dim = gradients.shape[-1] // 2
    first_half = gradients[..., :half_dim]
    second_half = gradients[..., half_dim:]
    return jnp.concatenate(
        [
            first_half * cosine + second_half * sine_table,
            second_half * cosine - first_half * sine_table,
        ],
        axis=-1,
    )


def norm_forward(values, gain_row):
    inverse = lax.rsqrt(jnp.mean(values * values, axis=-1, keepdims=True) + EPSILON)
    return (values * inverse * gain_row, inverse)


def norm_backward(values, inverse, gain_row, grad_normed):
    scaled = gain_row * grad_normed
    gain_term = jnp.sum(grad_normed * values * inverse, axis=0)
    grad_values = inverse * scaled - values * inverse**3 * jnp.mean(
        scaled * values, axis=-1, keepdims=True
    )
    return (grad_values, gain_term)


def route_onehot(routes, experts):
    return (routes[..., None] == jnp.arange(experts, dtype=jnp.int32)).astype(jnp.float32)


def gate_forward(logits, onehot):
    chosen = jnp.sum(logits[:, None, :] * onehot, axis=-1)
    return jax.nn.softmax(chosen, axis=-1)


def gate_backward(gate_probs, grad_gates, onehot):
    centered = gate_probs * (grad_gates - jnp.sum(gate_probs * grad_gates, axis=-1, keepdims=True))
    return jnp.sum(centered[..., None] * onehot, axis=1)


def dispatch_table(routes, experts, capacity):
    flat_routes = routes.reshape(-1)
    onehot = (flat_routes[:, None] == jnp.arange(experts, dtype=jnp.int32)[None, :]).astype(
        jnp.int32
    )
    slot_rank = jnp.sum((jnp.cumsum(onehot, axis=0) - 1) * onehot, axis=1)
    column = flat_routes * capacity + slot_rank
    return (column[:, None] == jnp.arange(experts * capacity, dtype=jnp.int32)[None, :]).astype(
        jnp.bfloat16
    )


def pack_rows(slot_table, pair_rows):
    return jnp.einsum(
        "pc,pd->cd", slot_table, pair_rows, preferred_element_type=jnp.float32
    ).astype(jnp.bfloat16)


def unpack_narrow(slot_table, buffer):
    return jnp.dot(slot_table, buffer, preferred_element_type=jnp.float32)


def unpack_wide(slot_table, buffer):
    return jnp.dot(slot_table.astype(jnp.float32), buffer, precision=PRECISION_TOP)


def to_experts(buffer):
    return lax.all_to_all(buffer, "expert", split_axis=0, concat_axis=0, tiled=True)


def back_home(buffer):
    return lax.all_to_all(buffer, "expert", split_axis=0, concat_axis=0, tiled=True)


def grads_home(buffer):
    return lax.all_to_all(
        buffer.astype(jnp.bfloat16), "expert", split_axis=0, concat_axis=0, tiled=True
    ).astype(buffer.dtype)


def attention_scores(query_vectors, key_matrix_rows, key_mask, score_scale):
    score_matrix = (
        jnp.einsum(
            "slkhd,smhd->skhlm", query_vectors, key_matrix_rows, preferred_element_type=jnp.float32
        )
        * score_scale
    )
    return jnp.where(key_mask[:, None, None], score_matrix, NEGATIVE)


def per_device(
    tokens,
    segment_ids,
    attn_routes,
    mlp_routes,
    cotangent,
    attn_gain,
    kv_weights,
    attn_router,
    query_maps,
    output_maps,
    mlp_gain,
    mlp_router,
    gate_up,
    down_maps,
):
    micro_count, seq_count, local_len, model_width = tokens.shape
    length = segment_ids.shape[2]
    experts = attn_router.shape[1]
    row_count = seq_count * local_len
    capacity = 2 * row_count // experts
    head_count = model_width // HEAD_WIDTH
    score_scale = HEAD_WIDTH ** (-0.5)
    first_pos = lax.axis_index("dp") * local_len
    local_pos = first_pos + jnp.arange(local_len, dtype=jnp.int32)
    key_pos = jnp.arange(length, dtype=jnp.int32)
    cosine, sine_table = rope_tables(jnp.tile(local_pos, seq_count), HEAD_WIDTH // 2)
    shared = (
        lax.all_gather(kv_weights, ("dp", "expert"), axis=0, tiled=True),
        lax.all_gather(attn_gain, ("dp", "expert"), axis=0, tiled=True),
        lax.all_gather(mlp_gain, ("dp", "expert"), axis=0, tiled=True),
        lax.all_gather(attn_router, ("dp", "expert"), axis=0, tiled=True),
        lax.all_gather(mlp_router, ("dp", "expert"), axis=0, tiled=True),
    )
    expert_full = (
        lax.all_gather(query_maps[0], "dp", axis=0, tiled=True),
        lax.all_gather(output_maps[0], "dp", axis=0, tiled=True),
        lax.all_gather(gate_up[0], "dp", axis=0, tiled=True),
        lax.all_gather(down_maps[0], "dp", axis=0, tiled=True),
    )
    held_weights = shared + expert_full
    mixed_parts = []
    input_parts = []
    attn_rows_list = []
    grad_query_list = []
    context_rows_list = []
    grad_attn_list = []
    mlp_rows_list = []
    grad_gate_list = []
    grad_up_list = []
    hidden_list = []
    grad_mlp_list = []
    normed_list = []
    grad_kv_list = []
    mlp_low_list = []
    logit_attn_list = []
    logit_mlp_list = []
    gain_one_sum = jnp.zeros((model_width,), jnp.float32)
    gain_two_sum = jnp.zeros((model_width,), jnp.float32)
    for micro_idx in range(micro_count):
        current = held_weights
        (
            kv_full,
            gain_attn,
            gain_mlp,
            router_attn,
            router_mlp,
            query_full,
            output_full,
            gate_up_full,
            down_full,
        ) = current
        kv_matrix = kv_full.reshape(model_width, 2 * model_width)
        inputs = tokens[micro_idx].reshape(row_count, model_width).astype(jnp.float32)
        seg_full = segment_ids[micro_idx]
        seg_query = lax.dynamic_slice_in_dim(seg_full, first_pos, local_len, axis=1)
        key_mask = (key_pos[None, None, :] <= local_pos[None, :, None]) & (
            seg_query[:, :, None] == seg_full[:, None, :]
        )
        route_attn = attn_routes[micro_idx].reshape(row_count, 2)
        route_mlp = mlp_routes[micro_idx].reshape(row_count, 2)
        onehot_attn = route_onehot(route_attn, experts)
        onehot_mlp = route_onehot(route_mlp, experts)
        table_attn = dispatch_table(route_attn, experts, capacity)
        table_mlp = dispatch_table(route_mlp, experts, capacity)
        normed_one, inverse_one = norm_forward(inputs, gain_attn.astype(jnp.float32))
        normed_low = normed_one.astype(jnp.bfloat16)
        gates_attn = gate_forward(
            jnp.dot(normed_low, router_attn, preferred_element_type=jnp.float32), onehot_attn
        )
        kv_proj = jnp.dot(normed_low, kv_matrix, preferred_element_type=jnp.float32)
        keys_local = rotate(
            kv_proj[:, :model_width].reshape(row_count, head_count, HEAD_WIDTH),
            cosine[:, None],
            sine_table[:, None],
        ).astype(jnp.bfloat16)
        values_local = kv_proj[:, model_width:].astype(jnp.bfloat16)
        keys_all, values_all = (
            lax.all_gather(
                keys_local.reshape(seq_count, local_len, model_width), "dp", axis=1, tiled=True
            ),
            lax.all_gather(
                values_local.reshape(seq_count, local_len, model_width), "dp", axis=1, tiled=True
            ),
        )
        keys_all = keys_all.reshape(seq_count, length, head_count, HEAD_WIDTH)
        values_all = values_all.reshape(seq_count, length, head_count, HEAD_WIDTH)
        attn_rows = to_experts(pack_rows(table_attn, jnp.repeat(normed_low, 2, axis=0)))
        query_rows = jnp.dot(attn_rows, query_full, preferred_element_type=jnp.float32).astype(
            jnp.bfloat16
        )
        query_raw = unpack_narrow(table_attn, back_home(query_rows)).reshape(
            row_count, 2, head_count, HEAD_WIDTH
        )
        query_vectors = rotate(query_raw, cosine[:, None, None], sine_table[:, None, None]).astype(
            jnp.bfloat16
        )
        query_vectors = query_vectors.reshape(seq_count, local_len, 2, head_count, HEAD_WIDTH)
        score_matrix = attention_scores(query_vectors, keys_all, key_mask, score_scale)
        row_top = jnp.max(score_matrix, axis=-1, keepdims=True)
        exponent = jnp.exp(score_matrix - row_top)
        row_total = jnp.sum(exponent, axis=-1, keepdims=True)
        log_total = row_top + jnp.log(row_total)
        attention_weights = (exponent / row_total).astype(jnp.bfloat16)
        context = jnp.einsum(
            "skhlm,smhd->slkhd", attention_weights, values_all, preferred_element_type=jnp.float32
        )
        context_rows = to_experts(
            pack_rows(table_attn, context.reshape(row_count * 2, model_width).astype(jnp.bfloat16))
        )
        attn_out_rows = jnp.dot(
            context_rows, output_full, preferred_element_type=jnp.float32
        ).astype(jnp.bfloat16)
        attn_back = unpack_narrow(table_attn, back_home(attn_out_rows)).reshape(
            row_count, 2, model_width
        )
        hidden_state = inputs + jnp.sum(gates_attn[..., None] * attn_back, axis=1)
        normed_two, inverse_two = norm_forward(hidden_state, gain_mlp.astype(jnp.float32))
        mlp_low = normed_two.astype(jnp.bfloat16)
        gates_mlp = gate_forward(
            jnp.dot(mlp_low, router_mlp, preferred_element_type=jnp.float32), onehot_mlp
        )
        mlp_rows = to_experts(pack_rows(table_mlp, jnp.repeat(mlp_low, 2, axis=0)))
        gate_up_rows = jnp.einsum(
            "rd,fcd->rcf", mlp_rows, gate_up_full, preferred_element_type=jnp.float32
        )
        gate_val = gate_up_rows[:, 0]
        up_val = gate_up_rows[:, 1]
        hidden_rows = (jax.nn.silu(gate_val) * up_val).astype(jnp.bfloat16)
        mlp_out_rows = jnp.dot(hidden_rows, down_full, preferred_element_type=jnp.float32).astype(
            jnp.bfloat16
        )
        mlp_back = unpack_narrow(table_mlp, back_home(mlp_out_rows)).reshape(
            row_count, 2, model_width
        )
        result = hidden_state + jnp.sum(gates_mlp[..., None] * mlp_back, axis=1)
        mixed_parts.append(result.astype(jnp.bfloat16).reshape(seq_count, local_len, model_width))
        current = held_weights
        (
            kv_full,
            gain_attn,
            gain_mlp,
            router_attn,
            router_mlp,
            query_full,
            output_full,
            gate_up_full,
            down_full,
        ) = current
        kv_matrix = kv_full.reshape(model_width, 2 * model_width)
        grad_out = cotangent[micro_idx].reshape(row_count, model_width).astype(jnp.float32)
        grad_logits_mlp = gate_backward(
            gates_mlp, jnp.sum(grad_out[:, None, :] * mlp_back, axis=-1), onehot_mlp
        )
        grad_mlp_pairs = (
            (gates_mlp[..., None] * grad_out[:, None, :])
            .astype(jnp.bfloat16)
            .reshape(row_count * 2, model_width)
        )
        grad_mlp_rows = to_experts(pack_rows(table_mlp, grad_mlp_pairs))
        grad_hidden = jnp.einsum(
            "rd,fd->rf", grad_mlp_rows, down_full, preferred_element_type=jnp.float32
        )
        sigmoid = jax.nn.sigmoid(gate_val)
        grad_gate = (grad_hidden * up_val * sigmoid * (1.0 + gate_val * (1.0 - sigmoid))).astype(
            jnp.bfloat16
        )
        grad_up = (grad_hidden * gate_val * sigmoid).astype(jnp.bfloat16)
        grad_input_rows = jnp.einsum(
            "rcf,fcd->rd",
            jnp.stack([grad_gate, grad_up], axis=1),
            gate_up_full,
            preferred_element_type=jnp.float32,
        )
        grad_input_mlp = unpack_wide(table_mlp, grads_home(grad_input_rows)).reshape(
            row_count, 2, model_width
        )
        grad_normed_two = jnp.sum(grad_input_mlp, axis=1) + jnp.einsum(
            "re,de->rd", grad_logits_mlp, router_mlp.astype(jnp.float32), precision=PRECISION_TOP
        )
        grad_state_part, gain_two_term = norm_backward(
            hidden_state, inverse_two, gain_mlp.astype(jnp.float32), grad_normed_two
        )
        grad_state = grad_out + grad_state_part
        grad_logits_attn = gate_backward(
            gates_attn, jnp.sum(grad_state[:, None, :] * attn_back, axis=-1), onehot_attn
        )
        grad_attn_pairs = (
            (gates_attn[..., None] * grad_state[:, None, :])
            .astype(jnp.bfloat16)
            .reshape(row_count * 2, model_width)
        )
        grad_attn_rows = to_experts(pack_rows(table_attn, grad_attn_pairs))
        grad_context_rows = jnp.einsum(
            "rd,cd->rc", grad_attn_rows, output_full, preferred_element_type=jnp.float32
        )
        grad_context = unpack_wide(table_attn, grads_home(grad_context_rows)).astype(jnp.bfloat16)
        grad_context = grad_context.reshape(seq_count, local_len, 2, head_count, HEAD_WIDTH)
        score_matrix = attention_scores(query_vectors, keys_all, key_mask, score_scale)
        probs_full = jnp.exp(score_matrix - log_total)
        probs_low = probs_full.astype(jnp.bfloat16)
        grad_probs = jnp.einsum(
            "slkhd,smhd->skhlm", grad_context, values_all, preferred_element_type=jnp.float32
        )
        grad_scores = (
            probs_full * (grad_probs - jnp.sum(probs_full * grad_probs, axis=-1, keepdims=True))
        ).astype(jnp.bfloat16)
        grad_queries = (
            jnp.einsum(
                "skhlm,smhd->slkhd", grad_scores, keys_all, preferred_element_type=jnp.float32
            )
            * score_scale
        )
        count = local_len * lax.axis_size("dp")
        grad_keys = (
            jnp.einsum(
                "skhlm,slkhd->mshd", grad_scores, query_vectors, preferred_element_type=jnp.float32
            )
            * score_scale
        )
        grad_values = jnp.einsum(
            "skhlm,slkhd->mshd", probs_low, grad_context, preferred_element_type=jnp.float32
        )
        key_grad = lax.psum_scatter(
            jnp.stack(
                [
                    grad_keys.reshape(count, seq_count, model_width),
                    grad_values.reshape(count, seq_count, model_width),
                ],
                axis=2,
            ).astype(jnp.bfloat16),
            "dp",
            scatter_dimension=0,
            tiled=True,
        ).astype(jnp.float32)
        key_grad = jnp.transpose(key_grad, (1, 0, 2, 3)).reshape(row_count, 2, model_width)
        grad_keys_raw = rotate_back(
            key_grad[:, 0].reshape(row_count, head_count, HEAD_WIDTH),
            cosine[:, None],
            sine_table[:, None],
        )
        grad_kv = jnp.concatenate(
            [grad_keys_raw.reshape(row_count, model_width), key_grad[:, 1]], axis=1
        ).astype(jnp.bfloat16)
        grad_query_raw = rotate_back(
            grad_queries.reshape(row_count, 2, head_count, HEAD_WIDTH),
            cosine[:, None, None],
            sine_table[:, None, None],
        )
        grad_query_rows = to_experts(
            pack_rows(
                table_attn, grad_query_raw.astype(jnp.bfloat16).reshape(row_count * 2, model_width)
            )
        )
        grad_normed_rows = jnp.einsum(
            "rc,dc->rd", grad_query_rows, query_full, preferred_element_type=jnp.float32
        )
        grad_normed_experts = unpack_wide(table_attn, grads_home(grad_normed_rows)).reshape(
            row_count, 2, model_width
        )
        grad_normed_one = (
            jnp.sum(grad_normed_experts, axis=1)
            + jnp.einsum("re,de->rd", grad_kv, kv_matrix, preferred_element_type=jnp.float32)
            + jnp.einsum(
                "re,de->rd",
                grad_logits_attn,
                router_attn.astype(jnp.float32),
                precision=PRECISION_TOP,
            )
        )
        grad_inputs_part, gain_one_term = norm_backward(
            inputs, inverse_one, gain_attn.astype(jnp.float32), grad_normed_one
        )
        input_parts.append(
            (grad_state + grad_inputs_part).reshape(seq_count, local_len, model_width)
        )
        gain_one_sum = gain_one_sum + gain_one_term
        gain_two_sum = gain_two_sum + gain_two_term
        attn_rows_list.append(attn_rows)
        grad_query_list.append(grad_query_rows)
        context_rows_list.append(context_rows)
        grad_attn_list.append(grad_attn_rows)
        mlp_rows_list.append(mlp_rows)
        grad_gate_list.append(grad_gate)
        grad_up_list.append(grad_up)
        hidden_list.append(hidden_rows)
        grad_mlp_list.append(grad_mlp_rows)
        normed_list.append(normed_low)
        grad_kv_list.append(grad_kv)
        mlp_low_list.append(mlp_low)
        logit_attn_list.append(grad_logits_attn)
        logit_mlp_list.append(grad_logits_mlp)
    attn_rows_all = jnp.concatenate(attn_rows_list, axis=0)
    grad_query_all = jnp.concatenate(grad_query_list, axis=0)
    context_all = jnp.concatenate(context_rows_list, axis=0)
    grad_attn_all = jnp.concatenate(grad_attn_list, axis=0)
    mlp_rows_all = jnp.concatenate(mlp_rows_list, axis=0)
    grad_gate_all = jnp.concatenate(grad_gate_list, axis=0)
    grad_up_all = jnp.concatenate(grad_up_list, axis=0)
    hidden_all = jnp.concatenate(hidden_list, axis=0)
    grad_mlp_all = jnp.concatenate(grad_mlp_list, axis=0)
    normed_all = jnp.concatenate(normed_list, axis=0)
    grad_kv_all = jnp.concatenate(grad_kv_list, axis=0)
    mlp_low_all = jnp.concatenate(mlp_low_list, axis=0)
    logit_attn_all = jnp.concatenate(logit_attn_list, axis=0)
    logit_mlp_all = jnp.concatenate(logit_mlp_list, axis=0)
    query_term = jnp.einsum(
        "rc,rd->cd", attn_rows_all, grad_query_all, preferred_element_type=jnp.float32
    )
    output_term = jnp.einsum(
        "rc,rd->cd", context_all, grad_attn_all, preferred_element_type=jnp.float32
    )
    map_grad = lax.psum_scatter(
        jnp.stack([query_term, output_term], axis=1).astype(jnp.bfloat16),
        "dp",
        scatter_dimension=0,
        tiled=True,
    ).astype(jnp.float32)
    gate_term = jnp.einsum(
        "rf,rd->fd", grad_gate_all, mlp_rows_all, preferred_element_type=jnp.float32
    )
    up_term = jnp.einsum("rf,rd->fd", grad_up_all, mlp_rows_all, preferred_element_type=jnp.float32)
    down_term = jnp.einsum(
        "rf,rd->fd", hidden_all, grad_mlp_all, preferred_element_type=jnp.float32
    )
    mlp_grad = lax.psum_scatter(
        jnp.stack([gate_term, up_term, down_term], axis=1).astype(jnp.bfloat16),
        "dp",
        scatter_dimension=0,
        tiled=True,
    ).astype(jnp.float32)
    kv_grad = lax.psum_scatter(
        jnp.einsum(
            "rc,re->ce", normed_all, grad_kv_all, preferred_element_type=jnp.float32
        ).reshape(kv_weights.shape[0] * lax.axis_size(("dp", "expert")), 2, model_width),
        ("dp", "expert"),
        scatter_dimension=0,
        tiled=True,
    )
    router_attn_term = jnp.einsum(
        "rd,re->de", normed_all.astype(jnp.float32), logit_attn_all, precision=PRECISION_TOP
    )
    router_mlp_term = jnp.einsum(
        "rd,re->de", mlp_low_all.astype(jnp.float32), logit_mlp_all, precision=PRECISION_TOP
    )
    gain_attn_grad, gain_mlp_grad, router_attn_grad, router_mlp_grad = (
        lax.psum_scatter(gain_one_sum, ("dp", "expert"), scatter_dimension=0, tiled=True),
        lax.psum_scatter(gain_two_sum, ("dp", "expert"), scatter_dimension=0, tiled=True),
        lax.psum_scatter(router_attn_term, ("dp", "expert"), scatter_dimension=0, tiled=True),
        lax.psum_scatter(router_mlp_term, ("dp", "expert"), scatter_dimension=0, tiled=True),
    )
    return (
        jnp.stack(mixed_parts, axis=0),
        jnp.stack(input_parts, axis=0),
        gain_attn_grad,
        kv_grad,
        router_attn_grad,
        map_grad[:, 0][None],
        map_grad[:, 1][None],
        gain_mlp_grad,
        router_mlp_grad,
        mlp_grad[:, :2][None],
        mlp_grad[:, 2][None],
    )


def solution(mesh):
    in_specs = (
        P(None, "expert", "dp", None),
        P(None, "expert", None),
        P(None, "expert", "dp", None),
        P(None, "expert", "dp", None),
        P(None, "expert", "dp", None),
        P(("dp", "expert")),
        P(("dp", "expert"), None, None),
        P(("dp", "expert"), None),
        P("expert", "dp", None),
        P("expert", "dp", None),
        P(("dp", "expert")),
        P(("dp", "expert"), None),
        P("expert", "dp", None, None),
        P("expert", "dp", None),
    )
    out_specs = (
        P(None, "expert", "dp", None),
        P(None, "expert", "dp", None),
        P(("dp", "expert")),
        P(("dp", "expert"), None, None),
        P(("dp", "expert"), None),
        P("expert", "dp", None),
        P("expert", "dp", None),
        P(("dp", "expert")),
        P(("dp", "expert"), None),
        P("expert", "dp", None, None),
        P("expert", "dp", None),
    )
    return jax.shard_map(
        per_device, mesh=mesh, in_specs=in_specs, out_specs=out_specs, check_vma=False
    )
```

profile of v0, /device:TPU:8, one launch (start us, length us, event | category | flops | bytes accessed | tf_op | source)
XLA Modules:
  0.0 2724.4 jit_solution(18306014615521503238)
XLA Ops:
  10.4 41.9 %all-reduce.6 = (bf16[2048]{0:T(1024)(128)(2,1)S(1)}, bf16[2048]{0:T(1024)(128)(2,1)}) all-reduce(bf16[2048]{0:T(1024)(128)(2,1)S(1)} %dynamic-update-slice, bf16[2048]{0:T(1024)(128)(2,1)S(1)} %dynamic-update-slice.1), channel_id=1, replica_groups=mesh['dp'=8,'expert'=4] {'dp','expert'}, use_global_device_ids=true, to_apply=%add | all-reduce | flops 4096 | bytes 16384
  54.1 73.2 %all-gather.18.cloned.1.call-done = bf16[2048,2,2048]{2,1,0:T(2,128)(2,1)} async-done(((bf16[64,2,2048]{2,1,0:T(2,128)(2,1)}), bf16[2048,2,2048]{2,1,0:T(2,128)(2,1)}) %all-gather.18.cloned.1.call-update) | async-done | bytes 16777232 | tf_op jit(solution)/shard_map/all_gather | solution.py:153
  156.7 29.0 %all_to_all.288 = bf16[4,64,2048]{2,1,0:T(8,128)(2,1)S(1)} all-to-all(bf16[4,64,2048]{2,1,0:T(8,128)(2,1)S(1)} %bitcast.762), channel_id=1, replica_groups=mesh['dp'=8,'expert'=4] {'expert'}, dimensions={0} | all-to-all | bytes 2097152 | tf_op jit(solution)/shard_map/all_to_all | solution.py:102
  198.9 21.7 all-to-all-done.1
  229.9 32.0 %all-gather.20.cloned.1.call-done = bf16[1,1024,2048]{1,2,0:T(8,128)(2,1)} async-done(((bf16[1,128,2048]{1,2,0:T(8,128)(2,1)}), bf16[1,1024,2048]{1,2,0:T(8,128)(2,1)}) %all-gather.20.cloned.1.call-update) | async-done | bytes 4194320 | tf_op jit(solution)/shard_map/all_gather | solution.py:223
  347.8 78.2 %all-gather.6 = bf16[32,64,4]{1,2,0:T(4,128)(2,1)S(1)} all-gather(bf16[1,64,4]{1,2,0:T(4,128)(2,1)} %bitcast.816), channel_id=1, replica_groups=mesh['dp'=8,'expert'=4] {'dp','expert'}, dimensions={0}, use_global_device_ids=true | all-gather | bytes 16896 | tf_op jit(solution)/shard_map/all_gather | solution.py:156
  460.9 26.2 all_to_all.289
  580.2 79.2 %all-gather.7 = bf16[32,64,4]{1,2,0:T(4,128)(2,1)S(1)} all-gather(bf16[1,64,4]{1,2,0:T(4,128)(2,1)S(1)} %bitcast.817), channel_id=1, replica_groups=mesh['dp'=8,'expert'=4] {'dp','expert'}, dimensions={0}, use_global_device_ids=true | all-gather | bytes 16896 | tf_op jit(solution)/shard_map/all_gather | solution.py:157
  755.6 22.4 fusion.26
  783.9 26.4 fusion.29
  815.7 37.4 %all-gather.32.cloned.1.call-done = bf16[1,5632,2048]{2,1,0:T(8,128)(2,1)} async-done(((bf16[1,704,2048]{2,1,0:T(8,128)(2,1)}), bf16[1,5632,2048]{2,1,0:T(8,128)(2,1)}) %all-gather.32.cloned.1.call-update) | async-done | bytes 23068688 | tf_op jit(solution)/shard_map/all_gather | solution.py:163
  853.0 24.9 multiply_convert_fusion.3
  896.7 25.0 multiply_convert_fusion.1
  1035.5 29.4 %all_to_all.290 = bf16[4,64,2048]{2,1,0:T(8,128)(2,1)S(1)} all-to-all(bf16[4,64,2048]{2,1,0:T(8,128)(2,1)S(1)} %bitcast.767), channel_id=1, replica_groups=mesh['dp'=8,'expert'=4] {'expert'}, dimensions={0} | all-to-all | bytes 2097152 | tf_op jit(solution)/shard_map/all_to_all | solution.py:102
  1077.4 21.5 all-to-all-done.15
  1172.9 30.0 %all_to_all.291 = bf16[4,64,2048]{2,1,0:T(8,128)(2,1)S(1)} all-to-all(bf16[4,64,2048]{2,1,0:T(8,128)(2,1)S(1)} %bitcast.768), channel_id=1, replica_groups=mesh['dp'=8,'expert'=4] {'expert'}, dimensions={0} | all-to-all | bytes 2097152 | tf_op jit(solution)/shard_map/all_to_all | solution.py:102
  1215.5 21.6 all-to-all-done.21
  1426.6 42.6 %reshape.1493 = f32[2048,2,2048]{2,1,0:T(2,128)} reshape(f32[2048,4096]{1,0:T(8,128)} %fusion.151) | data formatting | bytes 67108864 | tf_op jit(solution)/shard_map/reshape | solution.py:479
  1526.5 45.9 %pad_maximum_fusion = bf16[5632,3,2048]{2,0,1:T(8,128)(2,1)} fusion(bf16[5632,1,2048]{2,0,1:T(8,128)(2,1)} %convert_bitcast_fusion, bf16[5632,1,2048]{2,0,1:T(8,128)(2,1)} %convert_bitcast_fusion.1, bf16[5632,1,2048]{2,0,1:T(8,128)(2,1)} %convert_bitcast_fusion.2), kind=kLoop, calls=%fused_computation | loop fusion | flops 69206016 | bytes 138412032 | tf_op jit(solution)/shard_map/stack | solution.py:471
  1624.5 23.7 reduce-scatter.25.cloned.1.call-done
  1690.4 40.4 %all-reduce.5 = (f32[2048]{0:T(1024)S(1)}, f32[2048]{0:T(1024)S(1)}) all-reduce(f32[2048]{0:T(1024)S(1)} %add.288, f32[2048]{0:T(1024)S(1)} %add.289), channel_id=10, replica_groups=mesh['dp'=8,'expert'=4] {'dp','expert'}, use_global_device_ids=true, to_apply=%region_62.63.clone | all-reduce | flops 4096 | bytes 32768
  1735.7 33.5 %reduce-scatter.15.cloned.1.call-done = bf16[256,2,2048]{2,0,1:T(8,128)(2,1)} async-done(((bf16[2048,2,2048]{2,0,1:T(8,128)(2,1)}), bf16[256,2,2048]{2,0,1:T(8,128)(2,1)}) %reduce-scatter.15.cloned.1.call-update) | async-done | bytes 2097168 | tf_op jit(solution)/shard_map/reduce_scatter | solution.py:457
  1773.6 500.3 %all-reduce.9.cloned.1.call-done = f32[2048,2,2048]{2,1,0:T(2,128)} async-done(((f32[2048,2,2048]{2,1,0:T(2,128)}), f32[2048,2,2048]{2,1,0:T(2,128)}) %all-reduce.9.cloned.1.call-update) | async-done | bytes 33554448
  2276.2 396.1 %reduce-scatter.17.cloned.1.call-done = bf16[704,3,2048]{2,0,1:T(8,128)(2,1)} async-done(((bf16[5632,3,2048]{2,0,1:T(8,128)(2,1)}), bf16[704,3,2048]{2,0,1:T(8,128)(2,1)}) %reduce-scatter.17.cloned.1.call-update) | async-done | bytes 8650768 | tf_op jit(solution)/shard_map/reduce_scatter | solution.py:470
  (728 shorter events, 1005.1 us)
Async XLA Ops:
  7.2 120.2 %all-gather.18.cloned.1.call-start = ((), (), s32[]{:S(2)}) async-start(), calls=%async_computation.30 | async-start | bytes 17301504 | tf_op jit(solution)/shard_map/all_gather | solution.py:153
  7.9 177.7 %all-gather.26.cloned.1.call-start = ((), (), s32[]{:S(2)}) async-start(), calls=%async_computation.36 | async-start | bytes 9437184 | tf_op jit(solution)/shard_map/all_gather | solution.py:160
  8.7 215.3 %all-gather.24.cloned.1.call-start = ((), (), s32[]{:S(2)}) async-start(), calls=%async_computation.35 | async-start | bytes 4718592 | tf_op jit(solution)/shard_map/all_gather | solution.py:226
  146.8 115.2 %all-gather.20.cloned.1.call-start = ((), (), s32[]{:S(2)}) async-start(), calls=%async_computation.31 | async-start | bytes 4718592 | tf_op jit(solution)/shard_map/all_gather | solution.py:223
  150.2 167.9 %all-gather.28.cloned.1.call-start = ((), (), s32[]{:S(2)}) async-start(), calls=%async_computation.37 | async-start | bytes 9437184 | tf_op jit(solution)/shard_map/all_gather | solution.py:161
  296.2 37.8 %all-to-all-start.2 = ((bf16[4,64,2048]{2,1,0:T(8,128)(2,1)}), bf16[4,64,2048]{2,1,0:T(8,128)(2,1)S(1)}, u32[]{:S(2)}, u32[]{:S(2)}) async-start(bf16[4,64,2048]{2,1,0:T(8,128)(2,1)} %bitcast.28), calls=%async_computation.2 | async-start | bytes 2097152 | tf_op jit(solution)/shard_map/all_to_all | solution.py:102
  341.1 85.6 %all-to-all-start.3 = ((bf16[4,64,2048]{2,1,0:T(8,128)(2,1)}), bf16[4,64,2048]{2,1,0:T(8,128)(2,1)S(1)}, u32[]{:S(2)}, u32[]{:S(2)}) async-start(bf16[4,64,2048]{2,1,0:T(8,128)(2,1)} %bitcast.798), calls=%async_computation.3 | async-start | bytes 2097152 | tf_op jit(solution)/shard_map/all_to_all | solution.py:106
  347.8 178.3 %all-gather.34.cloned.1.call-start = ((), (), s32[]{:S(2)}) async-start(), calls=%async_computation.40 | async-start | bytes 4718592 | tf_op jit(solution)/shard_map/all_gather | solution.py:226
  440.7 92.8 %all-gather.22.cloned.1.call-start = ((), (), s32[]{:S(2)}) async-start(), calls=%async_computation.32 | async-start | bytes 4718592 | tf_op jit(solution)/shard_map/all_gather | solution.py:223
  444.4 311.2 %all-gather.30.cloned.1.call-start = ((), (), s32[]{:S(2)}) async-start(), calls=%async_computation.38 | async-start | bytes 51904512 | tf_op jit(solution)/shard_map/all_gather | solution.py:162
  452.2 400.8 %all-gather.32.cloned.1.call-start = ((), (), s32[]{:S(2)}) async-start(), calls=%async_computation.39 | async-start | bytes 25952256 | tf_op jit(solution)/shard_map/all_gather | solution.py:163
  571.0 108.7 %all-to-all-start.8 = ((bf16[4,64,2048]{2,1,0:T(8,128)(2,1)}), bf16[4,64,2048]{2,1,0:T(8,128)(2,1)}, u32[]{:S(2)}, u32[]{:S(2)}) async-start(bf16[4,64,2048]{2,1,0:T(8,128)(2,1)} %bitcast.755), calls=%async_computation.8 | async-start | bytes 2097152 | tf_op jit(solution)/shard_map/all_to_all | solution.py:102
  778.0 32.3 %all-to-all-start.12 = ((bf16[4,64,2048]{2,1,0:T(8,128)(2,1)}), bf16[4,64,2048]{2,1,0:T(8,128)(2,1)S(1)}, u32[]{:S(2)}, u32[]{:S(2)}) async-start(bf16[4,64,2048]{2,1,0:T(8,128)(2,1)} %bitcast.100), calls=%async_computation.12 | async-start | bytes 2097152 | tf_op jit(solution)/shard_map/all_to_all | solution.py:102
  810.3 81.2 %all-to-all-start.18 = ((bf16[4,64,2048]{2,1,0:T(8,128)(2,1)}), bf16[4,64,2048]{2,1,0:T(8,128)(2,1)S(1)}, u32[]{:S(2)}, u32[]{:S(2)}) async-start(bf16[4,64,2048]{2,1,0:T(8,128)(2,1)} %bitcast.146), calls=%async_computation.18 | async-start | bytes 2097152 | tf_op jit(solution)/shard_map/all_to_all | solution.py:102
  891.6 43.7 %all-to-all-start.5 = ((bf16[4,64,2048]{2,1,0:T(8,128)(2,1)}), bf16[4,64,2048]{2,1,0:T(8,128)(2,1)S(1)}, u32[]{:S(2)}, u32[]{:S(2)}) async-start(bf16[4,64,2048]{2,1,0:T(8,128)(2,1)} %bitcast.48), calls=%async_computation.5 | async-start | bytes 2097152 | tf_op jit(solution)/shard_map/all_to_all | solution.py:106
  1077.3 312.4 %reduce-scatter.19.cloned.1.call-start = ((), (), s32[]{:S(2)}) async-start(), calls=%async_computation.41 | async-start | bytes 9437184
  1215.5 179.9 %reduce-scatter.21.cloned.1.call-start = ((), (), s32[]{:S(2)}) async-start(), calls=%async_computation.42 | async-start | bytes 9437184
  1354.1 269.0 %reduce-scatter.23.cloned.1.call-start = ((), (), s32[]{:S(2)}) async-start(), calls=%async_computation.43 | async-start | bytes 1081344
  1356.4 291.8 %reduce-scatter.25.cloned.1.call-start = ((), (), s32[]{:S(2)}) async-start(), calls=%async_computation.44 | async-start | bytes 1081344
  1358.7 410.5 %reduce-scatter.15.cloned.1.call-start = ((), (), s32[]{:S(2)}) async-start(), calls=%async_computation.33 | async-start | bytes 18874368 | tf_op jit(solution)/shard_map/reduce_scatter | solution.py:457
  1389.4 884.5 %all-reduce.9.cloned.1.call-start = ((), (), s32[]{:S(2)}) async-start(), calls=%async_computation.45 | async-start | bytes 67108864
  1469.3 1203.0 %reduce-scatter.17.cloned.1.call-start = ((), (), s32[]{:S(2)}) async-start(), calls=%async_computation.34 | async-start | bytes 77856768 | tf_op jit(solution)/shard_map/reduce_scatter | solution.py:470
  1579.5 33.1 %all-to-all-start.23 = ((bf16[4,64,2048]{2,1,0:T(8,128)(2,1)}), bf16[4,64,2048]{2,1,0:T(8,128)(2,1)}, u32[]{:S(2)}, u32[]{:S(2)}) async-start(bf16[4,64,2048]{2,1,0:T(8,128)(2,1)} %bitcast.171), calls=%async_computation.23 | async-start | bytes 2097152 | tf_op jit(solution)/shard_map/all_to_all | solution.py:110
  1612.5 39.8 %all-to-all-start.17 = ((bf16[4,64,2048]{2,1,0:T(8,128)(2,1)}), bf16[4,64,2048]{2,1,0:T(8,128)(2,1)}, u32[]{:S(2)}, u32[]{:S(2)}) async-start(bf16[4,64,2048]{2,1,0:T(8,128)(2,1)} %bitcast.795), calls=%async_computation.17 | async-start | bytes 2097152 | tf_op jit(solution)/shard_map/all_to_all | solution.py:110
  (187 other events, 7152.1 us)
Sparse Core Ops, SparseCore 0:
  11.0 116.3 all-gather.17
  129.3 53.6 all-gather.25
  185.4 36.7 all-gather.23
  224.5 37.4 all-gather.19
  263.7 54.3 all-gather.27
  440.8 37.0 all-gather.33
  480.3 37.4 all-gather.21
  520.3 214.1 all-gather.29
  736.3 116.6 all-gather.31
  1163.5 72.1 reduce-scatter.18
  1297.8 72.1 reduce-scatter.20
  1372.7 131.4 reduce-scatter.22
  1507.1 141.0 reduce-scatter.24
  1651.6 117.5 reduce-scatter.14
  1775.4 498.4 all-reduce.8
  2277.9 394.3 reduce-scatter.16
where the time goes:
time: 2740 us; the launch traced here: 2720 us
  waiting for transfers between devices  1280 us (47%)
  matrix products  527 us (19%)
  blocking collectives  354 us (13%)
  local copies, waits for them, and re-layouts  239 us (9%)
  other arithmetic  161 us (6%)
  starting transfers between devices  142 us (5%)
    unnamed x21, waiting for transfers between devices  527 us
    reduce_scatter x1, waiting for transfers between devices, per_device(): lax.psum_scatter(jnp.stack([gate_term, up_term, down_term], axis=1).astyp...  396 us
    all_to_all x4, blocking collectives, to_experts(): lax.all_to_all(buffer, 'expert', split_axis=0, concat_axis=0, tiled=True)  115 us
    unnamed x384, local copies, waits for them, and re-layouts  112 us
    unnamed x2, blocking collectives  82.3 us
    all_gather x1, blocking collectives, per_device(): lax.all_gather(mlp_router, ('dp', 'expert'), axis=0, tiled=True)  79.2 us
    all_gather x1, blocking collectives, per_device(): lax.all_gather(attn_router, ('dp', 'expert'), axis=0, tiled=True)  78.2 us
    all_to_all x6, waiting for transfers between devices, grads_home(): lax.all_to_all(buffer.astype(jnp.bfloat16), 'expert', split_axis=0, conca...  73.8 us
  transfers between devices with their start and end apart: 36, of which 21 were waited for; matrix products, arithmetic and copies ran while one was open for 28% of the time, Pallas kernels for 0%

commit v1 on v0

v1 whole, which is shorter than its diff:
```python
import jax
import jax.numpy as jnp
from jax import lax
from jax.sharding import PartitionSpec as P

HEAD_WIDTH = 128


EPSILON = 1e-05
THETA_BASE = 10000.0
NEGATIVE = -1000000000.0
PRECISION_TOP = lax.Precision.HIGHEST
BF16 = jnp.bfloat16
F32 = jnp.float32


def rope_tables(positions, half_dim):
    frequency = THETA_BASE ** (-jnp.arange(half_dim, dtype=F32) / half_dim)
    angles = positions.astype(F32)[:, None] * frequency[None, :]
    return (jnp.cos(angles), jnp.sin(angles))


def rotate(values, cosine, sine_table):
    half_dim = values.shape[-1] // 2
    first_half = values[..., :half_dim]
    second_half = values[..., half_dim:]
    return jnp.concatenate(
        [
            first_half * cosine - second_half * sine_table,
            second_half * cosine + first_half * sine_table,
        ],
        axis=-1,
    )


def rotate_back(gradients, cosine, sine_table):
    return rotate(gradients, cosine, -sine_table)


def norm_forward(values, gain_row):
    inverse = lax.rsqrt(jnp.mean(values * values, axis=-1, keepdims=True) + EPSILON)
    return (values * inverse * gain_row, inverse)


def norm_backward(values, inverse, gain_row, grad_normed):
    scaled = gain_row * grad_normed
    gain_term = jnp.sum(grad_normed * values * inverse, axis=0)
    grad_values = inverse * scaled - values * inverse**3 * jnp.mean(
        scaled * values, axis=-1, keepdims=True
    )
    return (grad_values, gain_term)


def route_onehot(routes, experts):
    return (routes[..., None] == jnp.arange(experts, dtype=jnp.int32)).astype(F32)


def gate_forward(logits, onehot):
    chosen = jnp.sum(logits[:, None, :] * onehot, axis=-1)
    return jax.nn.softmax(chosen, axis=-1)


def gate_backward(gate_probs, grad_gates, onehot):
    centered = gate_probs * (grad_gates - jnp.sum(gate_probs * grad_gates, axis=-1, keepdims=True))
    return jnp.sum(centered[..., None] * onehot, axis=1)


def slot_columns(routes, experts, capacity):
    flat_routes = routes.reshape(-1)
    onehot = (flat_routes[:, None] == jnp.arange(experts, dtype=jnp.int32)[None, :]).astype(
        jnp.int32
    )
    slot_rank = jnp.sum((jnp.cumsum(onehot, axis=0) - 1) * onehot, axis=1)
    return (flat_routes * capacity + slot_rank).reshape(routes.shape)


def dot_f32(left, right):
    return jnp.dot(left, right, preferred_element_type=F32)


def to_planes(slots, experts):
    return lax.all_to_all(
        slots.reshape(experts, -1, slots.shape[-1]), "expert", split_axis=0, concat_axis=0, tiled=True
    ).reshape(slots.shape)


def per_device(
    tokens,
    segment_ids,
    attn_routes,
    mlp_routes,
    cotangent,
    attn_gain,
    kv_weights,
    attn_router,
    query_maps,
    output_maps,
    mlp_gain,
    mlp_router,
    gate_up,
    down_maps,
):
    micro_count, seq_count, local_len, width = tokens.shape
    units = micro_count * seq_count
    length = segment_ids.shape[2]
    experts = attn_router.shape[1]
    dp = lax.axis_size("dp")
    planes = lax.axis_size("expert")
    capacity = 2 * local_len // experts
    slots = experts * capacity
    both = ("dp", "expert")
    head_cols = width // dp
    heads = head_cols // HEAD_WIDTH
    scale = HEAD_WIDTH ** (-0.5)
    my_expert = lax.axis_index("expert")
    my_dp = lax.axis_index("dp")

    tokens = tokens.reshape(units, local_len, width)
    cotangent = cotangent.reshape(units, local_len, width)
    segments = segment_ids.reshape(units, length)
    attn_routes = attn_routes.reshape(units, local_len, 2)
    mlp_routes = mlp_routes.reshape(units, local_len, 2)

    columns = [slot_columns(mlp_routes[u], experts, capacity) for u in range(units)]
    slot_ids = jnp.arange(slots, dtype=jnp.int32)
    tables = []
    others = []
    for u in range(units):
        hits = (columns[u][None] == slot_ids[:, None, None]).astype(F32)
        tables.append(hits)
        others.append(jnp.sum(hits * mlp_routes[u][None, :, ::-1].astype(F32), axis=(1, 2)))
    small = jnp.concatenate(
        [
            attn_gain.astype(F32),
            mlp_gain.astype(F32),
            attn_router.astype(F32).reshape(-1),
            mlp_router.astype(F32).reshape(-1),
            attn_routes.astype(F32).reshape(-1),
        ]
        + others
    )
    small_all = lax.all_gather(small, both, axis=0)
    rows_each = attn_gain.shape[0]
    at = 0
    gain_one = small_all[:, at : at + rows_each].reshape(width)
    at += rows_each
    gain_two = small_all[:, at : at + rows_each].reshape(width)
    at += rows_each
    router_one = small_all[:, at : at + rows_each * experts].reshape(width, experts)
    at += rows_each * experts
    router_two = small_all[:, at : at + rows_each * experts].reshape(width, experts)
    at += rows_each * experts
    routes_count = units * local_len * 2
    grid = small_all[:, at:].reshape(dp, planes, -1)
    mine = lax.dynamic_index_in_dim(grid, my_expert, axis=1, keepdims=False)
    routes_all = (
        mine[:, :routes_count]
        .reshape(dp, units, local_len, 2)
        .transpose(1, 0, 2, 3)
        .reshape(units, length, 2)
        .astype(jnp.int32)
    )
    other_grid = grid[:, :, routes_count:].reshape(dp, planes, units, experts, capacity)
    other_rows = lax.dynamic_index_in_dim(other_grid, my_expert, axis=3, keepdims=False)
    other_rows = other_rows.transpose(2, 0, 1, 3).reshape(units, dp * slots).astype(jnp.int32)
    router_one_low = router_one.astype(BF16)
    router_two_low = router_two.astype(BF16)

    kv_rows = kv_weights.shape[0]
    packed = jnp.concatenate([query_maps[0], kv_weights.reshape(kv_rows * 2, width)], axis=0)
    packed = lax.all_to_all(
        packed.reshape(-1, dp, head_cols).transpose(1, 0, 2), "dp", split_axis=0, concat_axis=0, tiled=True
    )
    packed = lax.all_gather(packed, "expert", axis=0)
    query_rows = query_maps.shape[1]
    query_cols = packed[:, :, :query_rows].reshape(experts, width, head_cols)
    kv_cols = (
        packed[:, :, query_rows:]
        .reshape(planes, dp, kv_rows, 2, head_cols)
        .transpose(1, 0, 2, 3, 4)
        .reshape(width, 2 * head_cols)
    )
    qkv_cols = jnp.concatenate(
        [query_cols.transpose(1, 0, 2).reshape(width, experts * head_cols), kv_cols], axis=1
    )
    output_rows = lax.all_gather(output_maps[0], "expert", axis=0, tiled=True)

    positions = jnp.arange(length, dtype=jnp.int32)
    cosine, sine_table = rope_tables(positions, HEAD_WIDTH // 2)

    gate_up_local = gate_up[0]
    down_local = down_maps[0]

    mixed_parts = []
    input_parts = []
    a_list, g_list, ctx_list, dh_list = [], [], [], []
    b_rows_list, dgate_list, dup_list, hid_list, cot_rows_list = [], [], [], [], []
    a_home_list, dla_list, b_home_list, dlm_list = [], [], [], []
    gain_one_sum = jnp.zeros((width,), F32)
    gain_two_sum = jnp.zeros((width,), F32)
    for u in range(units):
        table = jnp.sum(tables[u], axis=2).astype(BF16)
        hits = tables[u]
        inputs = tokens[u].astype(F32)
        normed_one, inverse_one = norm_forward(inputs, gain_one)
        a_home = normed_one.astype(BF16)
        a_all = lax.all_gather(a_home, "dp", axis=0, tiled=True)

        cot = cotangent[u]
        cot_rows = lax.all_gather(
            to_planes(dot_f32(table, cot).astype(BF16), experts), "dp", axis=0, tiled=True
        )
        cot_hidden = jnp.einsum("rd,fd->rf", cot_rows, down_local, preferred_element_type=F32)

        onehot_all = route_onehot(routes_all[u], experts)
        gates_all = gate_forward(dot_f32(a_all, router_one_low), onehot_all)
        qkv = dot_f32(a_all, qkv_cols)
        query_dense = qkv[:, : experts * head_cols].astype(BF16).astype(F32)
        query_dense = query_dense.reshape(length, 1, experts, head_cols)
        query_raw = jnp.sum(query_dense * onehot_all[..., None], axis=2)
        query_vectors = rotate(
            query_raw.reshape(length, 2, heads, HEAD_WIDTH),
            cosine[:, None, None],
            sine_table[:, None, None],
        ).astype(BF16)
        keys = rotate(
            qkv[:, experts * head_cols : (experts + 1) * head_cols].reshape(
                length, heads, HEAD_WIDTH
            ),
            cosine[:, None],
            sine_table[:, None],
        ).astype(BF16)
        values = qkv[:, (experts + 1) * head_cols :].astype(BF16).reshape(length, heads, HEAD_WIDTH)
        mask = (positions[None, :] <= positions[:, None]) & (
            segments[u][:, None] == segments[u][None, :]
        )

        def score_of(query_vectors, keys, mask):
            score = jnp.einsum("lkhd,mhd->khlm", query_vectors, keys, preferred_element_type=F32)
            return jnp.where(mask[None, None], score * scale, NEGATIVE)

        score = score_of(query_vectors, keys, mask)
        row_top = jnp.max(score, axis=-1, keepdims=True)
        exponent = jnp.exp(score - row_top)
        row_total = jnp.sum(exponent, axis=-1, keepdims=True)
        log_total = row_top + jnp.log(row_total)
        probs = (exponent / row_total).astype(BF16)
        context = (
            jnp.einsum("khlm,mhd->lkhd", probs, values, preferred_element_type=F32)
            .astype(BF16)
            .reshape(length, 2, head_cols)
        )
        gated_onehot = gates_all[..., None] * onehot_all
        context_gated = (
            jnp.sum(context.astype(F32)[:, :, None, :] * gated_onehot[..., None], axis=1)
            .astype(BF16)
            .reshape(length, experts * head_cols)
        )
        attn_sum = lax.psum_scatter(
            dot_f32(context_gated, output_rows).astype(BF16), "dp", scatter_dimension=0, tiled=True
        )
        hidden_state = inputs + attn_sum.astype(F32)

        normed_two, inverse_two = norm_forward(hidden_state, gain_two)
        b_home = normed_two.astype(BF16)
        onehot_mlp = route_onehot(mlp_routes[u], experts)
        gates_mlp = gate_forward(dot_f32(b_home, router_two_low), onehot_mlp)
        b_rows = lax.all_gather(
            to_planes(dot_f32(table, b_home).astype(BF16), experts), "dp", axis=0, tiled=True
        )
        logits_rows = dot_f32(b_rows, router_two_low)
        own_logit = jnp.sum(
            jnp.where(jnp.arange(experts)[None] == my_expert, logits_rows, 0.0), axis=1
        )
        other_logit = jnp.sum(
            jnp.where(jnp.arange(experts)[None] == other_rows[u][:, None], logits_rows, 0.0), axis=1
        )
        gate_rows = jax.nn.sigmoid(own_logit - other_logit)[:, None]
        gate_up_rows = jnp.einsum("rd,fcd->rcf", b_rows, gate_up_local, preferred_element_type=F32)
        gate_val = gate_up_rows[:, 0]
        up_val = gate_up_rows[:, 1]
        sigmoid = jax.nn.sigmoid(gate_val)
        silu = gate_val * sigmoid
        hidden = silu * up_val
        hidden_low = hidden.astype(BF16)
        hidden_gated = (hidden * gate_rows).astype(BF16)
        grad_hidden = cot_hidden * gate_rows
        grad_gate = (grad_hidden * up_val * sigmoid * (1.0 + gate_val * (1.0 - sigmoid))).astype(BF16)
        grad_up = (grad_hidden * silu).astype(BF16)
        out_rows = lax.psum_scatter(
            dot_f32(hidden_low, down_local).astype(BF16), "dp", scatter_dimension=0, tiled=True
        )
        grad_b_rows = lax.psum_scatter(
            jnp.einsum(
                "rcf,fcd->rd",
                jnp.stack([grad_gate, grad_up], axis=1),
                gate_up_local,
                preferred_element_type=F32,
            ).astype(BF16),
            "dp",
            scatter_dimension=0,
            tiled=True,
        )
        out_slots = to_planes(out_rows, experts)
        grad_b_slots = to_planes(grad_b_rows, experts)

        gated_table = jnp.sum(hits * gates_mlp[None], axis=2).T
        gated_high = gated_table.astype(BF16)
        gated_low = (gated_table - gated_high.astype(F32)).astype(BF16)
        mlp_sum = dot_f32(gated_high, out_slots) + dot_f32(gated_low, out_slots)
        mixed_parts.append((hidden_state + mlp_sum).astype(BF16))

        cot_out = jnp.einsum("td,sd->st", cot, out_slots, preferred_element_type=F32)
        grad_gates_mlp = jnp.sum(hits * cot_out[..., None], axis=0)
        dlm = gate_backward(gates_mlp, grad_gates_mlp, onehot_mlp)
        grad_b = jnp.einsum("st,sd->td", table, grad_b_slots, preferred_element_type=F32) + jnp.einsum(
            "re,de->rd", dlm, router_two, precision=PRECISION_TOP
        )
        grad_state, gain_two_term = norm_backward(hidden_state, inverse_two, gain_two, grad_b)
        grad_state = cot.astype(F32) + grad_state
        dh_all = lax.all_gather(grad_state.astype(BF16), "dp", axis=0, tiled=True)

        grad_context_dense = jnp.einsum(
            "td,cd->tc", dh_all, output_rows, preferred_element_type=F32
        ).reshape(length, 1, experts, head_cols)
        grad_context = jnp.sum(grad_context_dense * onehot_all[..., None], axis=2)
        dga = lax.psum_scatter(
            jnp.sum(grad_context * context.astype(F32), axis=-1),
            "dp",
            scatter_dimension=0,
            tiled=True,
        )
        grad_context = (
            (grad_context * gates_all[..., None]).astype(BF16).reshape(length, 2, heads, HEAD_WIDTH)
        )
        score = score_of(query_vectors, keys, mask)
        probs_full = jnp.exp(score - log_total)
        probs_low = probs_full.astype(BF16)
        grad_probs = jnp.einsum("lkhd,mhd->khlm", grad_context, values, preferred_element_type=F32)
        grad_scores = (
            probs_full * (grad_probs - jnp.sum(probs_full * grad_probs, axis=-1, keepdims=True))
        ).astype(BF16)
        grad_queries = (
            jnp.einsum("khlm,mhd->lkhd", grad_scores, keys, preferred_element_type=F32) * scale
        )
        grad_keys = (
            jnp.einsum("khlm,lkhd->mhd", grad_scores, query_vectors, preferred_element_type=F32)
            * scale
        )
        grad_values = jnp.einsum("khlm,lkhd->mhd", probs_low, grad_context, preferred_element_type=F32)
        grad_keys = rotate_back(grad_keys, cosine[:, None], sine_table[:, None])
        grad_query_raw = (
            rotate_back(grad_queries, cosine[:, None, None], sine_table[:, None, None])
            .astype(BF16)
            .astype(F32)
            .reshape(length, 2, 1, head_cols)
        )
        grad_query_dense = jnp.sum(grad_query_raw * onehot_all[..., None], axis=1)
        grad_qkv = jnp.concatenate(
            [
                grad_query_dense.reshape(length, experts * head_cols).astype(BF16),
                grad_keys.reshape(length, head_cols).astype(BF16),
                grad_values.reshape(length, head_cols).astype(BF16),
            ],
            axis=1,
        )
        grad_a = lax.psum_scatter(
            jnp.einsum("tc,dc->td", grad_qkv, qkv_cols, preferred_element_type=F32).astype(BF16),
            "dp",
            scatter_dimension=0,
            tiled=True,
        ).astype(F32)
        onehot_home = route_onehot(attn_routes[u], experts)
        gates_home = lax.dynamic_slice_in_dim(gates_all, my_dp * local_len, local_len, axis=0)
        dla = gate_backward(gates_home, dga, onehot_home)
        grad_a = grad_a + jnp.einsum("re,de->rd", dla, router_one, precision=PRECISION_TOP)
        grad_inputs, gain_one_term = norm_backward(inputs, inverse_one, gain_one, grad_a)
        input_parts.append(grad_state + grad_inputs)

        gain_one_sum = gain_one_sum + gain_one_term
        gain_two_sum = gain_two_sum + gain_two_term
        a_list.append(a_all)
        g_list.append(grad_qkv)
        ctx_list.append(context_gated)
        dh_list.append(dh_all)
        b_rows_list.append(b_rows)
        dgate_list.append(grad_gate)
        dup_list.append(grad_up)
        hid_list.append(hidden_gated)
        cot_rows_list.append(cot_rows)
        a_home_list.append(a_home)
        dla_list.append(dla)
        b_home_list.append(b_home)
        dlm_list.append(dlm)

    def summed(pattern, lefts, rights):
        total = None
        for left, right in zip(lefts, rights):
            term = jnp.einsum(pattern, left, right, preferred_element_type=F32)
            total = term if total is None else total + term
        return total

    down_grad = summed("rf,rd->fd", hid_list, cot_rows_list)
    gate_grad = summed("rf,rd->fd", dgate_list, b_rows_list)
    up_grad = summed("rf,rd->fd", dup_list, b_rows_list)
    gate_up_grad = jnp.stack([gate_grad, up_grad], axis=1)

    output_grad = lax.psum_scatter(
        summed("tc,td->cd", ctx_list, dh_list).astype(BF16), "expert", scatter_dimension=0, tiled=True
    ).astype(F32)

    qkv_grad = summed("td,tc->dc", a_list, g_list).astype(BF16)
    query_part = (
        qkv_grad[:, : experts * head_cols]
        .reshape(dp, query_rows, experts, head_cols)
        .transpose(2, 0, 1, 3)
    )
    kv_part = (
        qkv_grad[:, experts * head_cols :]
        .reshape(dp, planes, kv_rows * 2, head_cols)
        .transpose(1, 0, 2, 3)
    )
    packed_grad = lax.psum_scatter(
        jnp.concatenate([query_part, kv_part], axis=2), "expert", scatter_dimension=0, tiled=False
    )
    packed_grad = lax.all_to_all(packed_grad, "dp", split_axis=0, concat_axis=0, tiled=True)
    packed_grad = packed_grad.transpose(1, 0, 2).reshape(-1, width).astype(F32)
    query_grad = packed_grad[:query_rows]
    kv_grad = packed_grad[query_rows:].reshape(kv_rows, 2, width)

    router_one_grad = jnp.einsum(
        "rd,re->de",
        jnp.concatenate(a_home_list, axis=0).astype(F32),
        jnp.concatenate(dla_list, axis=0),
        precision=PRECISION_TOP,
    )
    router_two_grad = jnp.einsum(
        "rd,re->de",
        jnp.concatenate(b_home_list, axis=0).astype(F32),
        jnp.concatenate(dlm_list, axis=0),
        precision=PRECISION_TOP,
    )
    small_grad = jnp.concatenate(
        [gain_one_sum[:, None], gain_two_sum[:, None], router_one_grad, router_two_grad], axis=1
    )
    small_grad = lax.psum_scatter(small_grad, both, scatter_dimension=0, tiled=True)

    shape = (micro_count, seq_count, local_len, width)
    return (
        jnp.stack(mixed_parts, axis=0).reshape(shape),
        jnp.stack(input_parts, axis=0).reshape(shape),
        small_grad[:, 0],
        kv_grad,
        small_grad[:, 2 : 2 + experts],
        query_grad[None],
        output_grad[None],
        small_grad[:, 1],
        small_grad[:, 2 + experts :],
        gate_up_grad[None],
        down_grad[None],
    )


def solution(mesh):
    in_specs = (
        P(None, "expert", "dp", None),
        P(None, "expert", None),
        P(None, "expert", "dp", None),
        P(None, "expert", "dp", None),
        P(None, "expert", "dp", None),
        P(("dp", "expert")),
        P(("dp", "expert"), None, None),
        P(("dp", "expert"), None),
        P("expert", "dp", None),
        P("expert", "dp", None),
        P(("dp", "expert")),
        P(("dp", "expert"), None),
        P("expert", "dp", None, None),
        P("expert", "dp", None),
    )
    out_specs = (
        P(None, "expert", "dp", None),
        P(None, "expert", "dp", None),
        P(("dp", "expert")),
        P(("dp", "expert"), None, None),
        P(("dp", "expert"), None),
        P("expert", "dp", None),
        P("expert", "dp", None),
        P(("dp", "expert")),
        P(("dp", "expert"), None),
        P("expert", "dp", None, None),
        P("expert", "dp", None),
    )
    return jax.shard_map(
        per_device, mesh=mesh, in_specs=in_specs, out_specs=out_specs, check_vma=False
    )
```

time: 2740 us -> 1840 us (0.67)
  waiting for transfers between devices: 1280 us -> 726 us
  blocking collectives: 354 us -> 207 us
  starting transfers between devices: 142 us -> 28 us
  matrix products: 527 us -> 456 us
    unnamed x21 -> x26, waiting for transfers between devices: 527 us -> 129 us
    all_to_all x20 -> x5, waiting for transfers between devices: 179 us -> 17.2 us  [the longest x4 17.2 us: to_planes(): lax.all_to_all(slots.reshape(experts, -1, slots.shape[-1]), 'expert', spl...]
    all_to_all x20 -> x5, starting transfers between devices: 141 us -> 25 us  [the longest x4 21.1 us: to_planes(): lax.all_to_all(slots.reshape(experts, -1, slots.shape[-1]), 'expert', spl...]
    all_gather x2 -> x1, blocking collectives: 157 us -> 65.4 us  [per_device(): small_all = lax.all_gather(small, both, axis=0)]
    another operation x23 -> x9, other arithmetic: 110 us -> 18 us  [the longest x1 45.9 us: per_device(): jnp.stack([gate_term, up_term, down_term], axis=1).astype(jnp.bfloat16)]
    unnamed x2 -> x0, blocking collectives: 82.3 us -> none
    dot_general x68 -> x60, matrix products: 481 us -> 420 us  [the longest x10 110 us: summed(): term = jnp.einsum(pattern, left, right, preferred_element_type=F32)]
    all_gather x9 -> x10, waiting for transfers between devices: 150 us -> 204 us  [the longest x1 110 us: per_device(): packed = lax.all_gather(packed, 'expert', axis=0)]
  transfers between devices with their start and end apart: 36 -> 28, of which waited for: 21 -> 16; matrix products, arithmetic and copies ran while one was open for 28% -> 39% of each run, Pallas kernels for 0% -> 0%
where the time goes in v1:
time: 1840 us; the launch traced here: 1830 us
  waiting for transfers between devices  726 us (39%)
  matrix products  456 us (25%)
  local copies, waits for them, and re-layouts  235 us (13%)
  blocking collectives  207 us (11%)
  other arithmetic  162 us (9%)
  starting transfers between devices  28 us (2%)
    reduce_scatter x2, waiting for transfers between devices, per_device(): lax.psum_scatter(dot_f32(hidden_low, down_local).astype(BF16), 'dp', scat...  139 us
    unnamed x26, waiting for transfers between devices  129 us
    all_to_all x4, blocking collectives, to_planes(): lax.all_to_all(slots.reshape(experts, -1, slots.shape[-1]), 'expert', spl...  113 us
    all_gather x1, waiting for transfers between devices, per_device(): packed = lax.all_gather(packed, 'expert', axis=0)  110 us
    dot_general x10, matrix products, summed(): term = jnp.einsum(pattern, left, right, preferred_element_type=F32)  110 us
    dot_general x20, matrix products, dot_f32(): return jnp.dot(left, right, preferred_element_type=F32)  92.7 us
    reduce_scatter x2, waiting for transfers between devices, per_device(): lax.psum_scatter(jnp.einsum('rcf,fcd->rd', jnp.stack([grad_gate, grad_up]...  79.6 us
    reduce_scatter x1, waiting for transfers between devices, per_device(): lax.psum_scatter(summed('tc,td->cd', ctx_list, dh_list).astype(BF16), 'ex...  75.4 us
  transfers between devices with their start and end apart: 28, of which 16 were waited for; matrix products, arithmetic and copies ran while one was open for 39% of the time, Pallas kernels for 0%

profile of v1, /device:TPU:8, one launch (start us, length us, event | category | flops | bytes accessed | tf_op | source)
XLA Modules:
  0.0 1829.8 jit_solution(9731859756047599677)
XLA Ops:
  21.5 65.4 %all-gather.3 = f32[32,1,1664]{2,1,0:T(1,128)S(1)} all-gather(f32[1,1,1664]{2,1,0:T(1,128)S(1)} %reshape.1029), channel_id=2, replica_groups=mesh['dp'=8,'expert'=4] {'dp','expert'}, dimensions={0}, use_global_device_ids=true | all-gather | bytes 219648 | tf_op jit(solution)/shard_map/all_gather | solution.py:142
  97.4 28.1 %all_to_all.50 = bf16[8,384,256]{1,2,0:T(8,128)(2,1)} all-to-all(bf16[8,384,256]{1,2,0:T(8,128)(2,1)S(1)} %maximum_bitcast_fusion.2), channel_id=1, replica_groups=mesh['dp'=8,'expert'=4] {'dp'}, dimensions={0} | all-to-all | bytes 3145728 | tf_op jit(solution)/shard_map/all_to_all | solution.py:171
  144.9 110.1 %all-gather.31.cloned.1.call-done = bf16[32,384,256]{2,1,0:T(8,128)(2,1)} async-done(((bf16[8,384,256]{2,1,0:T(8,128)(2,1)}), bf16[32,384,256]{2,1,0:T(8,128)(2,1)}) %all-gather.31.cloned.1.call-update) | async-done | bytes 6291472 | tf_op jit(solution)/shard_map/all_gather | solution.py:174
  493.8 51.5 %reduce-scatter.24.cloned.1.call-done = bf16[128,2048]{1,0:T(8,128)(2,1)} async-done(((bf16[1024,2048]{1,0:T(8,128)(2,1)}), bf16[128,2048]{1,0:T(8,128)(2,1)}) %reduce-scatter.24.cloned.1.call-update) | async-done | bytes 524304 | tf_op jit(solution)/shard_map/reduce_scatter | solution.py:259
  551.5 28.9 %all_to_all.51 = bf16[4,64,2048]{2,1,0:T(8,128)(2,1)} all-to-all(bf16[4,64,2048]{2,1,0:T(8,128)(2,1)S(1)} %bitcast.584), channel_id=1, replica_groups=mesh['dp'=8,'expert'=4] {'expert'}, dimensions={0} | all-to-all | bytes 2097152 | tf_op jit(solution)/shard_map/all_to_all | solution.py:82
  580.9 28.0 %all_to_all.52 = bf16[4,64,2048]{2,1,0:T(8,128)(2,1)} all-to-all(bf16[4,64,2048]{2,1,0:T(8,128)(2,1)S(1)} %bitcast.585), channel_id=1, replica_groups=mesh['dp'=8,'expert'=4] {'expert'}, dimensions={0} | all-to-all | bytes 2097152 | tf_op jit(solution)/shard_map/all_to_all | solution.py:82
  610.5 28.1 %all_to_all.53 = bf16[4,64,2048]{2,1,0:T(8,128)(2,1)} all-to-all(bf16[4,64,2048]{2,1,0:T(8,128)(2,1)S(1)} %bitcast.586), channel_id=1, replica_groups=mesh['dp'=8,'expert'=4] {'expert'}, dimensions={0} | all-to-all | bytes 2097152 | tf_op jit(solution)/shard_map/all_to_all | solution.py:82
  640.1 28.0 %all_to_all.54 = bf16[4,64,2048]{2,1,0:T(8,128)(2,1)} all-to-all(bf16[4,64,2048]{2,1,0:T(8,128)(2,1)S(1)} %bitcast.587), channel_id=1, replica_groups=mesh['dp'=8,'expert'=4] {'expert'}, dimensions={0} | all-to-all | bytes 2097152 | tf_op jit(solution)/shard_map/all_to_all | solution.py:82
  697.1 19.5 %fusion.47 = f32[2048,2,704]{0,2,1:T(8,128)} fusion(bf16[2048,2048]{1,0:T(8,128)(2,1)S(1)} %copy-done.4, bf16[704,2,2048]{2,1,0:T(2,128)(2,1)} %bitcast.633), kind=kOutput, calls=%fused_computation.91 | convolution fusion | flops 11811160064 | bytes 25690112 | tf_op jit(solution)/shard_map/rd,fcd->rcf/dot_general | solution.py:279
  716.7 30.3 %all-gather.27.cloned.1.call-done = bf16[2048,2048]{1,0:T(8,128)(2,1)} async-done(((bf16[256,2048]{1,0:T(8,128)(2,1)}), bf16[2048,2048]{1,0:T(8,128)(2,1)}) %all-gather.27.cloned.1.call-update) | async-done | bytes 8388624 | tf_op jit(solution)/shard_map/all_gather | solution.py:210
  762.7 18.3 %bitcast_convert_fusion = bf16[2048,2048]{1,0:T(8,128)(2,1)} fusion(bf16[2048,1,704]{0,2,1:T(8,128)(2,1)S(1)} %bitcast.637, bf16[2048,1,704]{0,2,1:T(8,128)(2,1)S(1)} %bitcast.638, bf16[704,2,2048]{2,1,0:T(2,128)(2,1)} %bitcast.634), kind=kOutput, calls=%fused_computation.5 | convolution fusion | flops 11818237952 | bytes 19922944 | tf_op jit(solution)/shard_map/rcf,fcd->rd/dot_general | solution.py:294
  794.8 20.2 %fusion.44 = f32[2048,2,704]{0,2,1:T(8,128)S(1)} fusion(bf16[2048,2048]{1,0:T(8,128)(2,1)} %all-gather.17.cloned.1.call-done, bf16[704,2,2048]{2,1,0:T(2,128)(2,1)} %bitcast.635), kind=kOutput, calls=%fused_computation.90 | convolution fusion | flops 11811160064 | bytes 25690112 | tf_op jit(solution)/shard_map/rd,fcd->rcf/dot_general | solution.py:279
  847.8 18.0 bitcast_convert_fusion.1
  883.1 70.4 %reduce-scatter.26.cloned.1.call-done = bf16[256,2048]{1,0:T(8,128)(2,1)} async-done(((bf16[2048,2048]{1,0:T(8,128)(2,1)}), bf16[256,2048]{1,0:T(8,128)(2,1)}) %reduce-scatter.26.cloned.1.call-update) | async-done | bytes 1048592 | tf_op jit(solution)/shard_map/reduce_scatter | solution.py:290
  959.6 68.6 %reduce-scatter.22.cloned.1.call-done = bf16[256,2048]{1,0:T(8,128)(2,1)} async-done(((bf16[2048,2048]{1,0:T(8,128)(2,1)}), bf16[256,2048]{1,0:T(8,128)(2,1)}) %reduce-scatter.22.cloned.1.call-update) | async-done | bytes 1048592 | tf_op jit(solution)/shard_map/reduce_scatter | solution.py:290
  1035.9 67.5 %reduce-scatter.28.cloned.1.call-done = bf16[256,2048]{1,0:T(8,128)(2,1)} async-done(((bf16[2048,2048]{1,0:T(8,128)(2,1)}), bf16[256,2048]{1,0:T(8,128)(2,1)}) %reduce-scatter.28.cloned.1.call-update) | async-done | bytes 1048592 | tf_op jit(solution)/shard_map/reduce_scatter | solution.py:293
  1114.2 17.2 all-to-all-done.6
  1141.4 36.6 %all-gather.29.cloned.1.call-done = bf16[1024,2048]{1,0:T(8,128)(2,1)} async-done(((bf16[128,2048]{1,0:T(8,128)(2,1)}), bf16[1024,2048]{1,0:T(8,128)(2,1)}) %all-gather.29.cloned.1.call-update) | async-done | bytes 4194320 | tf_op jit(solution)/shard_map/all_gather | solution.py:321
  1212.6 15.9 fusion.2
  1270.4 15.7 fusion.5
  1515.6 20.5 %copy.707 = f32[1,704,2,2048]{3,2,1,0:T(2,128)} copy(f32[1,704,2,2048]{3,1,2,0:T(8,128)} %maximum_bitcast_fusion) | data formatting | bytes 23068672
  1564.4 26.6 %reduce-scatter.36.cloned.1.call-done = bf16[1,8,384,256]{3,2,1,0:T(8,128)(2,1)} async-done(((bf16[4,8,384,256]{3,2,1,0:T(8,128)(2,1)}), bf16[1,8,384,256]{3,2,1,0:T(8,128)(2,1)}) %reduce-scatter.36.cloned.1.call-update) | async-done | bytes 1572880 | tf_op jit(solution)/shard_map/reduce_scatter | solution.py:423
  1599.3 126.9 %reduce-scatter.44.cloned.1.call-done = f32[64,10]{1,0:T(8,128)} async-done(((f32[2048,10]{1,0:T(8,128)}), f32[64,10]{1,0:T(8,128)}) %reduce-scatter.44.cloned.1.call-update) | async-done | bytes 2576
  1730.5 75.4 %reduce-scatter.38.cloned.1.call-done = bf16[256,2048]{1,0:T(8,128)(2,1)} async-done(((bf16[1024,2048]{1,0:T(8,128)(2,1)}), bf16[256,2048]{1,0:T(8,128)(2,1)}) %reduce-scatter.38.cloned.1.call-update) | async-done | bytes 1048592 | tf_op jit(solution)/shard_map/reduce_scatter | solution.py:408
  (650 shorter events, 797.7 us)
Async XLA Ops:
  7.2 133.3 %all-gather.15.cloned.1.call-start = ((), (), s32[]{:S(2)}) async-start(), calls=%async_computation.23 | async-start | bytes 4718592 | tf_op jit(solution)/shard_map/all_gather | solution.py:207
  91.0 164.0 %all-gather.31.cloned.1.call-start = ((), (), s32[]{:S(2)}) async-start(), calls=%async_computation.41 | async-start | bytes 7864320 | tf_op jit(solution)/shard_map/all_gather | solution.py:174
  128.3 166.6 %all-gather.19.cloned.1.call-start = ((), (), s32[]{:S(2)}) async-start(), calls=%async_computation.27 | async-start | bytes 4718592 | tf_op jit(solution)/shard_map/all_gather | solution.py:207
  129.0 291.4 %all-gather.33.cloned.1.call-start = ((), (), s32[]{:S(2)}) async-start(), calls=%async_computation.42 | async-start | bytes 5242880 | tf_op jit(solution)/shard_map/all_gather | solution.py:186
  129.6 364.2 %reduce-scatter.20.cloned.1.call-start = ((), (), s32[]{:S(2)}) async-start(), calls=%async_computation.24 | async-start | bytes 4718592 | tf_op jit(solution)/shard_map/reduce_scatter | solution.py:259
  429.9 115.4 %reduce-scatter.24.cloned.1.call-start = ((), (), s32[]{:S(2)}) async-start(), calls=%async_computation.28 | async-start | bytes 4718592 | tf_op jit(solution)/shard_map/reduce_scatter | solution.py:259
  493.6 178.6 %all-gather.17.cloned.1.call-start = ((), (), s32[]{:S(2)}) async-start(), calls=%async_computation.25 | async-start | bytes 9437184 | tf_op jit(solution)/shard_map/all_gather | solution.py:268
  580.4 110.3 %all-gather.21.cloned.1.call-start = ((), (), s32[]{:S(2)}) async-start(), calls=%async_computation.29 | async-start | bytes 9437184 | tf_op jit(solution)/shard_map/all_gather | solution.py:268
  609.0 138.1 %all-gather.27.cloned.1.call-start = ((), (), s32[]{:S(2)}) async-start(), calls=%async_computation.35 | async-start | bytes 9437184 | tf_op jit(solution)/shard_map/all_gather | solution.py:210
  638.6 192.5 %all-gather.23.cloned.1.call-start = ((), (), s32[]{:S(2)}) async-start(), calls=%async_computation.31 | async-start | bytes 9437184 | tf_op jit(solution)/shard_map/all_gather | solution.py:210
  668.1 209.8 %reduce-scatter.32.cloned.1.call-start = ((), (), s32[]{:S(2)}) async-start(), calls=%async_computation.36 | async-start | bytes 9437184 | tf_op jit(solution)/shard_map/reduce_scatter | solution.py:293
  781.1 172.5 %reduce-scatter.26.cloned.1.call-start = ((), (), s32[]{:S(2)}) async-start(), calls=%async_computation.30 | async-start | bytes 9437184 | tf_op jit(solution)/shard_map/reduce_scatter | solution.py:290
  794.8 233.5 %reduce-scatter.22.cloned.1.call-start = ((), (), s32[]{:S(2)}) async-start(), calls=%async_computation.26 | async-start | bytes 9437184 | tf_op jit(solution)/shard_map/reduce_scatter | solution.py:290
  830.4 272.9 %reduce-scatter.28.cloned.1.call-start = ((), (), s32[]{:S(2)}) async-start(), calls=%async_computation.32 | async-start | bytes 9437184 | tf_op jit(solution)/shard_map/reduce_scatter | solution.py:293
  878.0 75.6 %all-to-all-start.8 = ((bf16[4,64,2048]{2,1,0:T(8,128)(2,1)}), bf16[4,64,2048]{2,1,0:T(8,128)(2,1)S(1)}, u32[]{:S(2)}, u32[]{:S(2)}) async-start(bf16[4,64,2048]{2,1,0:T(8,128)(2,1)} %bitcast.605), calls=%async_computation.15 | async-start | bytes 2097152 | tf_op jit(solution)/shard_map/all_to_all | solution.py:82
  1140.2 96.7 %all-gather.25.cloned.1.call-start = ((), (), s32[]{:S(2)}) async-start(), calls=%async_computation.33 | async-start | bytes 4718592 | tf_op jit(solution)/shard_map/all_gather | solution.py:321
  1140.8 327.8 %reduce-scatter.42.cloned.1.call-start = ((), (), s32[]{:S(2)}) async-start(), calls=%async_computation.44 | async-start | bytes 589824
  1296.4 173.1 %reduce-scatter.40.cloned.1.call-start = ((), (), s32[]{:S(2)}) async-start(), calls=%async_computation.43 | async-start | bytes 589824
  1331.3 139.8 %reduce-scatter.34.cloned.1.call-start = ((), (), s32[]{:S(2)}) async-start(), calls=%async_computation.38 | async-start | bytes 4718592 | tf_op jit(solution)/shard_map/reduce_scatter | solution.py:367
  1342.8 135.2 %reduce-scatter.30.cloned.1.call-start = ((), (), s32[]{:S(2)}) async-start(), calls=%async_computation.34 | async-start | bytes 4718592 | tf_op jit(solution)/shard_map/reduce_scatter | solution.py:367
  1379.5 211.5 %reduce-scatter.36.cloned.1.call-start = ((), (), s32[]{:S(2)}) async-start(), calls=%async_computation.39 | async-start | bytes 7864320 | tf_op jit(solution)/shard_map/reduce_scatter | solution.py:423
  1429.4 296.8 %reduce-scatter.44.cloned.1.call-start = ((), (), s32[]{:S(2)}) async-start(), calls=%async_computation.45 | async-start | bytes 1081344
  1483.3 322.5 %reduce-scatter.38.cloned.1.call-start = ((), (), s32[]{:S(2)}) async-start(), calls=%async_computation.40 | async-start | bytes 5242880 | tf_op jit(solution)/shard_map/reduce_scatter | solution.py:408
  1591.1 217.6 %all-to-all-start.9 = ((bf16[8,384,256]{2,1,0:T(8,128)(2,1)}), bf16[8,384,256]{2,1,0:T(8,128)(2,1)S(1)}, u32[]{:S(2)}, u32[]{:S(2)}) async-start(bf16[8,384,256]{2,1,0:T(8,128)(2,1)} %bitcast.600), calls=%async_computation.18 | async-start | bytes 3145728 | tf_op jit(solution)/shard_map/all_to_all | solution.py:426
  (149 other events, 5167.2 us)
Sparse Core Ops, SparseCore 0:
  91.1 49.3 all-gather.14
  142.6 112.3 all-gather.30
  256.9 37.9 all-gather.18
  296.3 78.1 all-gather.32
  430.0 51.3 reduce-scatter.19
  493.7 51.4 reduce-scatter.23
  580.6 53.7 all-gather.16
  636.3 54.3 all-gather.20
  692.6 54.3 all-gather.26
  748.7 54.3 all-gather.22
  806.6 71.2 reduce-scatter.31
  882.2 71.2 reduce-scatter.25
  957.0 71.2 reduce-scatter.21
  1032.0 71.2 reduce-scatter.27
  1140.3 37.6 all-gather.28
  1179.8 36.7 all-gather.24
  1296.5 34.3 reduce-scatter.41
  1334.2 34.0 reduce-scatter.39
  1371.7 51.3 reduce-scatter.33
  1426.6 51.3 reduce-scatter.29
  1480.3 110.7 reduce-scatter.35
  1593.9 132.2 reduce-scatter.43
  1728.6 77.2 reduce-scatter.37

commit v2 on v1

v2 whole, which is shorter than its diff:
```python
import functools

import jax
import jax.numpy as jnp
from jax import lax
from jax.experimental import pallas as pl
from jax.experimental.pallas import tpu as pltpu
from jax.sharding import PartitionSpec as P

HEAD_WIDTH = 128


EPSILON = 1e-05
THETA_BASE = 10000.0
NEGATIVE = -1000000000.0
PRECISION_TOP = lax.Precision.HIGHEST
BF16 = jnp.bfloat16
F32 = jnp.float32


def rope_in(values, cosine, sine_signed):
    return values * cosine + pltpu.roll(values, HEAD_WIDTH // 2, 1) * sine_signed


def contract(left, right, left_dim, right_dim):
    return lax.dot_general(
        left, right, (((left_dim,), (right_dim,)), ((), ())), preferred_element_type=F32
    )


def attn_forward_kernel(
    routes_ref, gates_ref, seg_col_ref, seg_row_ref, cos_ref, sin_ref, qkv_ref,
    q_ref, k_ref, v_ref, o_ref, gated_ref, *, experts, block, scale,
):
    length = cos_ref.shape[0]
    width = HEAD_WIDTH
    cosine = cos_ref[...]
    sine = sin_ref[...]
    k_ref[0] = rope_in(qkv_ref[:, experts * width : (experts + 1) * width], cosine, sine).astype(BF16)
    v_ref[0] = qkv_ref[:, (experts + 1) * width :].astype(BF16)
    for choice in range(2):
        route = routes_ref[:, choice : choice + 1]
        raw = qkv_ref[:, :width]
        for e in range(1, experts):
            raw = jnp.where(route == e, qkv_ref[:, e * width : (e + 1) * width], raw)
        q_ref[0, choice] = rope_in(raw.astype(BF16).astype(F32), cosine, sine).astype(BF16)
    for i in range(length // block):
        rows = slice(i * block, (i + 1) * block)
        n = (i + 1) * block
        keys = k_ref[0, :n]
        values = v_ref[0, :n]
        mask = (
            lax.broadcasted_iota(jnp.int32, (block, n), 1)
            <= lax.broadcasted_iota(jnp.int32, (block, n), 0) + i * block
        ) & (seg_col_ref[rows, :] == seg_row_ref[:, :n])
        for choice in range(2):
            score = jnp.where(mask, contract(q_ref[0, choice, rows], keys, 1, 1) * scale, NEGATIVE)
            exponent = jnp.exp(score - jnp.max(score, axis=1, keepdims=True))
            inverse = 1.0 / jnp.sum(exponent, axis=1, keepdims=True)
            probs = (exponent * inverse).astype(BF16)
            o_ref[0, choice, rows] = contract(probs, values, 1, 0).astype(BF16)
    first = o_ref[0, 0].astype(F32) * gates_ref[:, 0:1]
    second = o_ref[0, 1].astype(F32) * gates_ref[:, 1:2]
    for e in range(experts):
        part = jnp.where(routes_ref[:, 0:1] == e, first, 0.0)
        part = jnp.where(routes_ref[:, 1:2] == e, second, part)
        gated_ref[:, e * width : (e + 1) * width] = part.astype(BF16)


def attn_backward_kernel(
    routes_ref, gates_ref, seg_col_ref, seg_row_ref, cos_ref, sin_ref, q_ref, k_ref, v_ref, o_ref, up_ref,
    grad_ref, dgate_ref, dctx_ref, dq_ref, dk_ref, dv_ref, *, experts, block, scale,
):
    length = cos_ref.shape[0]
    width = HEAD_WIDTH
    lanes = lax.broadcasted_iota(jnp.int32, (length, width), 1)
    dgate = jnp.zeros((length, width), F32)
    for choice in range(2):
        route = routes_ref[:, choice : choice + 1]
        up = up_ref[:, :width]
        for e in range(1, experts):
            up = jnp.where(route == e, up_ref[:, e * width : (e + 1) * width], up)
        part = jnp.sum(up * o_ref[0, choice].astype(F32), axis=1, keepdims=True)
        dgate = dgate + jnp.where(lanes == choice, part, 0.0)
        dctx_ref[choice] = (up * gates_ref[:, choice : choice + 1]).astype(BF16)
    dgate_ref[0] = dgate
    dk_ref[...] = jnp.zeros_like(dk_ref)
    dv_ref[...] = jnp.zeros_like(dv_ref)
    for i in range(length // block):
        rows = slice(i * block, (i + 1) * block)
        n = (i + 1) * block
        keys = k_ref[0, :n]
        values = v_ref[0, :n]
        mask = (
            lax.broadcasted_iota(jnp.int32, (n, block), 0)
            <= lax.broadcasted_iota(jnp.int32, (n, block), 1) + i * block
        ) & (seg_col_ref[:n, :] == seg_row_ref[:, rows])
        for choice in range(2):
            query = q_ref[0, choice, rows]
            dctx = dctx_ref[choice, rows]
            score = jnp.where(mask, contract(keys, query, 1, 1) * scale, NEGATIVE)
            exponent = jnp.exp(score - jnp.max(score, axis=0, keepdims=True))
            probs = exponent * (1.0 / jnp.sum(exponent, axis=0, keepdims=True))
            dprobs = contract(values, dctx, 1, 1)
            dscore = (probs * (dprobs - jnp.sum(probs * dprobs, axis=0, keepdims=True))).astype(BF16)
            dv_ref[:n] += contract(probs.astype(BF16), dctx, 1, 0)
            dk_ref[:n] += contract(dscore, query, 1, 0)
            dq_ref[choice, rows] = contract(dscore, keys, 0, 0)
    cosine = cos_ref[...]
    sine = -sin_ref[...]
    first = rope_in(dq_ref[0] * scale, cosine, sine)
    second = rope_in(dq_ref[1] * scale, cosine, sine)
    for e in range(experts):
        part = jnp.where(routes_ref[:, 0:1] == e, first, 0.0)
        part = jnp.where(routes_ref[:, 1:2] == e, second, part)
        grad_ref[:, e * width : (e + 1) * width] = part.astype(BF16)
    grad_ref[:, experts * width : (experts + 1) * width] = rope_in(
        dk_ref[...] * scale, cosine, sine
    ).astype(BF16)
    grad_ref[:, (experts + 1) * width :] = dv_ref[...].astype(BF16)


def attn_forward(routes, gates, segments, cosine, sine, qkv, experts):
    length = qkv.shape[0]
    width = HEAD_WIDTH
    heads = qkv.shape[1] // ((experts + 2) * width)
    whole = lambda *shape: pl.BlockSpec(shape, lambda h: (0,) * len(shape))
    head3 = pl.BlockSpec((1, length, width), lambda h: (h, 0, 0))
    head4 = pl.BlockSpec((1, 2, length, width), lambda h: (h, 0, 0, 0))
    cols = lambda parts: pl.BlockSpec((length, parts * width), lambda h: (0, h))
    scores = heads * length * length * 2
    return pl.pallas_call(
        functools.partial(attn_forward_kernel, experts=experts, block=min(256, length), scale=width**-0.5),
        grid=(heads,),
        in_specs=[whole(length, 2), whole(length, 2), whole(length, 1), whole(1, length),
                  whole(length, width), whole(length, width), cols(experts + 2)],
        out_specs=[head4, head3, head3, head4, cols(experts)],
        out_shape=[
            jax.ShapeDtypeStruct((heads, 2, length, width), BF16),
            jax.ShapeDtypeStruct((heads, length, width), BF16),
            jax.ShapeDtypeStruct((heads, length, width), BF16),
            jax.ShapeDtypeStruct((heads, 2, length, width), BF16),
            jax.ShapeDtypeStruct((length, heads * experts * width), BF16),
        ],
        compiler_params=pltpu.CompilerParams(vmem_limit_bytes=48 * 2**20),
        cost_estimate=pl.CostEstimate(flops=scores * width * 8, bytes_accessed=12 * 2**20, transcendentals=scores),
    )(routes, gates, segments[:, None], segments[None, :], cosine, sine, qkv)


def attn_backward(routes, gates, segments, cosine, sine, q, k, v, o, up, experts):
    heads, _, length, width = q.shape
    whole = lambda *shape: pl.BlockSpec(shape, lambda h: (0,) * len(shape))
    head3 = pl.BlockSpec((1, length, width), lambda h: (h, 0, 0))
    head4 = pl.BlockSpec((1, 2, length, width), lambda h: (h, 0, 0, 0))
    cols = lambda parts: pl.BlockSpec((length, parts * width), lambda h: (0, h))
    scores = heads * length * length * 2
    return pl.pallas_call(
        functools.partial(attn_backward_kernel, experts=experts, block=min(256, length), scale=width**-0.5),
        grid=(heads,),
        in_specs=[whole(length, 2), whole(length, 2), whole(length, 1), whole(1, length),
                  whole(length, width), whole(length, width), head4, head3, head3, head4, cols(experts)],
        out_specs=[cols(experts + 2), head3],
        out_shape=[
            jax.ShapeDtypeStruct((length, heads * (experts + 2) * width), BF16),
            jax.ShapeDtypeStruct((heads, length, width), F32),
        ],
        scratch_shapes=[
            pltpu.VMEM((2, length, width), BF16),
            pltpu.VMEM((2, length, width), F32),
            pltpu.VMEM((length, width), F32),
            pltpu.VMEM((length, width), F32),
        ],
        compiler_params=pltpu.CompilerParams(vmem_limit_bytes=48 * 2**20),
        cost_estimate=pl.CostEstimate(flops=scores * width * 20, bytes_accessed=12 * 2**20, transcendentals=scores),
    )(routes, gates, segments[:, None], segments[None, :], cosine, sine, q, k, v, o, up)


def rope_tables(positions, half_dim):
    frequency = THETA_BASE ** (-jnp.arange(half_dim, dtype=F32) / half_dim)
    angles = positions.astype(F32)[:, None] * frequency[None, :]
    return (jnp.cos(angles), jnp.sin(angles))


def norm_forward(values, gain_row):
    inverse = lax.rsqrt(jnp.mean(values * values, axis=-1, keepdims=True) + EPSILON)
    return (values * inverse * gain_row, inverse)


def norm_backward(values, inverse, gain_row, grad_normed):
    scaled = gain_row * grad_normed
    gain_term = jnp.sum(grad_normed * values * inverse, axis=0)
    grad_values = inverse * scaled - values * inverse**3 * jnp.mean(
        scaled * values, axis=-1, keepdims=True
    )
    return (grad_values, gain_term)


def route_onehot(routes, experts):
    return (routes[..., None] == jnp.arange(experts, dtype=jnp.int32)).astype(F32)


def gate_forward(logits, onehot):
    chosen = jnp.sum(logits[:, None, :] * onehot, axis=-1)
    return jax.nn.softmax(chosen, axis=-1)


def gate_backward(gate_probs, grad_gates, onehot):
    centered = gate_probs * (grad_gates - jnp.sum(gate_probs * grad_gates, axis=-1, keepdims=True))
    return jnp.sum(centered[..., None] * onehot, axis=1)


def slot_columns(routes, experts, capacity):
    flat_routes = routes.reshape(-1)
    onehot = (flat_routes[:, None] == jnp.arange(experts, dtype=jnp.int32)[None, :]).astype(
        jnp.int32
    )
    slot_rank = jnp.sum((jnp.cumsum(onehot, axis=0) - 1) * onehot, axis=1)
    return (flat_routes * capacity + slot_rank).reshape(routes.shape)


def dot_f32(left, right):
    return jnp.dot(left, right, preferred_element_type=F32)


def after(value, *others):
    return lax.optimization_barrier((value,) + others)[0]


def shift_planes(value, amount):
    planes = lax.axis_size("expert")
    return lax.ppermute(value, "expert", [(i, (i + amount) % planes) for i in range(planes)])


def exchange_planes(blocks, direction):
    arrived = [blocks[0]]
    for c in range(1, blocks.shape[0]):
        arrived.append(shift_planes(blocks[c], direction * c))
    return jnp.stack(arrived, axis=0)


def gather_planes(value, me):
    planes = lax.axis_size("expert")
    right, left = value, value
    rights, lefts = [], []
    for d in range(1, planes):
        right = lax.ppermute(right, "expert", [(i, i + 1) for i in range(d - 1, planes - 1)])
        left = lax.ppermute(left, "expert", [(i + 1, i) for i in range(0, planes - d)])
        rights.append(right)
        lefts.append(left)
    gathered = [value]
    for c in range(1, planes):
        gathered.append(jnp.where(me + c < planes, lefts[c - 1], rights[planes - c - 1]))
    return gathered


def reduce_planes(parts):
    planes = len(parts)
    right, left = None, None
    for t in range(1, planes):
        send_right, send_left = parts[planes - t], parts[t]
        if right is not None:
            send_right = (send_right.astype(F32) + right.astype(F32)).astype(BF16)
            send_left = (send_left.astype(F32) + left.astype(F32)).astype(BF16)
        right = lax.ppermute(send_right, "expert", [(i, i + 1) for i in range(0, t)])
        left = lax.ppermute(
            send_left, "expert", [(i, i - 1) for i in range(planes - t, planes)]
        )
    return parts[0].astype(F32) + right.astype(F32) + left.astype(F32)


def swap_dp(value, mask):
    size = lax.axis_size("dp")
    return lax.ppermute(value, "dp", [(i, i ^ mask) for i in range(size)])


def all_sum(value, axis):
    size = lax.axis_size(axis)
    mask = 1
    while mask < size:
        value = value + lax.ppermute(value, axis, [(i, i ^ mask) for i in range(size)])
        mask *= 2
    return value


def reduce_rows(left, matmul, me):
    size = lax.axis_size("dp")
    blocks = left.reshape(size // 2, 2, left.shape[0] // size, left.shape[1])
    core, chip = me % 2, me // 2

    def half(index):
        rows = lax.dynamic_index_in_dim(blocks, index, axis=1, keepdims=False)
        return matmul(rows.reshape(-1, left.shape[1])).reshape(size // 2, blocks.shape[2], -1)

    arrived = swap_dp(half(1 - core).astype(BF16), 1)
    mine = half(core) + arrived.astype(F32)
    low = mine.astype(BF16)
    total = lax.dynamic_index_in_dim(low, chip, axis=0, keepdims=False).astype(F32)
    for other in range(1, size // 2):
        send = lax.dynamic_index_in_dim(low, chip ^ other, axis=0, keepdims=False)
        total = total + swap_dp(send, 2 * other).astype(F32)
    return total


def per_device(
    tokens,
    segment_ids,
    attn_routes,
    mlp_routes,
    cotangent,
    attn_gain,
    kv_weights,
    attn_router,
    query_maps,
    output_maps,
    mlp_gain,
    mlp_router,
    gate_up,
    down_maps,
):
    micro_count, seq_count, local_len, width = tokens.shape
    units = micro_count * seq_count
    length = segment_ids.shape[2]
    experts = attn_router.shape[1]
    dp = lax.axis_size("dp")
    planes = lax.axis_size("expert")
    capacity = 2 * local_len // experts
    slots = experts * capacity
    head_cols = width // dp
    heads = head_cols // HEAD_WIDTH
    plane = lax.axis_index("expert")
    my_dp = lax.axis_index("dp")

    tokens = tokens.reshape(units, local_len, width)
    cotangent = cotangent.reshape(units, local_len, width)
    segments = segment_ids.reshape(units, length)
    attn_routes = attn_routes.reshape(units, local_len, 2)
    mlp_routes = mlp_routes.reshape(units, local_len, 2)

    slot_ids = jnp.arange(slots, dtype=jnp.int32)
    hits_list, tables, x_alls, infos = [], [], [], []
    for u in range(units):
        columns = slot_columns((mlp_routes[u] - plane) % experts, experts, capacity)
        hits = (columns[None] == slot_ids[:, None, None]).astype(F32)
        hits_list.append(hits)
        tables.append(jnp.sum(hits, axis=2).astype(BF16))
        other = jnp.sum(hits * mlp_routes[u][None, :, ::-1].astype(F32), axis=(1, 2))
        info = jnp.concatenate([attn_routes[u].astype(F32).reshape(-1), other])
        info = jnp.pad(info, (0, 16 * width - info.shape[0])).reshape(16, width).astype(BF16)
        gathered = lax.all_gather(jnp.concatenate([tokens[u], info], axis=0), "dp", axis=0)
        x_alls.append(gathered[:, :local_len].reshape(length, width))
        infos.append(gathered[:, local_len])
    routes_count = 2 * local_len
    others = jnp.stack([i[:, routes_count : routes_count + slots] for i in infos], axis=0)
    others = others.reshape(units * dp, experts, capacity).transpose(1, 0, 2)
    others = exchange_planes(others, 1)
    other_rows = (
        others.reshape(planes, units, dp, capacity)
        .transpose(1, 2, 0, 3)
        .reshape(units, dp * slots)
        .astype(jnp.int32)
    )

    kv_rows = kv_weights.shape[0]
    query_rows = query_maps.shape[1]
    params = jnp.concatenate(
        [attn_gain[:, None], mlp_gain[:, None], attn_router, mlp_router], axis=1
    ).reshape(-1)
    param_count = params.shape[0]
    params = jnp.pad(params, (0, 16 * head_cols - param_count)).reshape(1, 16, head_cols)
    packed = jnp.concatenate([query_maps[0], kv_weights.reshape(kv_rows * 2, width)], axis=0)
    packed = packed.reshape(-1, dp, head_cols).transpose(1, 0, 2)
    packed = jnp.concatenate([packed, jnp.broadcast_to(params, (dp, 16, head_cols))], axis=1)
    packed = lax.all_to_all(packed, "dp", split_axis=0, concat_axis=0, tiled=True)
    packed = gather_planes(packed, plane)
    output_rows = after(output_maps[0], packed[-1])
    output_rows = gather_planes(output_rows, plane)

    shared = jnp.stack([p[:, query_rows:] for p in packed], axis=0)
    shared = lax.dynamic_slice_in_dim(
        jnp.concatenate([shared, shared], axis=0), (planes - plane) % planes, planes, axis=0
    ).transpose(1, 0, 2, 3)
    kv_cols = shared[:, :, : 2 * kv_rows].reshape(width, 2, heads, HEAD_WIDTH).transpose(0, 2, 1, 3)
    params = shared[:, :, 2 * kv_rows :].reshape(dp * planes, -1)[:, :param_count]
    params = params.reshape(width, 2 + 2 * experts)
    gain_one = params[:, 0].astype(F32)
    gain_two = params[:, 1].astype(F32)
    router_one_low = params[:, 2 : 2 + experts]
    router_two_low = params[:, 2 + experts :]
    router_one = router_one_low.astype(F32)
    router_two = router_two_low.astype(F32)
    query_cols = jnp.stack(
        [p[:, :query_rows].reshape(width, heads, HEAD_WIDTH) for p in packed], axis=2
    )
    qkv_cols = jnp.concatenate([query_cols, kv_cols], axis=2).reshape(width, -1)
    output_rows = jnp.stack(
        [o.reshape(heads, HEAD_WIDTH, width) for o in output_rows], axis=1
    ).reshape(experts * head_cols, width)

    cosine, sine_table = rope_tables(jnp.arange(length, dtype=jnp.int32), HEAD_WIDTH // 2)
    cosine = jnp.concatenate([cosine, cosine], axis=1)
    sine_table = jnp.concatenate([-sine_table, sine_table], axis=1)

    gate_up_local = gate_up[0]
    down_local = down_maps[0]

    def to_experts(slot_rows):
        moved = exchange_planes(slot_rows.reshape(planes, capacity, width), 1)
        return lax.all_gather(moved.reshape(slots, width), "dp", axis=0, tiled=True)

    def to_home(rows):
        return exchange_planes(rows.reshape(planes, capacity, width), -1).reshape(slots, width)

    mixed_parts = []
    input_parts = []
    a_list, g_list, ctx_list, dh_list = [], [], [], []
    b_rows_list, dgate_list, dup_list, hid_list, cot_rows_list = [], [], [], [], []
    a_home_list, dla_list, b_home_list, dlm_list = [], [], [], []
    gain_one_sum = jnp.zeros((width,), F32)
    gain_two_sum = jnp.zeros((width,), F32)
    for u in range(units):
        table = tables[u]
        hits = hits_list[u]
        inputs = tokens[u].astype(F32)
        normed_one, inverse_one = norm_forward(inputs, gain_one)
        a_home = normed_one.astype(BF16)
        a_all = norm_forward(x_alls[u].astype(F32), gain_one)[0].astype(BF16)

        cot = cotangent[u]
        cot_slots = after(dot_f32(table, cot).astype(BF16), output_rows[:16])
        cot_rows = to_experts(cot_slots)
        cot_hidden = jnp.einsum("rd,fd->rf", cot_rows, down_local, preferred_element_type=F32)

        routes_all = infos[u][:, :routes_count].reshape(length, 2).astype(jnp.int32)
        routes_here = (routes_all - plane) % experts
        gates_all = gate_forward(dot_f32(a_all, router_one_low), route_onehot(routes_all, experts))
        qkv = dot_f32(a_all, qkv_cols)
        queries, keys, values, context, context_gated = attn_forward(
            routes_here, gates_all, segments[u], cosine, sine_table, qkv, experts
        )
        hidden_state = inputs + reduce_rows(
            context_gated, lambda rows: dot_f32(rows, output_rows), my_dp
        )

        normed_two, inverse_two = norm_forward(hidden_state, gain_two)
        b_home = normed_two.astype(BF16)
        onehot_mlp = route_onehot(mlp_routes[u], experts)
        gates_mlp = gate_forward(dot_f32(b_home, router_two_low), onehot_mlp)
        b_rows = to_experts(dot_f32(table, b_home).astype(BF16))
        logits_rows = dot_f32(b_rows, router_two_low)
        own_logit = jnp.sum(jnp.where(jnp.arange(experts)[None] == plane, logits_rows, 0.0), axis=1)
        other_logit = jnp.sum(
            jnp.where(jnp.arange(experts)[None] == other_rows[u][:, None], logits_rows, 0.0), axis=1
        )
        gate_rows = jax.nn.sigmoid(own_logit - other_logit)[:, None]
        gate_up_rows = jnp.einsum("rd,fcd->rcf", b_rows, gate_up_local, preferred_element_type=F32)
        gate_val = gate_up_rows[:, 0]
        up_val = gate_up_rows[:, 1]
        sigmoid = jax.nn.sigmoid(gate_val)
        silu = gate_val * sigmoid
        hidden = silu * up_val
        hidden_low = hidden.astype(BF16)
        hidden_gated = (hidden * gate_rows).astype(BF16)
        grad_hidden = cot_hidden * gate_rows
        grad_gate = (grad_hidden * up_val * sigmoid * (1.0 + gate_val * (1.0 - sigmoid))).astype(BF16)
        grad_up = (grad_hidden * silu).astype(BF16)
        hidden_units = gate_val.shape[1]
        out_rows = lax.psum_scatter(
            dot_f32(hidden_low, down_local).astype(BF16), "dp", scatter_dimension=0, tiled=True
        )
        grad_b_rows = reduce_rows(
            jnp.concatenate([grad_gate, grad_up], axis=1),
            lambda rows: jnp.einsum(
                "rcf,fcd->rd",
                rows.reshape(-1, 2, hidden_units),
                gate_up_local,
                preferred_element_type=F32,
            ),
            my_dp,
        ).astype(BF16)
        out_slots = to_home(out_rows)
        grad_b_slots = to_home(grad_b_rows)

        gated_table = jnp.sum(hits * gates_mlp[None], axis=2).T
        gated_high = gated_table.astype(BF16)
        gated_low = (gated_table - gated_high.astype(F32)).astype(BF16)
        mlp_sum = dot_f32(gated_high, out_slots) + dot_f32(gated_low, out_slots)
        mixed_parts.append((hidden_state + mlp_sum).astype(BF16))

        cot_out = jnp.einsum("td,sd->st", cot, out_slots, preferred_element_type=F32)
        grad_gates_mlp = jnp.sum(hits * cot_out[..., None], axis=0)
        dlm = gate_backward(gates_mlp, grad_gates_mlp, onehot_mlp)
        grad_b = jnp.einsum("st,sd->td", table, grad_b_slots, preferred_element_type=F32) + jnp.einsum(
            "re,de->rd", dlm, router_two, precision=PRECISION_TOP
        )
        grad_state, gain_two_term = norm_backward(hidden_state, inverse_two, gain_two, grad_b)
        grad_state = cot.astype(F32) + grad_state
        dh_all = lax.all_gather(grad_state.astype(BF16), "dp", axis=0, tiled=True)

        grad_context = jnp.einsum("td,cd->tc", dh_all, output_rows, preferred_element_type=F32)
        grad_qkv, grad_gates = attn_backward(
            routes_here,
            gates_all,
            segments[u],
            cosine,
            sine_table,
            queries,
            keys,
            values,
            context,
            grad_context,
            experts,
        )
        dga = all_sum(jnp.sum(grad_gates[:, :, :2], axis=0), "dp")
        dga = lax.dynamic_slice_in_dim(dga, my_dp * local_len, local_len, axis=0)
        grad_a = reduce_rows(
            grad_qkv,
            lambda rows: jnp.einsum("tc,dc->td", rows, qkv_cols, preferred_element_type=F32),
            my_dp,
        )
        onehot_home = route_onehot(attn_routes[u], experts)
        gates_home = lax.dynamic_slice_in_dim(gates_all, my_dp * local_len, local_len, axis=0)
        dla = gate_backward(gates_home, dga, onehot_home)
        grad_a = grad_a + jnp.einsum("re,de->rd", dla, router_one, precision=PRECISION_TOP)
        grad_inputs, gain_one_term = norm_backward(inputs, inverse_one, gain_one, grad_a)
        input_parts.append(grad_state + grad_inputs)

        gain_one_sum = gain_one_sum + gain_one_term
        gain_two_sum = gain_two_sum + gain_two_term
        a_list.append(a_all)
        g_list.append(grad_qkv)
        ctx_list.append(context_gated)
        dh_list.append(dh_all)
        b_rows_list.append(b_rows)
        dgate_list.append(grad_gate)
        dup_list.append(grad_up)
        hid_list.append(hidden_gated)
        cot_rows_list.append(cot_rows)
        a_home_list.append(a_home)
        dla_list.append(dla)
        b_home_list.append(b_home)
        dlm_list.append(dlm)

    def summed(pattern, lefts, rights):
        total = None
        for left, right in zip(lefts, rights):
            term = jnp.einsum(pattern, left, right, preferred_element_type=F32)
            total = term if total is None else total + term
        return total

    down_grad = summed("rf,rd->fd", hid_list, cot_rows_list)
    gate_grad = summed("rf,rd->fd", dgate_list, b_rows_list)
    up_grad = summed("rf,rd->fd", dup_list, b_rows_list)
    gate_up_grad = jnp.stack([gate_grad, up_grad], axis=1)

    output_part = summed("tc,td->cd", ctx_list, dh_list).astype(BF16)
    output_part = output_part.reshape(heads, experts, HEAD_WIDTH, width)
    output_grad = reduce_planes([output_part[:, c] for c in range(planes)])
    output_grad = output_grad.reshape(head_cols, width)

    qkv_grad = summed("td,tc->dc", a_list, g_list).astype(BF16)
    qkv_grad = qkv_grad.reshape(width, heads, experts + 2, HEAD_WIDTH)
    kv_part = qkv_grad[:, :, experts:].transpose(0, 2, 1, 3).reshape(dp, planes, 2 * kv_rows, head_cols)
    kv_part = kv_part.transpose(1, 0, 2, 3)
    kv_part = lax.dynamic_slice_in_dim(
        jnp.concatenate([kv_part, kv_part], axis=0), plane, planes, axis=0
    )
    parts = [
        jnp.concatenate([qkv_grad[:, :, c].reshape(dp, query_rows, head_cols), kv_part[c]], axis=1)
        for c in range(planes)
    ]
    packed_grad = reduce_planes(parts).astype(BF16)
    packed_grad = lax.all_to_all(packed_grad, "dp", split_axis=0, concat_axis=0, tiled=True)
    packed_grad = packed_grad.transpose(1, 0, 2).reshape(-1, width).astype(F32)
    query_grad = packed_grad[:query_rows]
    kv_grad = packed_grad[query_rows:].reshape(kv_rows, 2, width)

    router_one_grad = jnp.einsum(
        "re,rd->ed",
        jnp.concatenate(dla_list, axis=0),
        jnp.concatenate(a_home_list, axis=0).astype(F32),
        precision=PRECISION_TOP,
    )
    router_two_grad = jnp.einsum(
        "re,rd->ed",
        jnp.concatenate(dlm_list, axis=0),
        jnp.concatenate(b_home_list, axis=0).astype(F32),
        precision=PRECISION_TOP,
    )
    small_grad = jnp.concatenate(
        [gain_one_sum[None], gain_two_sum[None], router_one_grad, router_two_grad], axis=0
    )
    small_grad = all_sum(all_sum(small_grad, "dp"), "expert")
    small_grad = lax.dynamic_index_in_dim(
        small_grad.reshape(-1, dp * planes, kv_rows), my_dp * planes + plane, axis=1, keepdims=False
    )

    shape = (micro_count, seq_count, local_len, width)
    return (
        jnp.stack(mixed_parts, axis=0).reshape(shape),
        jnp.stack(input_parts, axis=0).reshape(shape),
        small_grad[0],
        kv_grad,
        small_grad[2 : 2 + experts].T,
        query_grad[None],
        output_grad[None],
        small_grad[1],
        small_grad[2 + experts :].T,
        gate_up_grad[None],
        down_grad[None],
    )


def solution(mesh):
    in_specs = (
        P(None, "expert", "dp", None),
        P(None, "expert", None),
        P(None, "expert", "dp", None),
        P(None, "expert", "dp", None),
        P(None, "expert", "dp", None),
        P(("dp", "expert")),
        P(("dp", "expert"), None, None),
        P(("dp", "expert"), None),
        P("expert", "dp", None),
        P("expert", "dp", None),
        P(("dp", "expert")),
        P(("dp", "expert"), None),
        P("expert", "dp", None, None),
        P("expert", "dp", None),
    )
    out_specs = (
        P(None, "expert", "dp", None),
        P(None, "expert", "dp", None),
        P(("dp", "expert")),
        P(("dp", "expert"), None, None),
        P(("dp", "expert"), None),
        P("expert", "dp", None),
        P("expert", "dp", None),
        P(("dp", "expert")),
        P(("dp", "expert"), None),
        P("expert", "dp", None, None),
        P("expert", "dp", None),
    )
    return jax.shard_map(
        per_device, mesh=mesh, in_specs=in_specs, out_specs=out_specs, check_vma=False
    )
```

time: 1840 us -> 1560 us (0.85)
  waiting for transfers between devices: 726 us -> 537 us
  blocking collectives: 207 us -> 31.8 us
  starting transfers between devices: 28 us -> 150 us
  matrix products: 456 us -> 362 us
  Pallas kernels: 0 us -> 72.9 us
  other arithmetic: 162 us -> 140 us
    ppermute x0 -> x86, waiting for transfers between devices: none -> 457 us  [the longest x24 154 us: swap_dp(): return lax.ppermute(value, 'dp', [(i, i ^ mask) for i in range(size)])]
    reduce_scatter x8 -> x0, waiting for transfers between devices: 237 us -> none  [the longest x2 79.6 us: per_device(): lax.psum_scatter(jnp.einsum('rcf,fcd->rd', jnp.stack([grad_gate, grad_up]...]
    ppermute x0 -> x86, starting transfers between devices: none -> 145 us  [the longest x27 40.1 us: shift_planes(): lax.ppermute(value, 'expert', [(i, (i + amount) % planes) for i in range(...]
    reduce_scatter x2, waiting for transfers between devices: 139 us -> 0.01 us  [per_device(): lax.psum_scatter(dot_f32(hidden_low, down_local).astype(BF16), 'dp', scat...]
    unnamed x26 -> x10, waiting for transfers between devices: 129 us -> 0.16 us
    all_to_all x5 -> x1, blocking collectives: 141 us -> 31.8 us  [per_device(): lax.all_to_all(packed, 'dp', split_axis=0, concat_axis=0, tiled=True)]
    all_gather x8 -> x6, waiting for transfers between devices: 167 us -> 79.6 us  [the longest x4 79.5 us: to_experts(): return lax.all_gather(moved.reshape(slots, width), 'dp', axis=0, tiled=True)]
    dot_general x18 -> x10, matrix products: 147 us -> 70.5 us  [the longest x4 45.4 us: per_device(): jnp.einsum('rcf,fcd->rd', rows.reshape(-1, 2, hidden_units), gate_up_loca...]
  transfers between devices with their start and end apart: 28 -> 97, of which waited for: 16 -> 61; matrix products, arithmetic and copies ran while one was open for 39% -> 41% of each run, Pallas kernels for 0% -> 3%
where the time goes in v2:
time: 1560 us; the launch traced here: 1540 us
  waiting for transfers between devices  537 us (34%)
  matrix products  362 us (23%)
  local copies, waits for them, and re-layouts  231 us (15%)
  starting transfers between devices  150 us (10%)
  other arithmetic  140 us (9%)
  Pallas kernels  72.9 us (5%)
  blocking collectives  31.8 us (2%)
  between operations  17.6 us (1%)
    ppermute x24, waiting for transfers between devices, swap_dp(): return lax.ppermute(value, 'dp', [(i, i ^ mask) for i in range(size)])  154 us
    ppermute x27, waiting for transfers between devices, shift_planes(): lax.ppermute(value, 'expert', [(i, (i + amount) % planes) for i in range(...  152 us
    dot_general x10, matrix products, summed(): term = jnp.einsum(pattern, left, right, preferred_element_type=F32)  103 us
    dot_general x22, matrix products, dot_f32(): return jnp.dot(left, right, preferred_element_type=F32)  90.7 us
    ppermute x6, waiting for transfers between devices, gather_planes(): lax.ppermute(left, 'expert', [(i + 1, i) for i in range(0, planes - d)])  86.2 us
    all_gather x4, waiting for transfers between devices, to_experts(): return lax.all_gather(moved.reshape(slots, width), 'dp', axis=0, tiled=True)  79.5 us
    unnamed x384, local copies, waits for them, and re-layouts  70.4 us
    dot_general x4, matrix products, per_device(): jnp.einsum('rcf,fcd->rd', rows.reshape(-1, 2, hidden_units), gate_up_loca...  45.4 us
  transfers between devices with their start and end apart: 97, of which 61 were waited for; matrix products, arithmetic and copies ran while one was open for 41% of the time, Pallas kernels for 3%

profile of v2, /device:TPU:8, one launch (start us, length us, event | category | flops | bytes accessed | tf_op | source)
XLA Modules:
  0.0 1541.5 jit_solution(3415983120769615424)
XLA Ops:
  22.5 31.8 %all_to_all.10 = bf16[8,400,256]{2,1,0:T(8,128)(2,1)} all-to-all(bf16[8,400,256]{2,1,0:T(8,128)(2,1)S(1)} %pad_maximum_fusion.3), channel_id=1, replica_groups=mesh['dp'=8,'expert'=4] {'dp'}, dimensions={0} | all-to-all | bytes 3276800 | tf_op jit(solution)/shard_map/all_to_all | solution.py:373
  61.8 32.2 %collective-permute-done = bf16[8,400,256]{2,1,0:T(8,128)(2,1)} collective-permute-done((bf16[8,400,256]{2,1,0:T(8,128)(2,1)}, bf16[8,400,256]{2,1,0:T(8,128)(2,1)}, u32[]{:S(2)}, u32[]{:S(2)}) %collective-permute-start) | collective-permute-done | bytes 1638432 | tf_op jit(solution)/shard_map/ppermute | solution.py:247
  104.8 28.0 %collective-permute-done.4 = bf16[8,400,256]{2,1,0:T(8,128)(2,1)} collective-permute-done((bf16[8,400,256]{2,1,0:T(8,128)(2,1)}, bf16[8,400,256]{2,1,0:T(8,128)(2,1)}, u32[]{:S(2)}, u32[]{:S(2)}) %collective-permute-start.4) | collective-permute-done | bytes 1638432 | tf_op jit(solution)/shard_map/ppermute | solution.py:247
  210.5 16.3 %copy.470 = bf16[2048,2,6,128]{0,3,2,1:T(8,128)(2,1)} copy(bf16[2048,2,6,128]{3,1,2,0:T(2,128)(2,1)} %bitcast_dynamic-update-slice_fusion) | data formatting | bytes 12582912 | tf_op jit(solution)/shard_map/concatenate | solution.py:394
  309.3 17.2 %shard_map.222 = (bf16[2,2,1024,128]{3,2,1,0:T(8,128)(2,1)S(1)}, bf16[2,1024,128]{2,1,0:T(8,128)(2,1)S(1)}, bf16[2,1024,128]{2,1,0:T(8,128)(2,1)S(1)}, bf16[2,2,...) custom-call(s32[1024,2]{1,0:T(8,128)S(1)} %add_select_fusion.routes_ref, f32[1024,2]{1,0:T(8,128)S(1)} %exponential_divide_fusion.gates_ref, ...), custom_call_target="tpu_custom_call" | custom-call | flops 4294967296 | bytes 12582912 | tf_op jit(solution)/shard_map/pallas_call | solution.py:132
  330.6 15.8 %collective-permute-done.11 = bf16[256,2048]{1,0:T(8,128)(2,1)S(1)} collective-permute-done((bf16[256,2048]{1,0:T(8,128)(2,1)}, bf16[256,2048]{1,0:T(8,128)(2,1)S(1)}, u32[]{:S(2)}, u32[]{:S(2)}) %collective-permute-start.11) | collective-permute-done | bytes 1048608 | tf_op jit(solution)/shard_map/ppermute | solution.py:247
  353.8 17.1 %shard_map.221 = (bf16[2,2,1024,128]{3,2,1,0:T(8,128)(2,1)S(1)}, bf16[2,1024,128]{2,1,0:T(8,128)(2,1)S(1)}, bf16[2,1024,128]{2,1,0:T(8,128)(2,1)S(1)}, bf16[2,2,...) custom-call(s32[1024,2]{1,0:T(8,128)S(1)} %copy-done.14, f32[1024,2]{1,0:T(8,128)S(1)} %exponential_divide_fusion.1.gates_ref, ...), custom_call_target="tpu_custom_call" | custom-call | flops 4294967296 | bytes 12582912 | tf_op jit(solution)/shard_map/pallas_call | solution.py:132
  444.2 17.3 %collective-permute-done.18 = bf16[64,2048]{1,0:T(8,128)(2,1)S(1)} collective-permute-done((bf16[64,2048]{1,0:T(8,128)(2,1)S(1)}, bf16[64,2048]{1,0:T(8,128)(2,1)S(1)}, u32[]{:S(2)}, u32[]{:S(2)}) %collective-permute-start.18) | collective-permute-done | bytes 262176 | tf_op jit(solution)/shard_map/ppermute | solution.py:231
  501.8 18.0 %all-gather.11.cloned.1.call-done = bf16[2048,2048]{1,0:T(8,128)(2,1)} async-done(((bf16[256,2048]{1,0:T(8,128)(2,1)}), bf16[2048,2048]{1,0:T(8,128)(2,1)}) %all-gather.11.cloned.1.call-update) | async-done | bytes 8388624 | tf_op jit(solution)/shard_map/all_gather | solution.py:408
  525.8 19.8 %fusion.36 = f32[2048,2,704]{0,2,1:T(8,128)} fusion(bf16[2048,2048]{1,0:T(8,128)(2,1)S(1)} %copy-done.45, bf16[704,2,2048]{2,1,0:T(2,128)(2,1)} %bitcast.861), kind=kOutput, calls=%fused_computation.70 | convolution fusion | flops 11811160064 | bytes 25690112 | tf_op jit(solution)/shard_map/rd,fcd->rcf/dot_general | solution.py:455
  559.2 17.3 %all-gather.15.cloned.1.call-done = bf16[2048,2048]{1,0:T(8,128)(2,1)} async-done(((bf16[256,2048]{1,0:T(8,128)(2,1)}), bf16[2048,2048]{1,0:T(8,128)(2,1)}) %all-gather.15.cloned.1.call-update) | async-done | bytes 8388624 | tf_op jit(solution)/shard_map/all_gather | solution.py:408
  653.7 21.5 %collective-permute-done.39 = bf16[256,2048]{1,0:T(8,128)(2,1)} collective-permute-done((bf16[256,2048]{1,0:T(8,128)(2,1)}, bf16[256,2048]{1,0:T(8,128)(2,1)}, u32[]{:S(2)}, u32[]{:S(2)}) %collective-permute-start.39) | collective-permute-done | bytes 1048608 | tf_op jit(solution)/shard_map/ppermute | solution.py:273
  675.1 22.5 %collective-permute-done.41 = bf16[256,2048]{1,0:T(8,128)(2,1)} collective-permute-done((bf16[256,2048]{1,0:T(8,128)(2,1)}, bf16[256,2048]{1,0:T(8,128)(2,1)}, u32[]{:S(2)}, u32[]{:S(2)}) %collective-permute-start.41) | collective-permute-done | bytes 1048608 | tf_op jit(solution)/shard_map/ppermute | solution.py:273
  722.8 16.8 %collective-permute-done.43 = bf16[64,2048]{1,0:T(8,128)(2,1)} collective-permute-done((bf16[64,2048]{1,0:T(8,128)(2,1)}, bf16[64,2048]{1,0:T(8,128)(2,1)}, u32[]{:S(2)}, u32[]{:S(2)}) %collective-permute-start.43) | collective-permute-done | bytes 262176 | tf_op jit(solution)/shard_map/ppermute | solution.py:231
  762.0 16.0 %collective-permute-done.28 = bf16[64,2048]{1,0:T(8,128)(2,1)S(1)} collective-permute-done((bf16[64,2048]{1,0:T(8,128)(2,1)S(1)}, bf16[64,2048]{1,0:T(8,128)(2,1)S(1)}, u32[]{:S(2)}, u32[]{:S(2)}) %collective-permute-start.28) | collective-permute-done | bytes 262176 | tf_op jit(solution)/shard_map/ppermute | solution.py:231
  809.7 27.1 %all-gather.13.cloned.1.call-done = bf16[2048,2048]{1,0:T(8,128)(2,1)} async-done(((bf16[256,2048]{1,0:T(8,128)(2,1)}), bf16[2048,2048]{1,0:T(8,128)(2,1)}) %all-gather.13.cloned.1.call-update) | async-done | bytes 8388624 | tf_op jit(solution)/shard_map/all_gather | solution.py:408
  842.8 19.7 %fusion.39 = f32[2048,2,704]{0,2,1:T(8,128)} fusion(bf16[2048,2048]{1,0:T(8,128)(2,1)S(1)} %copy-done.46, bf16[704,2,2048]{2,1,0:T(2,128)(2,1)} %bitcast.863), kind=kOutput, calls=%fused_computation.71 | convolution fusion | flops 11811160064 | bytes 25690112 | tf_op jit(solution)/shard_map/rd,fcd->rcf/dot_general | solution.py:455
  876.2 17.1 %all-gather.19.cloned.1.call-done = bf16[2048,2048]{1,0:T(8,128)(2,1)} async-done(((bf16[256,2048]{1,0:T(8,128)(2,1)}), bf16[2048,2048]{1,0:T(8,128)(2,1)}) %all-gather.19.cloned.1.call-update) | async-done | bytes 8388624 | tf_op jit(solution)/shard_map/all_gather | solution.py:408
  924.2 14.4 constant_dynamic-slice_fusion.5
  1002.5 22.5 %collective-permute-done.58 = bf16[256,2048]{1,0:T(8,128)(2,1)} collective-permute-done((bf16[256,2048]{1,0:T(8,128)(2,1)}, bf16[256,2048]{1,0:T(8,128)(2,1)}, u32[]{:S(2)}, u32[]{:S(2)}) %collective-permute-start.58) | collective-permute-done | bytes 1048608 | tf_op jit(solution)/shard_map/ppermute | solution.py:273
  1049.2 17.0 %collective-permute-done.60 = bf16[64,2048]{1,0:T(8,128)(2,1)} collective-permute-done((bf16[64,2048]{1,0:T(8,128)(2,1)S(1)}, bf16[64,2048]{1,0:T(8,128)(2,1)}, u32[]{:S(2)}, u32[]{:S(2)}) %collective-permute-start.60) | collective-permute-done | bytes 262176 | tf_op jit(solution)/shard_map/ppermute | solution.py:231
  1137.4 20.9 %copy.522 = f32[1,704,2,2048]{3,2,1,0:T(2,128)} copy(f32[1,704,2,2048]{3,1,2,0:T(8,128)} %maximum_bitcast_fusion) | data formatting | bytes 23068672
  1184.8 19.3 %shard_map.223 = (bf16[1024,1536]{1,0:T(8,128)(2,1)}, f32[2,1024,128]{2,1,0:T(8,128)S(1)}) custom-call(s32[1024,2]{1,0:T(8,128)S(1)} %copy-done.15, f32[1024,2]{1,0:T(8,128)S(1)} %copy-done.3, s32[1024,1]{1,0:T(8,128)S(1)} %copy-done.13, s32[1,1024]{1,0:T(1,128)S(1)} %get-tuple-element.261.seg_row_ref, f32[1024,128]{1,0:T(8,128)S(1)} %copy-done.6, ...), custom_call_target="tpu_custom_call" | custom-call | flops 10737418240 | bytes 12582912 | tf_op jit(solution)/shard_map/pallas_call | solution.py:157
  1226.1 19.2 %shard_map.224 = (bf16[1024,1536]{1,0:T(8,128)(2,1)}, f32[2,1024,128]{2,1,0:T(8,128)S(1)}) custom-call(s32[1024,2]{1,0:T(8,128)S(1)} %copy-done.17, f32[1024,2]{1,0:T(8,128)S(1)} %exponential_divide_fusion.gates_ref, s32[1024,1]{1,0:T(8,128)S(1)} %copy-done.11, s32[1,1024]{1,0:T(1,128)S(1)} %get-tuple-element.262.seg_row_ref, f32[1024,128]{1,0:T(8,128)S(1)} %copy-done.6, ...), custom_call_target="tpu_custom_call" | custom-call | flops 10737418240 | bytes 12582912 | tf_op jit(solution)/shard_map/pallas_call | solution.py:157
  (887 shorter events, 1039.1 us)
Async XLA Ops:
  7.2 226.0 %all-gather.23.cloned.1.call-start = ((), (), s32[]{:S(2)}) async-start(), calls=%async_computation.12 | async-start | bytes 5308416 | tf_op jit(solution)/shard_map/all_gather | solution.py:349
  18.6 225.1 %all-gather.25.cloned.1.call-start = ((), (), s32[]{:S(2)}) async-start(), calls=%async_computation.13 | async-start | bytes 5308416 | tf_op jit(solution)/shard_map/all_gather | solution.py:349
  98.8 421.0 %all-gather.11.cloned.1.call-start = ((), (), s32[]{:S(2)}) async-start(), calls=%async_computation.4 | async-start | bytes 9437184 | tf_op jit(solution)/shard_map/all_gather | solution.py:408
  171.2 56.8 %collective-permute-start.7 = (bf16[256,2048]{1,0:T(8,128)(2,1)}, bf16[256,2048]{1,0:T(8,128)(2,1)}, u32[]{:S(2)}, u32[]{:S(2)}) collective-permute-start(bf16[256,2048]{1,0:T(8,128)(2,1)} %bitcast.29), channel_id=1, source_target_pairs={{0,1},{1,2},{2,3},{4,5},{5,6},{6,7},{8,9},{9,10},{10,11},{12,13},{... | collective-permute-start | bytes 3145736 | tf_op jit(solution)/shard_map/ppermute | solution.py:246
  173.3 58.1 %collective-permute-start.6 = (bf16[256,2048]{1,0:T(8,128)(2,1)}, bf16[256,2048]{1,0:T(8,128)(2,1)}, u32[]{:S(2)}, u32[]{:S(2)}) collective-permute-start(bf16[256,2048]{1,0:T(8,128)(2,1)} %bitcast.29), channel_id=1, source_target_pairs={{1,0},{2,1},{3,2},{5,4},{6,5},{7,6},{9,8},{10,9},{11,10},{13,12},{... | collective-permute-start | bytes 3145736 | tf_op jit(solution)/shard_map/ppermute | solution.py:247
  228.0 76.0 %collective-permute-start.8 = (bf16[256,2048]{1,0:T(8,128)(2,1)}, bf16[256,2048]{1,0:T(8,128)(2,1)}, u32[]{:S(2)}, u32[]{:S(2)}) collective-permute-start(bf16[256,2048]{1,0:T(8,128)(2,1)} %collective-permute-done.7), channel_id=1, source_target_pairs={{1,2},{2,3},{5,6},{6,7},{9,10},{10,11},{13,14},{14,15},{17,18},{18... | collective-permute-start | bytes 3145736 | tf_op jit(solution)/shard_map/ppermute | solution.py:246
  231.3 95.2 %collective-permute-start.10 = (bf16[256,2048]{1,0:T(8,128)(2,1)}, bf16[256,2048]{1,0:T(8,128)(2,1)}, u32[]{:S(2)}, u32[]{:S(2)}) collective-permute-start(bf16[256,2048]{1,0:T(8,128)(2,1)} %collective-permute-done.6), channel_id=1, source_target_pairs={{1,0},{2,1},{5,4},{6,5},{9,8},{10,9},{13,12},{14,13},{17,16},{18,1... | collective-permute-start | bytes 3145736 | tf_op jit(solution)/shard_map/ppermute | solution.py:247
  464.8 111.7 %all-gather.15.cloned.1.call-start = ((), (), s32[]{:S(2)}) async-start(), calls=%async_computation.8 | async-start | bytes 9437184 | tf_op jit(solution)/shard_map/all_gather | solution.py:408
  491.1 216.2 %reduce-scatter.3.cloned.1.call-start = ((), (), s32[]{:S(2)}) async-start(), calls=%async_computation.5 | async-start | bytes 9437184 | tf_op jit(solution)/shard_map/reduce_scatter | solution.py:467
  559.1 277.7 %all-gather.13.cloned.1.call-start = ((), (), s32[]{:S(2)}) async-start(), calls=%async_computation.6 | async-start | bytes 9437184 | tf_op jit(solution)/shard_map/all_gather | solution.py:408
  651.5 47.5 %collective-permute-start.40 = (bf16[256,2048]{1,0:T(8,128)(2,1)}, bf16[256,2048]{1,0:T(8,128)(2,1)}, u32[]{:S(2)}, u32[]{:S(2)}) collective-permute-start(bf16[256,2048]{1,0:T(8,128)(2,1)} %get-tuple-element.178), channel_id=1, source_target_pairs={{0,16},{4,20},{8,24},{12,28},{16,0},{20,4},{24,8},{28,12},{1,17},{... | collective-permute-start | bytes 3145736 | tf_op jit(solution)/shard_map/ppermute | solution.py:273
  781.6 111.7 %all-gather.19.cloned.1.call-start = ((), (), s32[]{:S(2)}) async-start(), calls=%async_computation.10 | async-start | bytes 9437184 | tf_op jit(solution)/shard_map/all_gather | solution.py:408
  809.6 224.7 %reduce-scatter.5.cloned.1.call-start = ((), (), s32[]{:S(2)}) async-start(), calls=%async_computation.7 | async-start | bytes 9437184 | tf_op jit(solution)/shard_map/reduce_scatter | solution.py:467
  876.1 298.5 %all-gather.17.cloned.1.call-start = ((), (), s32[]{:S(2)}) async-start(), calls=%async_computation.9 | async-start | bytes 4718592 | tf_op jit(solution)/shard_map/all_gather | solution.py:497
  1082.4 133.5 %all-gather.21.cloned.1.call-start = ((), (), s32[]{:S(2)}) async-start(), calls=%async_computation.11 | async-start | bytes 4718592 | tf_op jit(solution)/shard_map/all_gather | solution.py:497
  1267.1 49.1 %collective-permute-start.49 = (f32[1024,2]{1,0:T(8,128)}, f32[1024,2]{1,0:T(8,128)}, u32[]{:S(2)}, u32[]{:S(2)}) collective-permute-start(f32[1024,2]{1,0:T(8,128)} %slice_reduce_fusion.1), channel_id=1, source_target_pairs={{0,4},{4,0},{8,12},{12,8},{16,20},{20,16},{24,28},{28,24},{1,5},{5... | collective-permute-start | bytes 24584 | tf_op jit(solution)/shard_map/ppermute | solution.py:280
  1267.1 53.1 %collective-permute-start.66 = (f32[1024,2]{1,0:T(8,128)}, f32[1024,2]{1,0:T(8,128)}, u32[]{:S(2)}, u32[]{:S(2)}) collective-permute-start(f32[1024,2]{1,0:T(8,128)} %slice_reduce_fusion), channel_id=1, source_target_pairs={{0,4},{4,0},{8,12},{12,8},{16,20},{20,16},{24,28},{28,24},{1,5},{5... | collective-permute-start | bytes 24584 | tf_op jit(solution)/shard_map/ppermute | solution.py:280
  1275.0 94.4 %collective-permute-start.62 = (bf16[4,128,2048]{2,1,0:T(8,128)(2,1)}, bf16[4,128,2048]{2,1,0:T(8,128)(2,1)}, u32[]{:S(2)}, u32[]{:S(2)}) collective-permute-start(bf16[4,128,2048]{2,1,0:T(8,128)(2,1)} %convolution_convert_fusion.4), channel_id=1, source_target_pairs={{0,4},{4,0},{8,12},{12,8},{16,20},{20,16},{24,28},{28,24},{1,5},{5... | collective-permute-start | bytes 6291464 | tf_op jit(solution)/shard_map/ppermute | solution.py:273
  1296.3 66.6 %collective-permute-start.74 = (bf16[8,384,256]{2,1,0:T(8,128)(2,1)}, bf16[8,384,256]{2,1,0:T(8,128)(2,1)}, u32[]{:S(2)}, u32[]{:S(2)}) collective-permute-start(bf16[8,384,256]{2,1,0:T(8,128)(2,1)} %pad_maximum_fusion.6), channel_id=1, source_target_pairs={{0,1},{4,5},{8,9},{12,13},{16,17},{20,21},{24,25},{28,29}} | collective-permute-start | bytes 4718600 | tf_op jit(solution)/shard_map/ppermute | solution.py:264
  1300.1 63.8 %collective-permute-start.77 = (bf16[8,384,256]{2,1,0:T(8,128)(2,1)}, bf16[8,384,256]{2,1,0:T(8,128)(2,1)}, u32[]{:S(2)}, u32[]{:S(2)}) collective-permute-start(bf16[8,384,256]{2,1,0:T(8,128)(2,1)} %pad_maximum_fusion.4), channel_id=1, source_target_pairs={{3,2},{7,6},{11,10},{15,14},{19,18},{23,22},{27,26},{31,30}} | collective-permute-start | bytes 4718600 | tf_op jit(solution)/shard_map/ppermute | solution.py:265
  1366.5 66.4 %collective-permute-start.75 = (bf16[8,384,256]{2,1,0:T(8,128)(2,1)S(1)}, bf16[8,384,256]{2,1,0:T(8,128)(2,1)S(1)}, u32[]{:S(2)}, u32[]{:S(2)}) collective-permute-start(bf16[8,384,256]{2,1,0:T(8,128)(2,1)S(1)} %get-tuple-element.198), channel_id=1, source_target_pairs={{0,1},{1,2},{4,5},{5,6},{8,9},{9,10},{12,13},{13,14},{16,17},{17,1... | collective-permute-start | bytes 4718600 | tf_op jit(solution)/shard_map/ppermute | solution.py:264
  1436.3 50.8 %collective-permute-start.79 = (bf16[8,384,256]{2,1,0:T(8,128)(2,1)S(1)}, bf16[8,384,256]{2,1,0:T(8,128)(2,1)S(1)}, u32[]{:S(2)}, u32[]{:S(2)}) collective-permute-start(bf16[8,384,256]{2,1,0:T(8,128)(2,1)S(1)} %add_convert_fusion.7), channel_id=1, source_target_pairs={{1,0},{2,1},{3,2},{5,4},{6,5},{7,6},{9,8},{10,9},{11,10},{13,12},{... | collective-permute-start | bytes 4718600 | tf_op jit(solution)/shard_map/ppermute | solution.py:265
  1455.6 61.9 %collective-permute-start.82 = (bf16[2,128,2048]{2,1,0:T(8,128)(2,1)}, bf16[2,128,2048]{2,1,0:T(8,128)(2,1)}, u32[]{:S(2)}, u32[]{:S(2)}) collective-permute-start(bf16[2,128,2048]{2,1,0:T(8,128)(2,1)} %get-tuple-element.170), channel_id=1, source_target_pairs={{0,1},{1,2},{2,3},{4,5},{5,6},{6,7},{8,9},{9,10},{10,11},{12,13},{... | collective-permute-start | bytes 3145736 | tf_op jit(solution)/shard_map/ppermute | solution.py:264
  1457.9 59.6 %collective-permute-start.85 = (bf16[2,128,2048]{2,1,0:T(8,128)(2,1)}, bf16[2,128,2048]{2,1,0:T(8,128)(2,1)}, u32[]{:S(2)}, u32[]{:S(2)}) collective-permute-start(bf16[2,128,2048]{2,1,0:T(8,128)(2,1)} %get-tuple-element.171), channel_id=1, source_target_pairs={{1,0},{2,1},{3,2},{5,4},{6,5},{7,6},{9,8},{10,9},{11,10},{13,12},{... | collective-permute-start | bytes 3145736 | tf_op jit(solution)/shard_map/ppermute | solution.py:265
  (252 other events, 5506.5 us)
Sparse Core Ops, SparseCore 0:
  18.7 53.0 all-gather.22
  98.9 38.5 all-gather.24
  464.9 54.8 all-gather.10
  522.1 54.3 all-gather.14
  579.8 71.2 reduce-scatter.2
  781.7 55.0 all-gather.12
  838.9 54.3 all-gather.18
  897.2 71.3 reduce-scatter.4
  1082.5 37.0 all-gather.16
  1126.8 37.0 all-gather.20

commit v3 on v2

v3 whole, which is shorter than its diff:
```python
import functools

import jax
import jax.numpy as jnp
from jax import lax
from jax.experimental import pallas as pl
from jax.experimental.pallas import tpu as pltpu
from jax.sharding import PartitionSpec as P

HEAD_WIDTH = 128


EPSILON = 1e-05
THETA_BASE = 10000.0
NEGATIVE = -1000000000.0
PRECISION_TOP = lax.Precision.HIGHEST
BF16 = jnp.bfloat16
F32 = jnp.float32


def rope_in(values, cosine, sine_signed):
    return values * cosine + pltpu.roll(values, HEAD_WIDTH // 2, 1) * sine_signed


def contract(left, right, left_dim, right_dim):
    return lax.dot_general(
        left, right, (((left_dim,), (right_dim,)), ((), ())), preferred_element_type=F32
    )


def block_mask(seg_col_ref, seg_row_ref, i, block):
    n = (i + 1) * block
    rows = slice(i * block, n)
    return (
        lax.broadcasted_iota(jnp.int32, (n, block), 0)
        <= lax.broadcasted_iota(jnp.int32, (n, block), 1) + i * block
    ) & (seg_col_ref[:n, :] == seg_row_ref[:, rows])


def key_softmax(score):
    exponent = jnp.exp(score - jnp.max(score, axis=0, keepdims=True))
    return exponent * (1.0 / jnp.sum(exponent, axis=0, keepdims=True))


def attn_forward_kernel(*refs, experts, heads, block, scale):
    routes_ref, gates_ref, seg_col_ref, seg_row_ref, cos_ref, sin_ref, keys_ref, values_ref = refs[:8]
    raw_refs = refs[8 : 8 + experts]
    q_ref, k_ref, v_ref, o_ref, gated_ref = refs[8 + experts :]
    length = cos_ref.shape[0]
    width = HEAD_WIDTH
    cosine = cos_ref[...]
    sine = sin_ref[...]
    routes = [routes_ref[:, c : c + 1] for c in range(2)]
    for h in range(heads):
        cols = slice(h * width, (h + 1) * width)
        k_ref[h] = rope_in(keys_ref[:, cols], cosine, sine).astype(BF16)
        v_ref[h] = values_ref[:, cols]
        for choice in range(2):
            raw = raw_refs[0][:, cols].astype(F32)
            for e in range(1, experts):
                raw = jnp.where(routes[choice] == e, raw_refs[e][:, cols].astype(F32), raw)
            q_ref[h, choice] = rope_in(raw, cosine, sine).astype(BF16)
    for i in range(length // block):
        rows = slice(i * block, (i + 1) * block)
        n = (i + 1) * block
        mask = block_mask(seg_col_ref, seg_row_ref, i, block)
        for h in range(heads):
            for choice in range(2):
                score = contract(k_ref[h, :n], q_ref[h, choice, rows], 1, 1) * scale
                probs = key_softmax(jnp.where(mask, score, NEGATIVE)).astype(BF16)
                o_ref[h, choice, rows] = contract(probs, v_ref[h, :n], 0, 0).astype(BF16)
    for h in range(heads):
        first = o_ref[h, 0].astype(F32) * gates_ref[:, 0:1]
        second = o_ref[h, 1].astype(F32) * gates_ref[:, 1:2]
        for e in range(experts):
            part = jnp.where(routes[0] == e, first, 0.0)
            part = jnp.where(routes[1] == e, second, part)
            at = (e * heads + h) * width
            gated_ref[:, at : at + width] = part.astype(BF16)


def attn_backward_kernel(
    routes_ref, gates_ref, seg_col_ref, seg_row_ref, cos_ref, sin_ref, q_ref, k_ref, v_ref, o_ref, up_ref,
    grad_ref, dctx_ref, dq_ref, dk_ref, dv_ref, *, experts, heads, block, scale,
):
    length = cos_ref.shape[0]
    width = HEAD_WIDTH
    lanes = lax.broadcasted_iota(jnp.int32, (length, width), 1)
    routes = [routes_ref[:, c : c + 1] for c in range(2)]
    dgate = jnp.zeros((length, width), F32)
    for h in range(heads):
        for choice in range(2):
            up = up_ref[:, h * width : (h + 1) * width]
            for e in range(1, experts):
                at = (e * heads + h) * width
                up = jnp.where(routes[choice] == e, up_ref[:, at : at + width], up)
            part = jnp.sum(up * o_ref[h, choice].astype(F32), axis=1, keepdims=True)
            dgate = dgate + jnp.where(lanes == choice, part, 0.0)
            dctx_ref[h, choice] = (up * gates_ref[:, choice : choice + 1]).astype(BF16)
    grad_ref[:, (experts + 2) * heads * width :] = dgate.astype(BF16)
    dk_ref[...] = jnp.zeros_like(dk_ref)
    dv_ref[...] = jnp.zeros_like(dv_ref)
    for i in range(length // block):
        rows = slice(i * block, (i + 1) * block)
        n = (i + 1) * block
        mask = block_mask(seg_col_ref, seg_row_ref, i, block)
        for h in range(heads):
            for choice in range(2):
                query = q_ref[h, choice, rows]
                dctx = dctx_ref[h, choice, rows]
                score = contract(k_ref[h, :n], query, 1, 1) * scale
                probs = key_softmax(jnp.where(mask, score, NEGATIVE))
                dprobs = contract(v_ref[h, :n], dctx, 1, 1)
                dscore = probs * (dprobs - jnp.sum(probs * dprobs, axis=0, keepdims=True))
                dscore = dscore.astype(BF16)
                dv_ref[h, :n] += contract(probs.astype(BF16), dctx, 1, 0)
                dk_ref[h, :n] += contract(dscore, query, 1, 0)
                dq_ref[h, choice, rows] = contract(dscore, k_ref[h, :n], 0, 0)
    cosine = cos_ref[...]
    sine = -sin_ref[...]
    for h in range(heads):
        first = rope_in(dq_ref[h, 0] * scale, cosine, sine)
        second = rope_in(dq_ref[h, 1] * scale, cosine, sine)
        for e in range(experts):
            part = jnp.where(routes[0] == e, first, 0.0)
            part = jnp.where(routes[1] == e, second, part)
            at = (e * heads + h) * width
            grad_ref[:, at : at + width] = part.astype(BF16)
        at = (experts * heads + h) * width
        grad_ref[:, at : at + width] = rope_in(dk_ref[h] * scale, cosine, sine).astype(BF16)
        at = ((experts + 1) * heads + h) * width
        grad_ref[:, at : at + width] = dv_ref[h].astype(BF16)


def attn_forward(routes, gates, segments, cosine, sine, raws, keys, values):
    experts = len(raws)
    length, cols = raws[0].shape
    width = HEAD_WIDTH
    heads = cols // width
    scores = heads * length * length * 2
    return pl.pallas_call(
        functools.partial(
            attn_forward_kernel,
            experts=experts,
            heads=heads,
            block=min(256, length),
            scale=width**-0.5,
        ),
        out_shape=[
            jax.ShapeDtypeStruct((heads, 2, length, width), BF16),
            jax.ShapeDtypeStruct((heads, length, width), BF16),
            jax.ShapeDtypeStruct((heads, length, width), BF16),
            jax.ShapeDtypeStruct((heads, 2, length, width), BF16),
            jax.ShapeDtypeStruct((length, heads * experts * width), BF16),
        ],
        compiler_params=pltpu.CompilerParams(vmem_limit_bytes=48 * 2**20),
        cost_estimate=pl.CostEstimate(
            flops=scores * width * 8, bytes_accessed=12 * 2**20, transcendentals=scores
        ),
    )(routes, gates, segments[:, None], segments[None, :], cosine, sine, keys, values, *raws)


def attn_backward(routes, gates, segments, cosine, sine, q, k, v, o, up):
    heads, _, length, width = q.shape
    experts = up.shape[1] // (heads * width)
    scores = heads * length * length * 2
    return pl.pallas_call(
        functools.partial(
            attn_backward_kernel,
            experts=experts,
            heads=heads,
            block=min(256, length),
            scale=width**-0.5,
        ),
        out_shape=jax.ShapeDtypeStruct((length, (heads * (experts + 2) + 1) * width), BF16),
        scratch_shapes=[
            pltpu.VMEM((heads, 2, length, width), BF16),
            pltpu.VMEM((heads, 2, length, width), F32),
            pltpu.VMEM((heads, length, width), F32),
            pltpu.VMEM((heads, length, width), F32),
        ],
        compiler_params=pltpu.CompilerParams(vmem_limit_bytes=48 * 2**20),
        cost_estimate=pl.CostEstimate(
            flops=scores * width * 20, bytes_accessed=12 * 2**20, transcendentals=scores
        ),
    )(routes, gates, segments[:, None], segments[None, :], cosine, sine, q, k, v, o, up)


def mlp_kernel(
    place_ref, b_ref, cot_ref, other_ref, router_ref, gate_up_ref, down_ref,
    out_ref, grad_ref, hidden_ref, dhidden_ref,
):
    hidden_units = down_ref.shape[0]
    rows = b_ref[...]
    logits = contract(rows, router_ref[...], 1, 0)
    lanes = lax.broadcasted_iota(jnp.int32, logits.shape, 1)
    own = jnp.sum(jnp.where(lanes == place_ref[0], logits, 0.0), axis=1, keepdims=True)
    other = jnp.sum(jnp.where(lanes == other_ref[...], logits, 0.0), axis=1, keepdims=True)
    gates = jax.nn.sigmoid(own - other)
    both = contract(rows, gate_up_ref[...], 1, 1)
    gate_val = both[:, :hidden_units]
    up_val = both[:, hidden_units:]
    sigmoid = jax.nn.sigmoid(gate_val)
    silu = gate_val * sigmoid
    hidden = silu * up_val
    hidden_low = hidden.astype(BF16)
    hidden_ref[...] = (hidden * gates).astype(BF16)
    grad_plain = contract(cot_ref[...], down_ref[...], 1, 1)
    dgate = jnp.sum(grad_plain * hidden_low.astype(F32), axis=1, keepdims=True)
    width = out_ref.shape[1]
    grad_ref[:, width:] = jnp.broadcast_to(dgate, (dgate.shape[0], grad_ref.shape[1] - width)).astype(BF16)
    grad_hidden = grad_plain * gates
    dhidden_ref[:, :hidden_units] = (
        grad_hidden * up_val * sigmoid * (1.0 + gate_val * (1.0 - sigmoid))
    ).astype(BF16)
    dhidden_ref[:, hidden_units:] = (grad_hidden * silu).astype(BF16)
    out_ref[...] = contract(hidden_low, down_ref[...], 1, 0).astype(BF16)
    grad_ref[:, :width] = contract(dhidden_ref[...], gate_up_ref[...], 1, 0).astype(BF16)


def mlp_experts(place, b_rows, cot_rows, other_rows, router, gate_up, down, blocks):
    total, width = b_rows.shape
    hidden_units = down.shape[0]
    block = total // blocks
    by_row = lambda cols: pl.BlockSpec((block, cols), lambda i, place: (i, 0))
    fixed = lambda shape: pl.BlockSpec(shape, lambda i, place: (0, 0), pipeline_mode=pl.Buffered(1))
    return pl.pallas_call(
        mlp_kernel,
        grid_spec=pltpu.PrefetchScalarGridSpec(
            num_scalar_prefetch=1,
            grid=(blocks,),
            in_specs=[
                by_row(width),
                by_row(width),
                by_row(1),
                fixed(router.shape),
                fixed(gate_up.shape),
                fixed(down.shape),
            ],
            out_specs=[
                by_row(width),
                by_row(width + 128),
                by_row(hidden_units),
                by_row(2 * hidden_units),
            ],
        ),
        out_shape=[
            jax.ShapeDtypeStruct((total, width), BF16),
            jax.ShapeDtypeStruct((total, width + 128), BF16),
            jax.ShapeDtypeStruct((total, hidden_units), BF16),
            jax.ShapeDtypeStruct((total, 2 * hidden_units), BF16),
        ],
        compiler_params=pltpu.CompilerParams(vmem_limit_bytes=56 * 2**20),
        cost_estimate=pl.CostEstimate(
            flops=total * width * hidden_units * 12,
            bytes_accessed=4 * total * width * 2 + 6 * total * hidden_units + 6 * width * hidden_units,
            transcendentals=total * hidden_units,
        ),
    )(place, b_rows, cot_rows, other_rows, router, gate_up, down)


def rope_tables(positions, half_dim):
    frequency = THETA_BASE ** (-jnp.arange(half_dim, dtype=F32) / half_dim)
    angles = positions.astype(F32)[:, None] * frequency[None, :]
    return (jnp.cos(angles), jnp.sin(angles))


def norm_forward(values, gain_row):
    inverse = lax.rsqrt(jnp.mean(values * values, axis=-1, keepdims=True) + EPSILON)
    return (values * inverse * gain_row, inverse)


def norm_backward(values, inverse, gain_row, grad_normed):
    scaled = gain_row * grad_normed
    gain_term = jnp.sum(grad_normed * values * inverse, axis=0)
    grad_values = inverse * scaled - values * inverse**3 * jnp.mean(
        scaled * values, axis=-1, keepdims=True
    )
    return (grad_values, gain_term)


def route_onehot(routes, experts):
    return (routes[..., None] == jnp.arange(experts, dtype=jnp.int32)).astype(F32)


def gate_forward(logits, onehot):
    chosen = jnp.sum(logits[:, None, :] * onehot, axis=-1)
    return jax.nn.softmax(chosen, axis=-1)


def gate_backward(gate_probs, grad_gates, onehot):
    centered = gate_probs * (grad_gates - jnp.sum(gate_probs * grad_gates, axis=-1, keepdims=True))
    return jnp.sum(centered[..., None] * onehot, axis=1)


def slot_columns(routes, experts, capacity):
    flat_routes = routes.reshape(-1)
    onehot = (flat_routes[:, None] == jnp.arange(experts, dtype=jnp.int32)[None, :]).astype(
        jnp.int32
    )
    slot_rank = jnp.sum((jnp.cumsum(onehot, axis=0) - 1) * onehot, axis=1)
    return (flat_routes * capacity + slot_rank).reshape(routes.shape)


def dot_f32(left, right):
    return jnp.dot(left, right, preferred_element_type=F32)


def after(value, *others):
    return lax.optimization_barrier((value,) + others)[0]


def shift_planes(value, amount):
    planes = lax.axis_size("expert")
    return lax.ppermute(value, "expert", [(i, (i + amount) % planes) for i in range(planes)])


def exchange_planes(blocks, direction):
    arrived = [blocks[0]]
    for c in range(1, blocks.shape[0]):
        arrived.append(shift_planes(blocks[c], direction * c))
    return jnp.stack(arrived, axis=0)


def gather_planes(value, me, holds):
    planes = lax.axis_size("expert")
    right, left = value, value
    rights, lefts = [], []
    for d in range(1, planes):
        if d - 1 in holds:
            right, left = after(right, *holds[d - 1]), after(left, *holds[d - 1])
        right = lax.ppermute(right, "expert", [(i, i + 1) for i in range(d - 1, planes - 1)])
        left = lax.ppermute(left, "expert", [(i + 1, i) for i in range(0, planes - d)])
        rights.append(right)
        lefts.append(left)
    gathered = [value]
    for c in range(1, planes):
        gathered.append(jnp.where(me + c < planes, lefts[c - 1], rights[planes - c - 1]))
    return gathered


def reduce_planes(parts, holds):
    planes = len(parts)
    right, left = None, None
    for t in range(1, planes):
        send_right, send_left = parts[planes - t], parts[t]
        if right is not None:
            send_right = (send_right.astype(F32) + right.astype(F32)).astype(BF16)
            send_left = (send_left.astype(F32) + left.astype(F32)).astype(BF16)
        if t in holds:
            send_right, send_left = after(send_right, *holds[t]), after(send_left, *holds[t])
        right = lax.ppermute(send_right, "expert", [(i, i + 1) for i in range(0, t)])
        left = lax.ppermute(
            send_left, "expert", [(i, i - 1) for i in range(planes - t, planes)]
        )
    return parts[0].astype(F32) + right.astype(F32) + left.astype(F32)


def swap_dp(value, mask):
    size = lax.axis_size("dp")
    return lax.ppermute(value, "dp", [(i, i ^ mask) for i in range(size)])


def all_sum(value, axis):
    size = lax.axis_size(axis)
    mask = 1
    while mask < size:
        value = value + lax.ppermute(value, axis, [(i, i ^ mask) for i in range(size)])
        mask *= 2
    return value


def reduce_rows(left, matmul, me):
    size = lax.axis_size("dp")
    blocks = left.reshape(size // 2, 2, left.shape[0] // size, left.shape[1])
    core, chip = me % 2, me // 2

    def half(index):
        rows = lax.dynamic_index_in_dim(blocks, index, axis=1, keepdims=False)
        return matmul(rows.reshape(-1, left.shape[1])).reshape(size // 2, blocks.shape[2], -1)

    arrived = swap_dp(half(1 - core).astype(BF16), 1)
    mine = half(core) + arrived.astype(F32)
    low = mine.astype(BF16)
    total = lax.dynamic_index_in_dim(low, chip, axis=0, keepdims=False).astype(F32)
    for other in range(1, size // 2):
        send = lax.dynamic_index_in_dim(low, chip ^ other, axis=0, keepdims=False)
        total = total + swap_dp(send, 2 * other).astype(F32)
    return total


def from_plane_order(relative, plane):
    planes = relative.shape[0]
    return lax.dynamic_slice_in_dim(
        jnp.concatenate([relative, relative], axis=0), (planes - plane) % planes, planes, axis=0
    )


def per_device(
    tokens,
    segment_ids,
    attn_routes,
    mlp_routes,
    cotangent,
    attn_gain,
    kv_weights,
    attn_router,
    query_maps,
    output_maps,
    mlp_gain,
    mlp_router,
    gate_up,
    down_maps,
):
    micro_count, seq_count, local_len, width = tokens.shape
    units = micro_count * seq_count
    length = segment_ids.shape[2]
    experts = attn_router.shape[1]
    dp = lax.axis_size("dp")
    planes = lax.axis_size("expert")
    capacity = 2 * local_len // experts
    slots = experts * capacity
    head_cols = width // dp
    heads = head_cols // HEAD_WIDTH
    plane = lax.axis_index("expert")
    my_dp = lax.axis_index("dp")

    tokens = tokens.reshape(units, local_len, width)
    cotangent = cotangent.reshape(units, local_len, width)
    segments = segment_ids.reshape(units, length)
    attn_routes = attn_routes.reshape(units, local_len, 2)
    mlp_routes = mlp_routes.reshape(units, local_len, 2)

    slot_ids = jnp.arange(slots, dtype=jnp.int32)
    hits_list, tables, other_list = [], [], []
    for u in range(units):
        columns = slot_columns((mlp_routes[u] - plane) % experts, experts, capacity)
        hits = (columns[None] == slot_ids[:, None, None]).astype(F32)
        hits_list.append(hits)
        tables.append(jnp.sum(hits, axis=2).astype(BF16))
        other_list.append(jnp.sum(hits * mlp_routes[u][None, :, ::-1].astype(F32), axis=(1, 2)))

    def send_slots(slot_rows):
        moved = exchange_planes(slot_rows.reshape(planes, capacity, width), 1)
        return moved.reshape(slots, width)

    def gather_rows(moved):
        return lax.all_gather(moved, "dp", axis=0, tiled=True)

    def to_home(rows):
        return exchange_planes(rows.reshape(planes, capacity, -1), -1).reshape(slots, -1)

    kv_rows = kv_weights.shape[0]
    query_rows = query_maps.shape[1]
    packed = jnp.concatenate(
        [query_maps[0], kv_weights.transpose(1, 0, 2).reshape(2 * kv_rows, width)], axis=0
    )
    packed = packed.reshape(-1, dp, head_cols).transpose(1, 0, 2)
    packed = lax.all_to_all(packed, "dp", split_axis=0, concat_axis=0, tiled=True)
    cot_moved = [send_slots(dot_f32(tables[u], cotangent[u]).astype(BF16)) for u in range(units)]

    params = jnp.concatenate(
        [attn_gain[:, None], mlp_gain[:, None], attn_router, mlp_router], axis=1
    ).reshape(-1)
    param_count = params.shape[0]
    routes_count = 2 * local_len
    x_alls, infos = [], []
    for u in range(units):
        info = jnp.concatenate([attn_routes[u].astype(F32).reshape(-1), other_list[u]]).astype(BF16)
        info = jnp.concatenate([info, params])
        info = jnp.pad(info, (0, 16 * width - info.shape[0])).reshape(16, width)
        extended = jnp.concatenate([tokens[u], info], axis=0)
        gathered = lax.all_gather(extended, "dp", axis=0)
        x_alls.append(gathered[:, :local_len].reshape(length, width))
        infos.append(gathered[:, local_len])
    cot_rows_list = [gather_rows(part) for part in cot_moved]
    others = jnp.stack([i[:, routes_count : routes_count + slots] for i in infos], axis=0)
    others = others.reshape(units * dp, experts, capacity).transpose(1, 0, 2)
    others = exchange_planes(others, 1)
    other_rows = (
        others.reshape(planes, units, dp, capacity)
        .transpose(1, 2, 0, 3)
        .reshape(units, dp * slots)
        .astype(jnp.int32)
    )
    params = infos[0][:, routes_count + slots : routes_count + slots + param_count]
    params = [params] + [shift_planes(params, -c) for c in range(1, planes)]
    params = from_plane_order(jnp.stack(params, axis=0), plane)
    params = params.transpose(1, 0, 2).reshape(width, 2 + 2 * experts)
    gain_one = params[:, 0].astype(F32)
    gain_two = params[:, 1].astype(F32)
    router_one_low = params[:, 2 : 2 + experts]
    router_two_low = params[:, 2 + experts :]
    router_one = router_one_low.astype(F32)
    router_two = router_two_low.astype(F32)
    router_wide = jnp.pad(router_two_low, ((0, 0), (0, 128 - experts)))

    hidden_units = down_maps.shape[1]
    padding = ((0, -hidden_units % 128), (0, 0))
    gate_up_local = jnp.concatenate(
        [jnp.pad(gate_up[0, :, 0], padding), jnp.pad(gate_up[0, :, 1], padding)], axis=0
    )
    down_local = jnp.pad(down_maps[0], padding)
    hidden_padded = down_local.shape[0]
    place = plane.astype(jnp.int32)[None]

    cosine, sine_table = rope_tables(jnp.arange(length, dtype=jnp.int32), HEAD_WIDTH // 2)
    cosine = jnp.concatenate([cosine, cosine], axis=1)
    sine_table = jnp.concatenate([-sine_table, sine_table], axis=1)

    mixed_parts = []
    input_parts = []
    gain_one_sum = jnp.zeros((width,), F32)
    gain_two_sum = jnp.zeros((width,), F32)
    each = range(units)

    inputs, a_home, inverse_one, a_all, routes_here, gates_all, kept, gated, states = (
        [], [], [], [], [], [], [], [], []
    )
    for u in each:
        inputs.append(tokens[u].astype(F32))
        normed, inverse = norm_forward(inputs[u], gain_one)
        a_home.append(normed.astype(BF16))
        inverse_one.append(inverse)
        a_all.append(norm_forward(x_alls[u].astype(F32), gain_one)[0].astype(BF16))

    packed = gather_planes(packed, plane, {1: tuple(cot_moved), 2: tuple(a_all)})
    query_cols = [p[:, :query_rows].reshape(width, head_cols) for p in packed]
    kv_cols = from_plane_order(jnp.stack([p[:, query_rows:] for p in packed], axis=0), plane)
    kv_cols = kv_cols.transpose(1, 0, 2, 3)
    key_cols = kv_cols[:, :, :kv_rows].reshape(width, head_cols)
    value_cols = kv_cols[:, :, kv_rows:].reshape(width, head_cols)
    for u in each:
        routes_all = infos[u][:, :routes_count].reshape(length, 2).astype(jnp.int32)
        routes_here.append((routes_all - plane) % experts)
        gates_all.append(
            gate_forward(dot_f32(a_all[u], router_one_low), route_onehot(routes_all, experts))
        )
        a_now = after(a_all[u], *gated)
        raws = [dot_f32(a_now, cols).astype(BF16) for cols in query_cols]
        keys = dot_f32(a_now, key_cols)
        values = dot_f32(a_now, value_cols).astype(BF16)
        *saved, context_gated = attn_forward(
            routes_here[u], gates_all[u], segments[u], cosine, sine_table, raws, keys, values
        )
        kept.append(saved)
        gated.append(context_gated)
    output_list = after(output_maps[0], packed[1], packed[-1])
    output_list = gather_planes(output_list, plane, {1: (gated[0], cot_rows_list[0]), 2: (gated[-1], cot_rows_list[-1])})
    output_rows = jnp.concatenate(output_list, axis=0)
    for u in each:
        states.append(
            inputs[u] + reduce_rows(gated[u], lambda rows: dot_f32(rows, output_rows), my_dp)
        )

    b_home, inverse_two, onehot_mlp, gates_mlp, moved = [], [], [], [], []
    for u in each:
        normed, inverse = norm_forward(states[u], gain_two)
        b_home.append(normed.astype(BF16))
        inverse_two.append(inverse)
        onehot_mlp.append(route_onehot(mlp_routes[u], experts))
        gates_mlp.append(gate_forward(dot_f32(b_home[u], router_two_low), onehot_mlp[u]))
        moved.append(send_slots(dot_f32(tables[u], b_home[u]).astype(BF16)))
    b_rows_list, hid_list, dhid_list, out_parts, grad_b_rows = [], [], [], [], []
    for u in each:
        b_rows_list.append(gather_rows(moved[u]))
        b_rows = b_rows_list[u]
        b_rows = after(b_rows, *moved[1:], *out_parts)
        out_part, grad_part, hidden, dhidden = mlp_experts(
            place,
            b_rows,
            cot_rows_list[u],
            other_rows[u][:, None],
            router_wide,
            gate_up_local,
            down_local,
            dp,
        )
        hid_list.append(hidden)
        dhid_list.append(dhidden)
        out_parts.append(out_part)
        grad_b_rows.append(lax.psum_scatter(grad_part, "dp", scatter_dimension=0, tiled=True))

    dlm_list, grad_states, dh_list = [], [], []
    down_grad, both_grad, last = 0.0, 0.0, out_parts[-1]
    for u in each:
        down_grad = down_grad + jnp.einsum(
            "rf,rd->fd", after(hid_list[u], last), cot_rows_list[u], preferred_element_type=F32
        )
        both_grad = both_grad + jnp.einsum(
            "rf,rd->fd", after(dhid_list[u], down_grad), b_rows_list[u], preferred_element_type=F32
        )
        grad_b_slots = after(to_home(after(grad_b_rows[u], *grad_states)), both_grad)
        hits = hits_list[u]
        cot = cotangent[u]
        dgm_slots = grad_b_slots[:, width].astype(F32)
        grad_b_slots = grad_b_slots[:, :width]
        dlm = gate_backward(
            gates_mlp[u], jnp.sum(hits * dgm_slots[:, None, None], axis=0), onehot_mlp[u]
        )
        dlm_list.append(dlm)
        grad_b = jnp.einsum(
            "st,sd->td", tables[u], grad_b_slots, preferred_element_type=F32
        ) + jnp.einsum("re,de->rd", dlm, router_two, precision=PRECISION_TOP)
        grad_state, gain_two_term = norm_backward(states[u], inverse_two[u], gain_two, grad_b)
        gain_two_sum = gain_two_sum + gain_two_term
        grad_states.append(cot.astype(F32) + grad_state)
        last = grad_states[u]
        dh_list.append(lax.all_gather(grad_states[u].astype(BF16), "dp", axis=0, tiled=True))

    qkv_cols = jnp.concatenate(
        [after(cols, *moved) for cols in query_cols + [key_cols, value_cols]], axis=1
    )
    qkv_cols = jnp.concatenate(
        [
            jnp.pad(qkv_cols, ((0, 0), (0, 128))),
            jnp.pad(jnp.eye(128, dtype=BF16), ((0, 0), (qkv_cols.shape[1], 0))),
        ],
        axis=0,
    )
    g_list, dla_list, output_part = [], [], 0.0
    for u in each:
        dh_now = after(dh_list[u], *(g_list[-1:] or grad_states[-1:]))
        output_part = output_part + jnp.einsum(
            "tc,td->cd", gated[u], dh_now, preferred_element_type=F32
        )
        grad_context = jnp.einsum("td,cd->tc", dh_now, output_rows, preferred_element_type=F32)
        if u == units - 1:
            output_part = output_part.astype(BF16)
            grad_context = after(grad_context, output_part)
        grad_qkv = attn_backward(
            routes_here[u],
            gates_all[u],
            segments[u],
            cosine,
            sine_table,
            *kept[u],
            grad_context,
        )
        g_list.append(grad_qkv)
        grad_a = reduce_rows(
            grad_qkv,
            lambda rows: jnp.einsum("tc,dc->td", rows, qkv_cols, preferred_element_type=F32),
            my_dp,
        )
        dga = grad_a[:, width : width + 2]
        grad_a = grad_a[:, :width]
        gates_home = lax.dynamic_slice_in_dim(gates_all[u], my_dp * local_len, local_len, axis=0)
        dla = gate_backward(gates_home, dga, route_onehot(attn_routes[u], experts))
        dla_list.append(dla)
        grad_a = grad_a + jnp.einsum("re,de->rd", dla, router_one, precision=PRECISION_TOP)
        grad_inputs, gain_one_term = norm_backward(inputs[u], inverse_one[u], gain_one, grad_a)
        gain_one_sum = gain_one_sum + gain_one_term
        input_parts.append(grad_states[u] + grad_inputs)

    both_grad = after(both_grad, g_list[-1])
    gate_up_grad = jnp.stack(
        [both_grad[:hidden_units], both_grad[hidden_padded : hidden_padded + hidden_units]], axis=1
    )
    def cols_grad(c):
        total = 0.0
        for u in each:
            piece = g_list[u][:, c * head_cols : (c + 1) * head_cols]
            total = total + jnp.einsum("td,tc->dc", a_all[u], piece, preferred_element_type=F32)
        return total.astype(BF16)

    query_parts = [cols_grad(c).reshape(dp, query_rows, head_cols) for c in range(planes)]
    kv_part = jnp.concatenate(
        [cols_grad(experts + i).reshape(dp, planes, kv_rows, head_cols) for i in range(2)], axis=2
    )
    kv_parts = [
        lax.dynamic_index_in_dim(kv_part, (plane + c) % planes, axis=1, keepdims=False)
        for c in range(planes)
    ]
    for u in each:
        out_part = after(out_parts[u], output_part)
        out_rows = lax.psum_scatter(out_part, "dp", scatter_dimension=0, tiled=True)
        out_slots = to_home(out_rows)
        gated_table = jnp.sum(hits_list[u] * gates_mlp[u][None], axis=2).T
        gated_high = gated_table.astype(BF16)
        gated_low = (gated_table - gated_high.astype(F32)).astype(BF16)
        mlp_sum = dot_f32(gated_high, out_slots) + dot_f32(gated_low, out_slots)
        mixed_parts.append((states[u] + mlp_sum).astype(BF16))

    output_grad = lax.psum_scatter(
        from_plane_order(output_part.reshape(planes, head_cols, width), plane),
        "expert",
        scatter_dimension=0,
        tiled=False,
    ).astype(F32)

    def to_rows(grads):
        grads = lax.all_to_all(grads.astype(BF16), "dp", split_axis=0, concat_axis=0, tiled=True)
        return grads.transpose(1, 0, 2).reshape(-1, width).astype(F32)

    query_grad = reduce_planes(query_parts, {3: (gate_up_grad, mixed_parts[0])})
    kv_grad = reduce_planes(kv_parts, {1: (query_grad,), 3: (mixed_parts[-1],)})
    query_grad = to_rows(query_grad)
    kv_grad = to_rows(kv_grad)
    kv_grad = kv_grad.reshape(2, kv_rows, width).transpose(1, 0, 2)

    down_grad = down_grad[:hidden_units]
    router_one_grad = jnp.einsum(
        "re,rd->ed",
        jnp.concatenate(dla_list, axis=0),
        jnp.concatenate(a_home, axis=0).astype(F32),
        precision=PRECISION_TOP,
    )
    router_two_grad = jnp.einsum(
        "re,rd->ed",
        jnp.concatenate(dlm_list, axis=0),
        jnp.concatenate(b_home, axis=0).astype(F32),
        precision=PRECISION_TOP,
    )
    small_grad = jnp.concatenate(
        [gain_one_sum[None], gain_two_sum[None], router_one_grad, router_two_grad], axis=0
    )
    small_grad = all_sum(all_sum(small_grad, "dp"), "expert")
    small_grad = lax.dynamic_index_in_dim(
        small_grad.reshape(-1, dp * planes, kv_rows), my_dp * planes + plane, axis=1, keepdims=False
    )

    shape = (micro_count, seq_count, local_len, width)
    return (
        jnp.stack(mixed_parts, axis=0).reshape(shape),
        jnp.stack(input_parts, axis=0).reshape(shape),
        small_grad[0],
        kv_grad,
        small_grad[2 : 2 + experts].T,
        query_grad[None],
        output_grad[None],
        small_grad[1],
        small_grad[2 + experts :].T,
        gate_up_grad[None],
        down_grad[None],
    )


def solution(mesh):
    in_specs = (
        P(None, "expert", "dp", None),
        P(None, "expert", None),
        P(None, "expert", "dp", None),
        P(None, "expert", "dp", None),
        P(None, "expert", "dp", None),
        P(("dp", "expert")),
        P(("dp", "expert"), None, None),
        P(("dp", "expert"), None),
        P("expert", "dp", None),
        P("expert", "dp", None),
        P(("dp", "expert")),
        P(("dp", "expert"), None),
        P("expert", "dp", None, None),
        P("expert", "dp", None),
    )
    out_specs = (
        P(None, "expert", "dp", None),
        P(None, "expert", "dp", None),
        P(("dp", "expert")),
        P(("dp", "expert"), None, None),
        P(("dp", "expert"), None),
        P("expert", "dp", None),
        P("expert", "dp", None),
        P(("dp", "expert")),
        P(("dp", "expert"), None),
        P("expert", "dp", None, None),
        P("expert", "dp", None),
    )
    return jax.shard_map(
        per_device, mesh=mesh, in_specs=in_specs, out_specs=out_specs, check_vma=False
    )
```

time: 1560 us -> 1250 us (0.80)
  waiting for transfers between devices: 537 us -> 373 us
  matrix products: 362 us -> 251 us
  local copies, waits for them, and re-layouts: 231 us -> 128 us
  Pallas kernels: 72.9 us -> 164 us
    ppermute x24 -> x16, waiting for transfers between devices: 154 us -> 37.2 us  [swap_dp(): return lax.ppermute(value, 'dp', [(i, i ^ mask) for i in range(size)])]
    dot_general x24 -> x22, matrix products: 240 us -> 148 us  [the longest x2 41.6 us: per_device(): jnp.einsum('rf,rd->fd', after(dhid_list[u], down_grad), b_rows_list[u], p...]
    pallas_call x4 -> x6, Pallas kernels: 72.9 us -> 164 us  [the longest x2 101 us: mlp_experts(): pl.pallas_call(mlp_kernel, grid_spec=pltpu.PrefetchScalarGridSpec(num_sca...]
    all_gather x8, waiting for transfers between devices: 79.6 us -> 0.03 us  [the longest x2 0.02 us: per_device(): lax.all_gather(grad_states[u].astype(BF16), 'dp', axis=0, tiled=True)]
    ppermute x6, waiting for transfers between devices: 9.41 us -> 70.8 us  [reduce_planes(): lax.ppermute(send_right, 'expert', [(i, i + 1) for i in range(0, t)])]
    ppermute x6, waiting for transfers between devices: 86.2 us -> 38.4 us  [gather_planes(): lax.ppermute(left, 'expert', [(i + 1, i) for i in range(0, planes - d)])]
    dynamic_slice x6 -> x0, local copies, waits for them, and re-layouts: 34.8 us -> none  [half(): rows = lax.dynamic_index_in_dim(blocks, index, axis=1, keepdims=False)]
    reduce_scatter x2 -> x5, waiting for transfers between devices: 0.01 us -> 32.5 us  [the longest x2 32.5 us: per_device(): lax.psum_scatter(grad_part, 'dp', scatter_dimension=0, tiled=True)]
  transfers between devices with their start and end apart: 97 -> 90, of which waited for: 61 -> 37; matrix products, arithmetic and copies ran while one was open for 41% -> 37% of each run, Pallas kernels for 3% -> 13%
where the time goes in v3:
time: 1250 us; the launch traced here: 1230 us
  waiting for transfers between devices  373 us (30%)
  matrix products  251 us (20%)
  Pallas kernels  164 us (13%)
  starting transfers between devices  146 us (12%)
  local copies, waits for them, and re-layouts  128 us (10%)
  other arithmetic  127 us (10%)
  blocking collectives  26.1 us (2%)
  between operations  16.8 us (1%)
    ppermute x30, waiting for transfers between devices, shift_planes(): lax.ppermute(value, 'expert', [(i, (i + amount) % planes) for i in range(...  138 us
    pallas_call x2, Pallas kernels, mlp_experts(): pl.pallas_call(mlp_kernel, grid_spec=pltpu.PrefetchScalarGridSpec(num_sca...  101 us
    ppermute x6, waiting for transfers between devices, reduce_planes(): lax.ppermute(send_right, 'expert', [(i, i + 1) for i in range(0, t)])  70.8 us
    dot_general x28, matrix products, dot_f32(): return jnp.dot(left, right, preferred_element_type=F32)  60.5 us
    ppermute x30, starting transfers between devices, shift_planes(): lax.ppermute(value, 'expert', [(i, (i + amount) % planes) for i in range(...  44.2 us
    dot_general x2, matrix products, per_device(): jnp.einsum('rf,rd->fd', after(dhid_list[u], down_grad), b_rows_list[u], p...  41.6 us
    unnamed x295, local copies, waits for them, and re-layouts  41 us
    dot_general x12, matrix products, cols_grad(): jnp.einsum('td,tc->dc', a_all[u], piece, preferred_element_type=F32)  38.7 us
  transfers between devices with their start and end apart: 90, of which 37 were waited for; matrix products, arithmetic and copies ran while one was open for 37% of the time, Pallas kernels for 13%

profile of v3, /device:TPU:8, one launch (start us, length us, event | category | flops | bytes accessed | tf_op | source)
XLA Modules:
  0.0 1231.3 jit_solution(7565764149083776198)
XLA Ops:
  26.2 14.9 %collective-permute-done.7 = bf16[64,2048]{1,0:T(8,128)(2,1)S(1)} collective-permute-done((bf16[64,2048]{1,0:T(8,128)(2,1)S(1)}, bf16[64,2048]{1,0:T(8,128)(2,1)S(1)}, u32[]{:S(2)}, u32[]{:S(2)}) %collective-permute-start.7) | collective-permute-done | bytes 262176 | tf_op jit(solution)/shard_map/ppermute | solution.py:315
  49.2 26.1 %all_to_all.15 = bf16[8,384,256]{2,1,0:T(8,128)(2,1)S(1)} all-to-all(bf16[8,384,256]{2,1,0:T(8,128)(2,1)S(1)} %maximum_bitcast_fusion.1), channel_id=1, replica_groups=mesh['dp'=8,'expert'=4] {'dp'}, dimensions={0} | all-to-all | bytes 3145728 | tf_op jit(solution)/shard_map/all_to_all | solution.py:459
  88.2 46.6 %collective-permute-done.10 = bf16[64,2048]{1,0:T(8,128)(2,1)S(1)} collective-permute-done((bf16[64,2048]{1,0:T(8,128)(2,1)S(1)}, bf16[64,2048]{1,0:T(8,128)(2,1)S(1)}, u32[]{:S(2)}, u32[]{:S(2)}) %collective-permute-start.10) | collective-permute-done | bytes 262176 | tf_op jit(solution)/shard_map/ppermute | solution.py:315
  152.1 20.7 %collective-permute-done.11 = bf16[8,384,256]{2,1,0:T(8,128)(2,1)} collective-permute-done((bf16[8,384,256]{2,1,0:T(8,128)(2,1)}, bf16[8,384,256]{2,1,0:T(8,128)(2,1)}, u32[]{:S(2)}, u32[]{:S(2)}) %collective-permute-start.11) | collective-permute-done | bytes 1572896 | tf_op jit(solution)/shard_map/ppermute | solution.py:332
  247.5 18.5 %collective-permute-done.14 = bf16[8,384,256]{2,1,0:T(8,128)(2,1)S(1)} collective-permute-done((bf16[8,384,256]{2,1,0:T(8,128)(2,1)}, bf16[8,384,256]{2,1,0:T(8,128)(2,1)S(1)}, u32[]{:S(2)}, u32[]{:S(2)}) %collective-permute-start.14) | collective-permute-done | bytes 1572896 | tf_op jit(solution)/shard_map/ppermute | solution.py:333
  282.9 12.1 shard_map.221
  341.2 12.7 %collective-permute-done.20 = bf16[256,2048]{1,0:T(8,128)(2,1)S(1)} collective-permute-done((bf16[256,2048]{1,0:T(8,128)(2,1)}, bf16[256,2048]{1,0:T(8,128)(2,1)S(1)}, u32[]{:S(2)}, u32[]{:S(2)}) %collective-permute-start.20) | collective-permute-done | bytes 1048608 | tf_op jit(solution)/shard_map/ppermute | solution.py:333
  437.2 16.8 %collective-permute-done.27 = bf16[64,2048]{1,0:T(8,128)(2,1)S(1)} collective-permute-done((bf16[64,2048]{1,0:T(8,128)(2,1)S(1)}, bf16[64,2048]{1,0:T(8,128)(2,1)S(1)}, u32[]{:S(2)}, u32[]{:S(2)}) %collective-permute-start.27) | collective-permute-done | bytes 262176 | tf_op jit(solution)/shard_map/ppermute | solution.py:315
  463.3 16.6 %collective-permute-done.34 = bf16[64,2048]{1,0:T(8,128)(2,1)S(1)} collective-permute-done((bf16[64,2048]{1,0:T(8,128)(2,1)S(1)}, bf16[64,2048]{1,0:T(8,128)(2,1)S(1)}, u32[]{:S(2)}, u32[]{:S(2)}) %collective-permute-start.34) | collective-permute-done | bytes 262176 | tf_op jit(solution)/shard_map/ppermute | solution.py:315
  483.4 12.1 fusion.242
  519.6 51.1 %shard_map.223 = (bf16[2048,2048]{1,0:T(8,128)(2,1)}, bf16[2048,2176]{1,0:T(8,128)(2,1)}, bf16[2048,768]{1,0:T(8,128)(2,1)}, bf16[2048,1536]{1,0:T(8,128)(2,1)}) custom-call(s32[1]{0:T(128)} %bitcast.68.place_ref, bf16[2048,2048]{1,0:T(8,128)(2,1)} %all-gather.15.cloned.1.call-done.b_ref, bf16[2048,2048]{1,0:T(8,128)(2,1)} %all-gather.11.cloned.1.call-done.cot_ref, ...), custom_call_target="tpu_custom_call" | custom-call | flops 38654705664 | bytes 52428800 | tf_op jit(solution)/shard_map/pallas_call | solution.py:227
  573.0 50.3 %shard_map.224 = (bf16[2048,2048]{1,0:T(8,128)(2,1)}, bf16[2048,2176]{1,0:T(8,128)(2,1)}, bf16[2048,768]{1,0:T(8,128)(2,1)}, bf16[2048,1536]{1,0:T(8,128)(2,1)}) custom-call(s32[1]{0:T(128)} %bitcast.68.place_ref, bf16[2048,2048]{1,0:T(8,128)(2,1)} %all-gather.17.cloned.1.call-done.b_ref, bf16[2048,2048]{1,0:T(8,128)(2,1)} %all-gather.13.cloned.1.call-done.cot_ref, ...), custom_call_target="tpu_custom_call" | custom-call | flops 38654705664 | bytes 52428800 | tf_op jit(solution)/shard_map/pallas_call | solution.py:227
  653.3 19.1 %fusion.252 = f32[1536,2048]{1,0:T(8,128)} fusion(bf16[2048,1536]{1,0:T(8,128)(2,1)} %get-tuple-element.86, bf16[2048,2048]{1,0:T(8,128)(2,1)} %all-gather.15.cloned.1.call-done.b_ref), kind=kOutput, calls=%fused_computation.520 | convolution fusion | flops 12884901888 | bytes 27262976 | tf_op jit(solution)/shard_map/rf,rd->fd/dot_general | solution.py:590
  687.0 13.8 %convolution_add_fusion.1 = f32[768,2048]{1,0:T(8,128)} fusion(f32[768,2048]{1,0:T(8,128)} %fusion.251, bf16[2048,768]{1,0:T(8,128)(2,1)} %get-tuple-element.92, bf16[2048,2048]{1,0:T(8,128)(2,1)} %all-gather.13.cloned.1.call-done.cot_ref), kind=kOutput, calls=%fused_computation.43 | convolution fusion | flops 6444023808 | bytes 24117248 | tf_op jit(solution)/shard_map/rf,rd->fd/dot_general | solution.py:587
  700.7 24.4 %reduce-scatter.8.cloned.1.call-done = bf16[256,2176]{1,0:T(8,128)(2,1)} async-done(((bf16[2048,2176]{1,0:T(8,128)(2,1)}), bf16[256,2176]{1,0:T(8,128)(2,1)}) %reduce-scatter.8.cloned.1.call-update) | async-done | bytes 1114128 | tf_op jit(solution)/shard_map/reduce_scatter | solution.py:582
  731.0 22.5 %convolution_add_fusion = f32[1536,2048]{1,0:T(8,128)} fusion(f32[1536,2048]{1,0:T(8,128)} %fusion.252, bf16[2048,1536]{1,0:T(8,128)(2,1)} %get-tuple-element.93, bf16[2048,2048]{1,0:T(8,128)(2,1)} %all-gather.17.cloned.1.call-done.b_ref), kind=kOutput, calls=%fused_computation.7 | convolution fusion | flops 12888047616 | bytes 39845888 | tf_op jit(solution)/shard_map/rf,rd->fd/dot_general | solution.py:590
  783.9 19.0 %shard_map.225 = bf16[1024,1664]{1,0:T(8,128)(2,1)} custom-call(s32[1024,2]{1,0:T(8,128)S(1)} %copy-done.3, f32[1024,2]{1,0:T(8,128)S(1)} %copy-done.1, s32[1024,1]{1,0:T(8,128)S(1)} %copy.238.refs_2_.seg_col_ref, s32[1,1024]{1,0:T(1,128)S(1)} %get-tuple-element.286.refs_3_.seg_row_ref, f32[1024,128]{1,0:T(8,128)S(1)} %get-tuple-element.320.refs_4_.cos_ref, ...), custom_call_target="tpu_custom_call" | custom-call | flops 10737418240 | bytes 12582912 | tf_op jit(solution)/shard_map/pallas_call | solution.py:167
  802.9 12.0 add_convert_fusion
  864.2 19.3 %shard_map.226 = bf16[1024,1664]{1,0:T(8,128)(2,1)} custom-call(s32[1024,2]{1,0:T(8,128)S(1)} %add_select_fusion.refs_0_.routes_ref, f32[1024,2]{1,0:T(8,128)S(1)} %exponential_divide_fusion.refs_1_.gates_ref, s32[1024,1]{1,0:T(8,128)S(1)} %copy.242.refs_2_.seg_col_ref, s32[1,1024]{1,0:T(1,128)S(1)} %get-tuple-element.287.refs_3_.seg_row_ref, ...), custom_call_target="tpu_custom_call" | custom-call | flops 10737418240 | bytes 12582912 | tf_op jit(solution)/shard_map/pallas_call | solution.py:167
  919.9 20.5 %copy.266 = f32[1,704,2,2048]{3,2,1,0:T(2,128)} copy(f32[1,704,2,2048]{3,1,2,0:T(8,128)} %fusion.234) | data formatting | bytes 23068672
  977.7 41.2 %collective-permute-done.64 = bf16[8,256,256]{2,1,0:T(8,128)(2,1)S(1)} collective-permute-done((bf16[8,256,256]{2,1,0:T(8,128)(2,1)S(1)}, bf16[8,256,256]{2,1,0:T(8,128)(2,1)S(1)}, u32[]{:S(2)}, u32[]{:S(2)}) %collective-permute-start.64) | collective-permute-done | bytes 1048608 | tf_op jit(solution)/shard_map/ppermute | solution.py:352
  1022.2 16.2 %collective-permute-done.67 = bf16[8,256,256]{2,1,0:T(8,128)(2,1)S(1)} collective-permute-done((bf16[8,256,256]{2,1,0:T(8,128)(2,1)S(1)}, bf16[8,256,256]{2,1,0:T(8,128)(2,1)S(1)}, u32[]{:S(2)}, u32[]{:S(2)}) %collective-permute-start.67) | collective-permute-done | bytes 1048608 | tf_op jit(solution)/shard_map/ppermute | solution.py:353
  1059.2 16.0 %collective-permute-done.46 = bf16[64,2048]{1,0:T(8,128)(2,1)} collective-permute-done((bf16[64,2048]{1,0:T(8,128)(2,1)}, bf16[64,2048]{1,0:T(8,128)(2,1)}, u32[]{:S(2)}, u32[]{:S(2)}) %collective-permute-start.46) | collective-permute-done | bytes 262176 | tf_op jit(solution)/shard_map/ppermute | solution.py:315
  1096.9 14.6 %collective-permute-done.65 = bf16[8,256,256]{2,1,0:T(8,128)(2,1)} collective-permute-done((bf16[8,256,256]{2,1,0:T(8,128)(2,1)}, bf16[8,256,256]{2,1,0:T(8,128)(2,1)}, u32[]{:S(2)}, u32[]{:S(2)}) %collective-permute-start.65) | collective-permute-done | bytes 1048608 | tf_op jit(solution)/shard_map/ppermute | solution.py:352
  (762 shorter events, 677.4 us)
Async XLA Ops:
  7.2 174.8 %all-gather.23.cloned.1.call-start = ((), (), s32[]{:S(2)}) async-start(), calls=%async_computation.19 | async-start | bytes 5308416 | tf_op jit(solution)/shard_map/all_gather | solution.py:473
  19.0 169.9 %all-gather.25.cloned.1.call-start = ((), (), s32[]{:S(2)}) async-start(), calls=%async_computation.20 | async-start | bytes 5308416 | tf_op jit(solution)/shard_map/all_gather | solution.py:473
  20.0 283.2 %all-gather.11.cloned.1.call-start = ((), (), s32[]{:S(2)}) async-start(), calls=%async_computation.8 | async-start | bytes 9437184 | tf_op jit(solution)/shard_map/all_gather | solution.py:448
  47.0 282.8 %all-gather.13.cloned.1.call-start = ((), (), s32[]{:S(2)}) async-start(), calls=%async_computation.9 | async-start | bytes 9437184 | tf_op jit(solution)/shard_map/all_gather | solution.py:448
  75.3 60.6 %collective-permute-start.4 = (bf16[8,384,256]{2,1,0:T(8,128)(2,1)S(1)}, bf16[8,384,256]{2,1,0:T(8,128)(2,1)S(1)}, u32[]{:S(2)}, u32[]{:S(2)}) collective-permute-start(bf16[8,384,256]{2,1,0:T(8,128)(2,1)S(1)} %all_to_all.15), channel_id=1, source_target_pairs={{0,1},{1,2},{2,3},{4,5},{5,6},{6,7},{8,9},{9,10},{10,11},{12,13},{... | collective-permute-start | bytes 4718600 | tf_op jit(solution)/shard_map/ppermute | solution.py:332
  78.6 63.8 %collective-permute-start.3 = (bf16[8,384,256]{2,1,0:T(8,128)(2,1)S(1)}, bf16[8,384,256]{2,1,0:T(8,128)(2,1)}, u32[]{:S(2)}, u32[]{:S(2)}) collective-permute-start(bf16[8,384,256]{2,1,0:T(8,128)(2,1)S(1)} %all_to_all.15), channel_id=1, source_target_pairs={{1,0},{2,1},{3,2},{5,4},{6,5},{7,6},{9,8},{10,9},{11,10},{13,12},{... | collective-permute-start | bytes 4718600 | tf_op jit(solution)/shard_map/ppermute | solution.py:333
  81.7 53.0 %collective-permute-start.10 = (bf16[64,2048]{1,0:T(8,128)(2,1)S(1)}, bf16[64,2048]{1,0:T(8,128)(2,1)S(1)}, u32[]{:S(2)}, u32[]{:S(2)}) collective-permute-start(bf16[64,2048]{1,0:T(8,128)(2,1)S(1)} %get-tuple-element.261), channel_id=1, source_target_pairs={{0,3},{1,0},{2,1},{3,2},{4,7},{5,4},{6,5},{7,6},{8,11},{9,8},{10,9... | collective-permute-start | bytes 786440 | tf_op jit(solution)/shard_map/ppermute | solution.py:315
  147.9 371.7 %all-gather.15.cloned.1.call-start = ((), (), s32[]{:S(2)}) async-start(), calls=%async_computation.10 | async-start | bytes 9437184 | tf_op jit(solution)/shard_map/all_gather | solution.py:448
  457.4 115.6 %all-gather.17.cloned.1.call-start = ((), (), s32[]{:S(2)}) async-start(), calls=%async_computation.12 | async-start | bytes 9437184 | tf_op jit(solution)/shard_map/all_gather | solution.py:448
  483.2 163.9 %reduce-scatter.6.cloned.1.call-start = ((), (), s32[]{:S(2)}) async-start(), calls=%async_computation.11 | async-start | bytes 10027008 | tf_op jit(solution)/shard_map/reduce_scatter | solution.py:582
  570.7 154.4 %reduce-scatter.8.cloned.1.call-start = ((), (), s32[]{:S(2)}) async-start(), calls=%async_computation.14 | async-start | bytes 10027008 | tf_op jit(solution)/shard_map/reduce_scatter | solution.py:582
  623.3 141.5 %all-gather.19.cloned.1.call-start = ((), (), s32[]{:S(2)}) async-start(), calls=%async_computation.13 | async-start | bytes 4718592 | tf_op jit(solution)/shard_map/all_gather | solution.py:609
  686.9 116.0 %all-gather.21.cloned.1.call-start = ((), (), s32[]{:S(2)}) async-start(), calls=%async_computation.15 | async-start | bytes 4718592 | tf_op jit(solution)/shard_map/all_gather | solution.py:609
  764.5 289.0 %reduce-scatter.10.cloned.1.call-start = ((), (), s32[]{:S(2)}) async-start(), calls=%async_computation.16 | async-start | bytes 9437184 | tf_op jit(solution)/shard_map/reduce_scatter | solution.py:677
  814.9 319.9 %reduce-scatter.12.cloned.1.call-start = ((), (), s32[]{:S(2)}) async-start(), calls=%async_computation.17 | async-start | bytes 9437184 | tf_op jit(solution)/shard_map/reduce_scatter | solution.py:677
  816.9 386.3 %reduce-scatter.14.cloned.1.call-start = ((), (), s32[]{:S(2)}) async-start(), calls=%async_computation.18 | async-start | bytes 5242880 | tf_op jit(solution)/shard_map/reduce_scatter | solution.py:685
  838.4 128.6 %collective-permute-start.50 = (bf16[4,128,2176]{2,1,0:T(8,128)(2,1)}, bf16[4,128,2176]{2,1,0:T(8,128)(2,1)}, u32[]{:S(2)}, u32[]{:S(2)}) collective-permute-start(bf16[4,128,2176]{2,1,0:T(8,128)(2,1)} %convolution_convert_fusion.1), channel_id=1, source_target_pairs={{0,4},{4,0},{8,12},{12,8},{16,20},{20,16},{24,28},{28,24},{1,5},{5... | collective-permute-start | bytes 6684680 | tf_op jit(solution)/shard_map/ppermute | solution.py:361
  887.8 72.4 %collective-permute-start.63 = (bf16[8,256,256]{2,1,0:T(8,128)(2,1)}, bf16[8,256,256]{2,1,0:T(8,128)(2,1)}, u32[]{:S(2)}, u32[]{:S(2)}) collective-permute-start(bf16[8,256,256]{2,1,0:T(8,128)(2,1)} %bitcast.160), channel_id=1, source_target_pairs={{0,1},{4,5},{8,9},{12,13},{16,17},{20,21},{24,25},{28,29}} | collective-permute-start | bytes 3145736 | tf_op jit(solution)/shard_map/ppermute | solution.py:352
  891.6 68.7 %collective-permute-start.66 = (bf16[8,256,256]{2,1,0:T(8,128)(2,1)}, bf16[8,256,256]{2,1,0:T(8,128)(2,1)}, u32[]{:S(2)}, u32[]{:S(2)}) collective-permute-start(bf16[8,256,256]{2,1,0:T(8,128)(2,1)} %bitcast.158), channel_id=1, source_target_pairs={{3,2},{7,6},{11,10},{15,14},{19,18},{23,22},{27,26},{31,30}} | collective-permute-start | bytes 3145736 | tf_op jit(solution)/shard_map/ppermute | solution.py:353
  900.3 140.6 %collective-permute-start.54 = (bf16[4,128,2176]{2,1,0:T(8,128)(2,1)}, bf16[4,128,2176]{2,1,0:T(8,128)(2,1)}, u32[]{:S(2)}, u32[]{:S(2)}) collective-permute-start(bf16[4,128,2176]{2,1,0:T(8,128)(2,1)} %convolution_convert_fusion), channel_id=1, source_target_pairs={{0,4},{4,0},{8,12},{12,8},{16,20},{20,16},{24,28},{28,24},{1,5},{5... | collective-permute-start | bytes 6684680 | tf_op jit(solution)/shard_map/ppermute | solution.py:361
  962.4 56.5 %collective-permute-start.64 = (bf16[8,256,256]{2,1,0:T(8,128)(2,1)S(1)}, bf16[8,256,256]{2,1,0:T(8,128)(2,1)S(1)}, u32[]{:S(2)}, u32[]{:S(2)}) collective-permute-start(bf16[8,256,256]{2,1,0:T(8,128)(2,1)S(1)} %get-tuple-element.238), channel_id=1, source_target_pairs={{0,1},{1,2},{4,5},{5,6},{8,9},{9,10},{12,13},{13,14},{16,17},{17,1... | collective-permute-start | bytes 3145736 | tf_op jit(solution)/shard_map/ppermute | solution.py:352
  965.6 72.7 %collective-permute-start.67 = (bf16[8,256,256]{2,1,0:T(8,128)(2,1)S(1)}, bf16[8,256,256]{2,1,0:T(8,128)(2,1)S(1)}, u32[]{:S(2)}, u32[]{:S(2)}) collective-permute-start(bf16[8,256,256]{2,1,0:T(8,128)(2,1)S(1)} %get-tuple-element.239), channel_id=1, source_target_pairs={{2,1},{3,2},{6,5},{7,6},{10,9},{11,10},{14,13},{15,14},{18,17},{19... | collective-permute-start | bytes 3145736 | tf_op jit(solution)/shard_map/ppermute | solution.py:353
  975.3 75.8 %collective-permute-start.51 = (bf16[128,2176]{1,0:T(8,128)(2,1)S(1)}, bf16[128,2176]{1,0:T(8,128)(2,1)S(1)}, u32[]{:S(2)}, u32[]{:S(2)}) collective-permute-start(bf16[128,2176]{1,0:T(8,128)(2,1)S(1)} %get-tuple-element.212), channel_id=1, source_target_pairs={{0,8},{4,12},{8,0},{12,4},{16,24},{20,28},{24,16},{28,20},{1,9},{5... | collective-permute-start | bytes 1671176 | tf_op jit(solution)/shard_map/ppermute | solution.py:361
  976.7 74.5 %collective-permute-start.53 = (bf16[128,2176]{1,0:T(8,128)(2,1)S(1)}, bf16[128,2176]{1,0:T(8,128)(2,1)S(1)}, u32[]{:S(2)}, u32[]{:S(2)}) collective-permute-start(bf16[128,2176]{1,0:T(8,128)(2,1)S(1)} %get-tuple-element.213), channel_id=1, source_target_pairs={{0,24},{4,28},{8,16},{12,20},{16,8},{20,12},{24,0},{28,4},{1,25},{... | collective-permute-start | bytes 1671176 | tf_op jit(solution)/shard_map/ppermute | solution.py:361
  (201 other events, 3762.7 us)
Sparse Core Ops, SparseCore 0:
  19.1 42.2 all-gather.22
  63.9 47.7 all-gather.24
  113.6 54.3 all-gather.10
  169.8 54.3 all-gather.12
  457.5 55.3 all-gather.14
  515.2 54.3 all-gather.16
  573.2 73.8 reduce-scatter.5
  651.3 73.7 reduce-scatter.7
  727.0 36.6 all-gather.18
  766.0 36.7 all-gather.20
  815.0 71.1 reduce-scatter.9
  890.0 73.8 reduce-scatter.11
  966.2 112.0 reduce-scatter.13

commit v4 on v3

--- a/solution.py
+++ b/solution.py
@@ -188,8 +188,9 @@
 
 def mlp_kernel(
     place_ref, b_ref, cot_ref, other_ref, router_ref, gate_up_ref, down_ref,
-    out_ref, grad_ref, hidden_ref, dhidden_ref,
+    *rest,
 ):
+    out_ref, grad_ref, hidden_ref, dhidden_ref = rest[-4:]
     hidden_units = down_ref.shape[0]
     rows = b_ref[...]
     logits = contract(rows, router_ref[...], 1, 0)
@@ -207,7 +208,7 @@
     hidden_ref[...] = (hidden * gates).astype(BF16)
     grad_plain = contract(cot_ref[...], down_ref[...], 1, 1)
     dgate = jnp.sum(grad_plain * hidden_low.astype(F32), axis=1, keepdims=True)
-    width = out_ref.shape[1]
+    width = b_ref.shape[1]
     grad_ref[:, width:] = jnp.broadcast_to(dgate, (dgate.shape[0], grad_ref.shape[1] - width)).astype(BF16)
     grad_hidden = grad_plain * gates
     dhidden_ref[:, :hidden_units] = (
@@ -218,7 +219,7 @@
     grad_ref[:, :width] = contract(dhidden_ref[...], gate_up_ref[...], 1, 0).astype(BF16)
 
 
-def mlp_experts(place, b_rows, cot_rows, other_rows, router, gate_up, down, blocks):
+def mlp_experts(place, b_rows, cot_rows, other_rows, router, gate_up, down, blocks, unit, units, outs):
     total, width = b_rows.shape
     hidden_units = down.shape[0]
     block = total // blocks
@@ -236,16 +237,17 @@
                 fixed(router.shape),
                 fixed(gate_up.shape),
                 fixed(down.shape),
-            ],
+            ]
+            + [pl.BlockSpec(memory_space=pl.ANY)] * len(outs),
             out_specs=[
-                by_row(width),
+                pl.BlockSpec((block, width), lambda i, place: (i, unit)),
                 by_row(width + 128),
                 by_row(hidden_units),
                 by_row(2 * hidden_units),
             ],
         ),
         out_shape=[
-            jax.ShapeDtypeStruct((total, width), BF16),
+            jax.ShapeDtypeStruct((total, units * width), BF16),
             jax.ShapeDtypeStruct((total, width + 128), BF16),
             jax.ShapeDtypeStruct((total, hidden_units), BF16),
             jax.ShapeDtypeStruct((total, 2 * hidden_units), BF16),
@@ -256,7 +258,55 @@
             bytes_accessed=4 * total * width * 2 + 6 * total * hidden_units + 6 * width * hidden_units,
             transcendentals=total * hidden_units,
         ),
-    )(place, b_rows, cot_rows, other_rows, router, gate_up, down)
+        input_output_aliases={7: 0} if outs else {},
+    )(place, b_rows, cot_rows, other_rows, router, gate_up, down, *outs)
+
+
+def weave_kernel(first_ref, second_ref, out_ref):
+    out_ref[0, :, 0, :] = first_ref[...]
+    out_ref[0, :, 1, :] = second_ref[...]
+
+
+def weave_rows(both, units):
+    total, width = both.shape
+    block = 32
+    half = total // 2 // block
+    return pl.pallas_call(
+        weave_kernel,
+        grid=(units // block,),
+        in_specs=[
+            pl.BlockSpec((block, width), lambda i: (i, 0)),
+            pl.BlockSpec((block, width), lambda i: (i + half, 0)),
+        ],
+        out_specs=pl.BlockSpec((1, block, 2, width), lambda i: (0, i, 0, 0)),
+        out_shape=jax.ShapeDtypeStruct((1, units, 2, width), F32),
+        cost_estimate=pl.CostEstimate(
+            flops=0, bytes_accessed=16 * units * width, transcendentals=0
+        ),
+    )(both, both)
+
+
+def norm_kernel(x_ref, gain_ref, out_ref):
+    values = x_ref[0].astype(F32)
+    inverse = lax.rsqrt(jnp.mean(values * values, axis=1, keepdims=True) + EPSILON)
+    out_ref[...] = (values * inverse * gain_ref[...]).astype(BF16)
+
+
+def norm_sequence(gathered, unit, gain, rows):
+    blocks, _, width = gathered.shape
+    return pl.pallas_call(
+        norm_kernel,
+        grid=(blocks,),
+        in_specs=[
+            pl.BlockSpec((1, rows, width), lambda i: (i, unit, 0)),
+            pl.BlockSpec((1, width), lambda i: (0, 0)),
+        ],
+        out_specs=pl.BlockSpec((rows, width), lambda i: (i, 0)),
+        out_shape=jax.ShapeDtypeStruct((blocks * rows, width), BF16),
+        cost_estimate=pl.CostEstimate(
+            flops=blocks * rows * width * 6, bytes_accessed=blocks * rows * width * 4, transcendentals=0
+        ),
+    )(gathered, gain[None])
 
 
 def rope_tables(positions, half_dim):
@@ -370,7 +420,7 @@
     return value
 
 
-def reduce_rows(left, matmul, me):
+def reduce_rows(left, matmul, me, hold=None):
     size = lax.axis_size("dp")
     blocks = left.reshape(size // 2, 2, left.shape[0] // size, left.shape[1])
     core, chip = me % 2, me // 2
@@ -382,11 +432,12 @@
     arrived = swap_dp(half(1 - core).astype(BF16), 1)
     mine = half(core) + arrived.astype(F32)
     low = mine.astype(BF16)
-    total = lax.dynamic_index_in_dim(low, chip, axis=0, keepdims=False).astype(F32)
+    total = lax.dynamic_index_in_dim(low, chip, axis=0, keepdims=False)
+    total = (total if hold is None else after(total, hold)).astype(F32)
     for other in range(1, size // 2):
         send = lax.dynamic_index_in_dim(low, chip ^ other, axis=0, keepdims=False)
         total = total + swap_dp(send, 2 * other).astype(F32)
-    return total
+    return total, low
 
 
 def from_plane_order(relative, plane):
@@ -455,42 +506,39 @@
     packed = jnp.concatenate(
         [query_maps[0], kv_weights.transpose(1, 0, 2).reshape(2 * kv_rows, width)], axis=0
     )
+    params = jnp.concatenate([attn_gain, mlp_gain, attn_router.reshape(-1), mlp_router.reshape(-1)])
+    sizes = [units * local_len * 2, units * slots, params.shape[0]]
+    info = jnp.concatenate(
+        [attn_routes.astype(BF16).reshape(-1)] + [o.astype(BF16) for o in other_list] + [params]
+    )
+    info = jnp.pad(info, (0, -info.shape[0] % (16 * head_cols))).reshape(1, -1, head_cols)
     packed = packed.reshape(-1, dp, head_cols).transpose(1, 0, 2)
+    weight_rows = packed.shape[1]
+    packed = jnp.concatenate([packed, jnp.broadcast_to(info, (dp,) + info.shape[1:])], axis=1)
     packed = lax.all_to_all(packed, "dp", split_axis=0, concat_axis=0, tiled=True)
+    info = packed[:, weight_rows:].reshape(dp, -1)
     cot_moved = [send_slots(dot_f32(tables[u], cotangent[u]).astype(BF16)) for u in range(units)]
-
-    params = jnp.concatenate(
-        [attn_gain[:, None], mlp_gain[:, None], attn_router, mlp_router], axis=1
-    ).reshape(-1)
-    param_count = params.shape[0]
-    routes_count = 2 * local_len
-    x_alls, infos = [], []
-    for u in range(units):
-        info = jnp.concatenate([attn_routes[u].astype(F32).reshape(-1), other_list[u]]).astype(BF16)
-        info = jnp.concatenate([info, params])
-        info = jnp.pad(info, (0, 16 * width - info.shape[0])).reshape(16, width)
-        extended = jnp.concatenate([tokens[u], info], axis=0)
-        gathered = lax.all_gather(extended, "dp", axis=0)
-        x_alls.append(gathered[:, :local_len].reshape(length, width))
-        infos.append(gathered[:, local_len])
     cot_rows_list = [gather_rows(part) for part in cot_moved]
-    others = jnp.stack([i[:, routes_count : routes_count + slots] for i in infos], axis=0)
-    others = others.reshape(units * dp, experts, capacity).transpose(1, 0, 2)
-    others = exchange_planes(others, 1)
-    other_rows = (
-        others.reshape(planes, units, dp, capacity)
-        .transpose(1, 2, 0, 3)
-        .reshape(units, dp * slots)
-        .astype(jnp.int32)
-    )
-    params = infos[0][:, routes_count + slots : routes_count + slots + param_count]
+
+    x_all = lax.all_gather(tokens.reshape(units * local_len, width), "dp", axis=0)
+
+    routes_info = info[:, : sizes[0]].reshape(dp, units, local_len, 2).transpose(1, 0, 2, 3)
+    routes_info = routes_info.reshape(units, length, 2).astype(jnp.int32)
+    others = info[:, sizes[0] : sizes[0] + sizes[1]].reshape(dp, units, experts, capacity)
+    others = exchange_planes(others.transpose(2, 1, 0, 3), 1)
+    other_rows = others.transpose(1, 2, 0, 3).reshape(units, dp * slots).astype(jnp.int32)
+    params = info[:, sizes[0] + sizes[1] : sum(sizes)]
     params = [params] + [shift_planes(params, -c) for c in range(1, planes)]
     params = from_plane_order(jnp.stack(params, axis=0), plane)
-    params = params.transpose(1, 0, 2).reshape(width, 2 + 2 * experts)
-    gain_one = params[:, 0].astype(F32)
-    gain_two = params[:, 1].astype(F32)
-    router_one_low = params[:, 2 : 2 + experts]
-    router_two_low = params[:, 2 + experts :]
+
+    def param(start, each):
+        part = params[:, :, start : start + kv_rows * each]
+        return part.reshape(planes, dp, kv_rows, each).transpose(1, 0, 2, 3).reshape(width, each)
+
+    gain_one = param(0, 1).reshape(-1).astype(F32)
+    gain_two = param(kv_rows, 1).reshape(-1).astype(F32)
+    router_one_low = param(2 * kv_rows, experts)
+    router_two_low = param((2 + experts) * kv_rows, experts)
     router_one = router_one_low.astype(F32)
     router_two = router_two_low.astype(F32)
     router_wide = jnp.pad(router_two_low, ((0, 0), (0, 128 - experts)))
@@ -522,20 +570,19 @@
         normed, inverse = norm_forward(inputs[u], gain_one)
         a_home.append(normed.astype(BF16))
         inverse_one.append(inverse)
-        a_all.append(norm_forward(x_alls[u].astype(F32), gain_one)[0].astype(BF16))
-
-    packed = gather_planes(packed, plane, {1: tuple(cot_moved), 2: tuple(a_all)})
+        a_all.append(norm_sequence(x_all, u, gain_one, local_len))
+        gates_all.append(
+            gate_forward(dot_f32(a_all[u], router_one_low), route_onehot(routes_info[u], experts))
+        )
+
+    packed = gather_planes(packed, plane, {1: tuple(cot_moved + a_all), 2: tuple(gates_all)})
     query_cols = [p[:, :query_rows].reshape(width, head_cols) for p in packed]
-    kv_cols = from_plane_order(jnp.stack([p[:, query_rows:] for p in packed], axis=0), plane)
+    kv_cols = from_plane_order(jnp.stack([p[:, query_rows:weight_rows] for p in packed], axis=0), plane)
     kv_cols = kv_cols.transpose(1, 0, 2, 3)
     key_cols = kv_cols[:, :, :kv_rows].reshape(width, head_cols)
     value_cols = kv_cols[:, :, kv_rows:].reshape(width, head_cols)
     for u in each:
-        routes_all = infos[u][:, :routes_count].reshape(length, 2).astype(jnp.int32)
-        routes_here.append((routes_all - plane) % experts)
-        gates_all.append(
-            gate_forward(dot_f32(a_all[u], router_one_low), route_onehot(routes_all, experts))
-        )
+        routes_here.append((routes_info[u] - plane) % experts)
         a_now = after(a_all[u], *gated)
         raws = [dot_f32(a_now, cols).astype(BF16) for cols in query_cols]
         keys = dot_f32(a_now, key_cols)
@@ -548,25 +595,27 @@
     output_list = after(output_maps[0], packed[1], packed[-1])
     output_list = gather_planes(output_list, plane, {1: (gated[0], cot_rows_list[0]), 2: (gated[-1], cot_rows_list[-1])})
     output_rows = jnp.concatenate(output_list, axis=0)
+    b_home, inverse_two, onehot_mlp, gates_mlp, moved, sent = [], [], [], [], [], []
     for u in each:
-        states.append(
-            inputs[u] + reduce_rows(gated[u], lambda rows: dot_f32(rows, output_rows), my_dp)
-        )
-
-    b_home, inverse_two, onehot_mlp, gates_mlp, moved = [], [], [], [], []
-    for u in each:
+        gated_now = after(gated[u], *sent)
+        attn_sum, low = reduce_rows(
+            gated_now, lambda rows: dot_f32(rows, output_rows), my_dp, moved[-1] if moved else None
+        )
+        sent.append(low)
+        states.append(inputs[u] + attn_sum)
         normed, inverse = norm_forward(states[u], gain_two)
         b_home.append(normed.astype(BF16))
         inverse_two.append(inverse)
         onehot_mlp.append(route_onehot(mlp_routes[u], experts))
         gates_mlp.append(gate_forward(dot_f32(b_home[u], router_two_low), onehot_mlp[u]))
         moved.append(send_slots(dot_f32(tables[u], b_home[u]).astype(BF16)))
-    b_rows_list, hid_list, dhid_list, out_parts, grad_b_rows = [], [], [], [], []
+
+    b_rows_list, hid_list, dhid_list, grad_b_rows, outs = [], [], [], [], []
     for u in each:
         b_rows_list.append(gather_rows(moved[u]))
         b_rows = b_rows_list[u]
-        b_rows = after(b_rows, *moved[1:], *out_parts)
-        out_part, grad_part, hidden, dhidden = mlp_experts(
+        b_rows = after(b_rows, *moved[1:], *hid_list)
+        outs, grad_part, hidden, dhidden = mlp_experts(
             place,
             b_rows,
             cot_rows_list[u],
@@ -575,22 +624,28 @@
             gate_up_local,
             down_local,
             dp,
-        )
+            u,
+            units,
+            outs,
+        )
+        outs = [outs]
         hid_list.append(hidden)
         dhid_list.append(dhidden)
-        out_parts.append(out_part)
         grad_b_rows.append(lax.psum_scatter(grad_part, "dp", scatter_dimension=0, tiled=True))
 
     dlm_list, grad_states, dh_list = [], [], []
-    down_grad, both_grad, last = 0.0, 0.0, out_parts[-1]
+    down_grad, both_grad, last = 0.0, 0.0, hid_list[-1]
     for u in each:
         down_grad = down_grad + jnp.einsum(
-            "rf,rd->fd", after(hid_list[u], last), cot_rows_list[u], preferred_element_type=F32
+            "rf,rd->fd",
+            after(hid_list[u], last),
+            cot_rows_list[u],
+            preferred_element_type=F32,
         )
         both_grad = both_grad + jnp.einsum(
             "rf,rd->fd", after(dhid_list[u], down_grad), b_rows_list[u], preferred_element_type=F32
         )
-        grad_b_slots = after(to_home(after(grad_b_rows[u], *grad_states)), both_grad)
+        grad_b_slots = after(to_home(after(grad_b_rows[u], *grad_states)), both_grad, *dh_list)
         hits = hits_list[u]
         cot = cotangent[u]
         dgm_slots = grad_b_slots[:, width].astype(F32)
@@ -618,28 +673,37 @@
         ],
         axis=0,
     )
-    g_list, dla_list, output_part = [], [], 0.0
+    g_list = []
     for u in each:
         dh_now = after(dh_list[u], *(g_list[-1:] or grad_states[-1:]))
-        output_part = output_part + jnp.einsum(
-            "tc,td->cd", gated[u], dh_now, preferred_element_type=F32
-        )
         grad_context = jnp.einsum("td,cd->tc", dh_now, output_rows, preferred_element_type=F32)
-        if u == units - 1:
-            output_part = output_part.astype(BF16)
-            grad_context = after(grad_context, output_part)
-        grad_qkv = attn_backward(
-            routes_here[u],
-            gates_all[u],
-            segments[u],
-            cosine,
-            sine_table,
-            *kept[u],
-            grad_context,
-        )
-        g_list.append(grad_qkv)
-        grad_a = reduce_rows(
-            grad_qkv,
+        g_list.append(
+            attn_backward(
+                routes_here[u],
+                gates_all[u],
+                segments[u],
+                cosine,
+                sine_table,
+                *kept[u],
+                grad_context,
+            )
+        )
+
+    dla_list = []
+
+    def cols_grad(c, hold):
+        total = 0.0
+        for u in each:
+            piece = lax.dynamic_slice_in_dim(
+                after(g_list[u], hold), c * head_cols, head_cols, axis=1
+            )
+            total = total + jnp.einsum("td,tc->dc", a_all[u], piece, preferred_element_type=F32)
+        return total.astype(BF16)
+
+    def finish_inputs(u, hold):
+        nonlocal gain_one_sum
+        grad_a, low = reduce_rows(
+            after(g_list[u], hold),
             lambda rows: jnp.einsum("tc,dc->td", rows, qkv_cols, preferred_element_type=F32),
             my_dp,
         )
@@ -652,54 +716,52 @@
         grad_inputs, gain_one_term = norm_backward(inputs[u], inverse_one[u], gain_one, grad_a)
         gain_one_sum = gain_one_sum + gain_one_term
         input_parts.append(grad_states[u] + grad_inputs)
-
-    both_grad = after(both_grad, g_list[-1])
-    gate_up_grad = jnp.stack(
-        [both_grad[:hidden_units], both_grad[hidden_padded : hidden_padded + hidden_units]], axis=1
-    )
-    def cols_grad(c):
-        total = 0.0
-        for u in each:
-            piece = g_list[u][:, c * head_cols : (c + 1) * head_cols]
-            total = total + jnp.einsum("td,tc->dc", a_all[u], piece, preferred_element_type=F32)
-        return total.astype(BF16)
-
-    query_parts = [cols_grad(c).reshape(dp, query_rows, head_cols) for c in range(planes)]
-    kv_part = jnp.concatenate(
-        [cols_grad(experts + i).reshape(dp, planes, kv_rows, head_cols) for i in range(2)], axis=2
-    )
-    kv_parts = [
-        lax.dynamic_index_in_dim(kv_part, (plane + c) % planes, axis=1, keepdims=False)
-        for c in range(planes)
-    ]
+        return low
+
+    done = g_list[-1]
+    query_parts = []
+    for e in range(planes):
+        done = cols_grad((e - plane) % planes, done)
+        query_parts.append(done.reshape(dp, query_rows, head_cols))
+    kv_part = []
+    for i in range(2):
+        done = cols_grad(experts + i, done)
+        kv_part.append(done.reshape(dp, planes, kv_rows, head_cols))
+    packed_grad = jnp.concatenate(
+        [jnp.stack(query_parts, axis=0)] + [part.transpose(1, 0, 2, 3) for part in kv_part], axis=2
+    )
+    packed_grad = lax.psum_scatter(packed_grad, "expert", scatter_dimension=0, tiled=False)
+    for u in each[:-1]:
+        done = finish_inputs(u, done)
+    done = finish_inputs(units - 1, done)
+    output_part = 0.0
     for u in each:
-        out_part = after(out_parts[u], output_part)
-        out_rows = lax.psum_scatter(out_part, "dp", scatter_dimension=0, tiled=True)
-        out_slots = to_home(out_rows)
+        output_part = output_part + jnp.einsum(
+            "tc,td->cd", after(gated[u], done), dh_list[u], preferred_element_type=F32
+        )
+    output_part = output_part.astype(BF16)
+
+    both_grad = after(both_grad, output_part)
+    gate_up_grad = weave_rows(both_grad, hidden_units)
+    down_grad = after(down_grad, output_part)[:hidden_units]
+
+    out_rows = lax.psum_scatter(after(outs[0], dh_list[-1]), "dp", scatter_dimension=0, tiled=True)
+    for u in each:
+        out_slots = to_home(out_rows[:, u * width : (u + 1) * width])
         gated_table = jnp.sum(hits_list[u] * gates_mlp[u][None], axis=2).T
         gated_high = gated_table.astype(BF16)
         gated_low = (gated_table - gated_high.astype(F32)).astype(BF16)
         mlp_sum = dot_f32(gated_high, out_slots) + dot_f32(gated_low, out_slots)
         mixed_parts.append((states[u] + mlp_sum).astype(BF16))
 
-    output_grad = lax.psum_scatter(
-        from_plane_order(output_part.reshape(planes, head_cols, width), plane),
-        "expert",
-        scatter_dimension=0,
-        tiled=False,
-    ).astype(F32)
-
-    def to_rows(grads):
-        grads = lax.all_to_all(grads.astype(BF16), "dp", split_axis=0, concat_axis=0, tiled=True)
-        return grads.transpose(1, 0, 2).reshape(-1, width).astype(F32)
-
-    query_grad = reduce_planes(query_parts, {3: (gate_up_grad, mixed_parts[0])})
-    kv_grad = reduce_planes(kv_parts, {1: (query_grad,), 3: (mixed_parts[-1],)})
-    query_grad = to_rows(query_grad)
-    kv_grad = to_rows(kv_grad)
-    kv_grad = kv_grad.reshape(2, kv_rows, width).transpose(1, 0, 2)
-
-    down_grad = down_grad[:hidden_units]
+    output_grad = reduce_planes(
+        [output_part[c * head_cols : (c + 1) * head_cols] for c in range(planes)], {}
+    )
+    packed_grad = lax.all_to_all(packed_grad, "dp", split_axis=0, concat_axis=0, tiled=True)
+    packed_grad = packed_grad.transpose(1, 0, 2).reshape(-1, width).astype(F32)
+    query_grad = packed_grad[:query_rows]
+    kv_grad = packed_grad[query_rows:].reshape(2, kv_rows, width).transpose(1, 0, 2)
+
     router_one_grad = jnp.einsum(
         "re,rd->ed",
         jnp.concatenate(dla_list, axis=0),
@@ -731,7 +793,7 @@
         output_grad[None],
         small_grad[1],
         small_grad[2 + experts :].T,
-        gate_up_grad[None],
+        gate_up_grad,
         down_grad[None],
     )
 

time: 1250 us -> 1150 us (0.920)
  other arithmetic: 127 us -> 81.5 us
  local copies, waits for them, and re-layouts: 128 us -> 86.8 us
  Pallas kernels: 164 us -> 194 us
  waiting for transfers between devices: 373 us -> 403 us
  matrix products: 251 us -> 223 us
  blocking collectives: 26.1 us -> 0 us
  starting transfers between devices: 146 us -> 133 us
    ppermute x16, waiting for transfers between devices: 37.2 us -> 89.4 us  [swap_dp(): return lax.ppermute(value, 'dp', [(i, i ^ mask) for i in range(size)])]
    ppermute x6 -> x3, waiting for transfers between devices: 70.8 us -> 22.6 us  [reduce_planes(): lax.ppermute(send_right, 'expert', [(i, i + 1) for i in range(0, t)])]
    convert_element_type x11 -> x4, other arithmetic: 35.3 us -> 1.72 us  [the longest x1 1.44 us: per_device(): gain_two = param(kv_rows, 1).reshape(-1).astype(F32)]
    pallas_call x0 -> x3, Pallas kernels: none -> 31.7 us  [the longest x1 16.7 us: weave_rows(): pl.pallas_call(weave_kernel, grid=(units // block,), in_specs=[pl.BlockSp...]
    reduce_scatter x3 -> x2, waiting for transfers between devices: 0.02 us -> 31.1 us  [the longest x1 31.1 us: per_device(): lax.psum_scatter(after(outs[0], dh_list[-1]), 'dp', scatter_dimension=0,...]
    ppermute x30, waiting for transfers between devices: 138 us -> 111 us  [shift_planes(): lax.ppermute(value, 'expert', [(i, (i + amount) % planes) for i in range(...]
    all_to_all x1 -> x0, blocking collectives: 26.1 us -> none  [per_device(): lax.all_to_all(packed, 'dp', split_axis=0, concat_axis=0, tiled=True)]
    dot_general x12, matrix products: 38.7 us -> 18.6 us  [cols_grad(): jnp.einsum('td,tc->dc', a_all[u], piece, preferred_element_type=F32)]
  transfers between devices with their start and end apart: 90 -> 82, of which waited for: 37 -> 48; matrix products, arithmetic and copies ran while one was open for 37% -> 28% of each run, Pallas kernels for 13% -> 15%
where the time goes in v4:
time: 1150 us; the launch traced here: 1140 us
  waiting for transfers between devices  403 us (35%)
  matrix products  223 us (19%)
  Pallas kernels  194 us (17%)
  starting transfers between devices  133 us (12%)
  local copies, waits for them, and re-layouts  86.8 us (8%)
  other arithmetic  81.5 us (7%)
  between operations  17 us (1%)
    ppermute x30, waiting for transfers between devices, shift_planes(): lax.ppermute(value, 'expert', [(i, (i + amount) % planes) for i in range(...  111 us
    pallas_call x2, Pallas kernels, mlp_experts(): pl.pallas_call(mlp_kernel, grid_spec=pltpu.PrefetchScalarGridSpec(num_sca...  101 us
    ppermute x16, waiting for transfers between devices, swap_dp(): return lax.ppermute(value, 'dp', [(i, i ^ mask) for i in range(size)])  89.4 us
    dot_general x28, matrix products, dot_f32(): return jnp.dot(left, right, preferred_element_type=F32)  53.3 us
    ppermute x30, starting transfers between devices, shift_planes(): lax.ppermute(value, 'expert', [(i, (i + amount) % planes) for i in range(...  44.7 us
    ppermute x6, waiting for transfers between devices, gather_planes(): lax.ppermute(left, 'expert', [(i + 1, i) for i in range(0, planes - d)])  44.4 us
    dot_general x2, matrix products, per_device(): jnp.einsum('rf,rd->fd', after(dhid_list[u], down_grad), b_rows_list[u], p...  41.7 us
    pallas_call x2, Pallas kernels, attn_backward(): pl.pallas_call(functools.partial(attn_backward_kernel, experts=experts, h...  37.6 us
  transfers between devices with their start and end apart: 82, of which 48 were waited for; matrix products, arithmetic and copies ran while one was open for 28% of the time, Pallas kernels for 15%

profile of v4, /device:TPU:8, one launch (start us, length us, event | category | flops | bytes accessed | tf_op | source)
XLA Modules:
  0.0 1138.6 jit_solution(16249780028633339548)
XLA Ops:
  21.4 14.9 %collective-permute-done.7 = bf16[64,2048]{1,0:T(8,128)(2,1)S(1)} collective-permute-done((bf16[64,2048]{1,0:T(8,128)(2,1)S(1)}, bf16[64,2048]{1,0:T(8,128)(2,1)S(1)}, u32[]{:S(2)}, u32[]{:S(2)}) %collective-permute-start.7) | collective-permute-done | bytes 262176 | tf_op jit(solution)/shard_map/ppermute | solution.py:365
  148.1 17.0 %collective-permute-done.11 = bf16[8,400,256]{2,1,0:T(8,128)(2,1)} collective-permute-done((bf16[8,400,256]{2,1,0:T(8,128)(2,1)}, bf16[8,400,256]{2,1,0:T(8,128)(2,1)}, u32[]{:S(2)}, u32[]{:S(2)}) %collective-permute-start.11) | collective-permute-done | bytes 1638432 | tf_op jit(solution)/shard_map/ppermute | solution.py:382
  181.9 21.4 %collective-permute-done.14 = bf16[8,400,256]{2,1,0:T(8,128)(2,1)S(1)} collective-permute-done((bf16[8,400,256]{2,1,0:T(8,128)(2,1)}, bf16[8,400,256]{2,1,0:T(8,128)(2,1)S(1)}, u32[]{:S(2)}, u32[]{:S(2)}) %collective-permute-start.14) | collective-permute-done | bytes 1638432 | tf_op jit(solution)/shard_map/ppermute | solution.py:383
  220.8 11.8 %shard_map.223 = (bf16[2,2,1024,128]{3,2,1,0:T(8,128)(2,1)}, bf16[2,1024,128]{2,1,0:T(8,128)(2,1)S(1)}, bf16[2,1024,128]{2,1,0:T(8,128)(2,1)S(1)}, bf16[2,2,1024,128]{3,2,1,0:T(8,128)(2,1)}, bf16[1024,1024]{1,0:T(8,128)(2,1)}) custom-call(s32[1024,2]{1,0:T(8,128)S(1)} %add_select_fusion.1.refs_0_.routes_ref, ...), custom_call_target="tpu_custom_call" | custom-call | flops 4294967296 | bytes 12582912 | tf_op jit(solution)/shard_map/pallas_call | solution.py:141
  276.1 11.6 %collective-permute-done.20 = bf16[256,2048]{1,0:T(8,128)(2,1)S(1)} collective-permute-done((bf16[256,2048]{1,0:T(8,128)(2,1)}, bf16[256,2048]{1,0:T(8,128)(2,1)S(1)}, u32[]{:S(2)}, u32[]{:S(2)}) %collective-permute-start.20) | collective-permute-done | bytes 1048608 | tf_op jit(solution)/shard_map/ppermute | solution.py:383
  346.5 17.1 %collective-permute-done.28 = bf16[64,2048]{1,0:T(8,128)(2,1)S(1)} collective-permute-done((bf16[64,2048]{1,0:T(8,128)(2,1)S(1)}, bf16[64,2048]{1,0:T(8,128)(2,1)S(1)}, u32[]{:S(2)}, u32[]{:S(2)}) %collective-permute-start.28) | collective-permute-done | bytes 262176 | tf_op jit(solution)/shard_map/ppermute | solution.py:365
  383.9 17.5 %collective-permute-done.31 = bf16[128,2048]{1,0:T(8,128)(2,1)S(1)} collective-permute-done((bf16[128,2048]{1,0:T(8,128)(2,1)S(1)}, bf16[128,2048]{1,0:T(8,128)(2,1)S(1)}, u32[]{:S(2)}, u32[]{:S(2)}) %collective-permute-start.31) | collective-permute-done | bytes 524320 | tf_op jit(solution)/shard_map/ppermute | solution.py:411
  420.0 15.1 %collective-permute-done.34 = bf16[64,2048]{1,0:T(8,128)(2,1)S(1)} collective-permute-done((bf16[64,2048]{1,0:T(8,128)(2,1)S(1)}, bf16[64,2048]{1,0:T(8,128)(2,1)S(1)}, u32[]{:S(2)}, u32[]{:S(2)}) %collective-permute-start.34) | collective-permute-done | bytes 262176 | tf_op jit(solution)/shard_map/ppermute | solution.py:365
  441.2 12.1 %fusion.214 = (bf16[1,704,1,2048]{3,2,1,0:T(2,128)(2,1)S(1)}, bf16[1,704,1,2048]{3,2,1,0:T(2,128)(2,1)S(1)}) fusion(bf16[1,704,2,2048]{3,2,1,0:T(2,128)(2,1)} %param.26), kind=kLoop, calls=%fused_computation.453 | loop fusion | bytes 11534336 | tf_op jit(solution)/shard_map/slice | solution.py:549
  477.1 50.3 %shard_map.225 = (bf16[2048,4096]{1,0:T(8,128)(2,1)}, bf16[2048,2176]{1,0:T(8,128)(2,1)}, bf16[2048,768]{1,0:T(8,128)(2,1)}, bf16[2048,1536]{1,0:T(8,128)(2,1)}) custom-call(s32[1]{0:T(128)} %bitcast.71.place_ref, bf16[2048,2048]{1,0:T(8,128)(2,1)} %all-gather.16.cloned.1.call-done.b_ref, bf16[2048,2048]{1,0:T(8,128)(2,1)} %all-gather.10.cloned.1.call-done.cot_ref, ...), custom_call_target="tpu_custom_call" | custom-call | flops 38654705664 | bytes 52428800 | tf_op jit(solution)/shard_map/pallas_call | solution.py:228
  529.8 51.1 %shard_map.226 = (bf16[2048,4096]{1,0:T(8,128)(2,1)}, bf16[2048,2176]{1,0:T(8,128)(2,1)}, bf16[2048,768]{1,0:T(8,128)(2,1)}, bf16[2048,1536]{1,0:T(8,128)(2,1)}) custom-call(s32[1]{0:T(128)} %bitcast.71.place_ref, bf16[2048,2048]{1,0:T(8,128)(2,1)} %all-gather.14.cloned.1.call-done.b_ref, ...), custom_call_target="tpu_custom_call", output_to_operand_aliasing={{0}: (7, {})} | custom-call | flops 38654705664 | bytes 52428800 | tf_op jit(solution)/shard_map/pallas_call | solution.py:228
  581.6 11.8 %fusion.230 = f32[768,2048]{1,0:T(8,128)} fusion(bf16[2048,768]{1,0:T(8,128)(2,1)} %get-tuple-element.100, bf16[2048,2048]{1,0:T(8,128)(2,1)} %all-gather.10.cloned.1.call-done.cot_ref), kind=kOutput, calls=%fused_computation.467 | convolution fusion | flops 6442450944 | bytes 17825792 | tf_op jit(solution)/shard_map/rf,rd->fd/dot_general | solution.py:639
  607.7 19.2 %fusion.231 = f32[1536,2048]{1,0:T(8,128)} fusion(bf16[2048,1536]{1,0:T(8,128)(2,1)} %get-tuple-element.101, bf16[2048,2048]{1,0:T(8,128)(2,1)} %all-gather.16.cloned.1.call-done.b_ref), kind=kOutput, calls=%fused_computation.468 | convolution fusion | flops 12884901888 | bytes 27262976 | tf_op jit(solution)/shard_map/rf,rd->fd/dot_general | solution.py:645
  641.4 13.8 %convolution_add_fusion.1 = f32[768,2048]{1,0:T(8,128)} fusion(f32[768,2048]{1,0:T(8,128)} %fusion.230, bf16[2048,768]{1,0:T(8,128)(2,1)} %get-tuple-element.105, bf16[2048,2048]{1,0:T(8,128)(2,1)} %all-gather.12.cloned.1.call-done.cot_ref), kind=kOutput, calls=%fused_computation.28 | convolution fusion | flops 6444023808 | bytes 24117248 | tf_op jit(solution)/shard_map/rf,rd->fd/dot_general | solution.py:639
  655.2 23.8 %reduce-scatter.5.cloned.1.call-done = bf16[256,2176]{1,0:T(8,128)(2,1)} async-done(((bf16[2048,2176]{1,0:T(8,128)(2,1)}), bf16[256,2176]{1,0:T(8,128)(2,1)}) %reduce-scatter.5.cloned.1.call-update) | async-done | bytes 1114128 | tf_op jit(solution)/shard_map/reduce_scatter | solution.py:634
  684.8 22.5 %convolution_add_fusion.first_ref.second_ref = f32[1536,2048]{1,0:T(8,128)} fusion(f32[1536,2048]{1,0:T(8,128)} %fusion.231, bf16[2048,1536]{1,0:T(8,128)(2,1)} %get-tuple-element.106, bf16[2048,2048]{1,0:T(8,128)(2,1)} %all-gather.14.cloned.1.call-done.b_ref), kind=kOutput, calls=%fused_computation.6 | convolution fusion | flops 12888047616 | bytes 39845888 | tf_op jit(solution)/shard_map/rf,rd->fd/dot_general | solution.py:645
  738.9 18.9 %shard_map.227 = bf16[1024,1664]{1,0:T(8,128)(2,1)} custom-call(s32[1024,2]{1,0:T(8,128)S(1)} %add_select_fusion.1.refs_0_.routes_ref, f32[1024,2]{1,0:T(8,128)S(1)} %copy-done.1, s32[1024,1]{1,0:T(8,128)S(1)} %copy.519.refs_2_.seg_col_ref, s32[1,1024]{1,0:T(1,128)S(1)} %get-tuple-element.349.refs_3_.seg_row_ref, f32[1024,128]{1,0:T(8,128)S(1)} %copy-done.3, ...), custom_call_target="tpu_custom_call" | custom-call | flops 10737418240 | bytes 12582912 | tf_op jit(solution)/shard_map/pallas_call | solution.py:167
  775.3 18.7 %shard_map.228 = bf16[1024,1664]{1,0:T(8,128)(2,1)} custom-call(s32[1024,2]{1,0:T(8,128)S(1)} %copy-done.9, f32[1024,2]{1,0:T(8,128)S(1)} %exponential_divide_fusion.refs_1_.gates_ref, s32[1024,1]{1,0:T(8,128)S(1)} %copy-done.7, s32[1,1024]{1,0:T(1,128)S(1)} %get-tuple-element.350.refs_3_.seg_row_ref, f32[1024,128]{1,0:T(8,128)S(1)} %copy-done.3, ...), custom_call_target="tpu_custom_call" | custom-call | flops 10737418240 | bytes 12582912 | tf_op jit(solution)/shard_map/pallas_call | solution.py:167
  870.6 12.0 %collective-permute-done.53 = bf16[128,2176]{1,0:T(8,128)(2,1)S(1)} collective-permute-done((bf16[128,2176]{1,0:T(8,128)(2,1)S(1)}, bf16[128,2176]{1,0:T(8,128)(2,1)S(1)}, u32[]{:S(2)}, u32[]{:S(2)}) %collective-permute-start.53) | collective-permute-done | bytes 557088 | tf_op jit(solution)/shard_map/ppermute | solution.py:411
  927.9 22.6 %collective-permute-done.63 = bf16[256,2048]{1,0:T(8,128)(2,1)} collective-permute-done((bf16[256,2048]{1,0:T(8,128)(2,1)}, bf16[256,2048]{1,0:T(8,128)(2,1)}, u32[]{:S(2)}, u32[]{:S(2)}) %collective-permute-start.63) | collective-permute-done | bytes 1048608 | tf_op jit(solution)/shard_map/ppermute | solution.py:402
  964.0 16.7 %shard_map.229 = f32[1,704,2,2048]{3,2,1,0:T(2,128)} custom-call(f32[1536,2048]{1,0:T(8,128)} %convolution_add_fusion.first_ref.second_ref, f32[1536,2048]{1,0:T(8,128)} %convolution_add_fusion.first_ref.second_ref), custom_call_target="tpu_custom_call" | custom-call | bytes 23068672 | tf_op jit(solution)/shard_map/pallas_call | solution.py:274
  1022.2 12.7 %collective-permute-done.62 = f32[10,2048]{1,0:T(8,128)S(1)} collective-permute-done((f32[10,2048]{1,0:T(8,128)S(1)}, f32[10,2048]{1,0:T(8,128)S(1)}, u32[]{:S(2)}, u32[]{:S(2)}) %collective-permute-start.62) | collective-permute-done | bytes 81952 | tf_op jit(solution)/shard_map/ppermute | solution.py:418
  1047.5 31.1 %reduce-scatter.9.cloned.1.call-done = bf16[256,4096]{1,0:T(8,128)(2,1)} async-done(((bf16[2048,4096]{1,0:T(8,128)(2,1)}), bf16[256,4096]{1,0:T(8,128)(2,1)}) %reduce-scatter.9.cloned.1.call-update) | async-done | bytes 2097168 | tf_op jit(solution)/shard_map/reduce_scatter | solution.py:748
  1100.6 17.4 %collective-permute-done.45 = bf16[64,2048]{1,0:T(8,128)(2,1)} collective-permute-done((bf16[64,2048]{1,0:T(8,128)(2,1)}, bf16[64,2048]{1,0:T(8,128)(2,1)}, u32[]{:S(2)}, u32[]{:S(2)}) %collective-permute-start.45) | collective-permute-done | bytes 262176 | tf_op jit(solution)/shard_map/ppermute | solution.py:365
  (722 shorter events, 640.8 us)
Async XLA Ops:
  7.2 101.8 %all-gather.8.cloned.1.call-start = ((), (), s32[]{:S(2)}) async-start(), calls=%async_computation.6 | async-start | bytes 9437184 | tf_op jit(solution)/shard_map/all_gather | solution.py:523
  7.9 232.9 %all-gather.10.cloned.1.call-start = ((), (), s32[]{:S(2)}) async-start(), calls=%async_computation.7 | async-start | bytes 9437184 | tf_op jit(solution)/shard_map/all_gather | solution.py:499
  45.7 36.4 %all-to-all-start = ((bf16[8,400,256]{2,1,0:T(8,128)(2,1)}), bf16[8,400,256]{2,1,0:T(8,128)(2,1)}, u32[]{:S(2)}, u32[]{:S(2)}) async-start(bf16[8,400,256]{2,1,0:T(8,128)(2,1)} %pad_maximum_fusion.2), calls=%async_computation | async-start | bytes 3276800 | tf_op jit(solution)/shard_map/all_to_all | solution.py:518
  50.1 214.4 %all-gather.12.cloned.1.call-start = ((), (), s32[]{:S(2)}) async-start(), calls=%async_computation.8 | async-start | bytes 9437184 | tf_op jit(solution)/shard_map/all_gather | solution.py:499
  77.9 399.3 %all-gather.16.cloned.1.call-start = ((), (), s32[]{:S(2)}) async-start(), calls=%async_computation.10 | async-start | bytes 9437184 | tf_op jit(solution)/shard_map/all_gather | solution.py:499
  91.7 39.3 %collective-permute-start.4 = (bf16[8,400,256]{2,1,0:T(8,128)(2,1)}, bf16[8,400,256]{2,1,0:T(8,128)(2,1)}, u32[]{:S(2)}, u32[]{:S(2)}) collective-permute-start(bf16[8,400,256]{2,1,0:T(8,128)(2,1)} %all-to-all-done), channel_id=1, source_target_pairs={{0,1},{1,2},{2,3},{4,5},{5,6},{6,7},{8,9},{9,10},{10,11},{12,13},{... | collective-permute-start | bytes 4915208 | tf_op jit(solution)/shard_map/ppermute | solution.py:382
  93.6 37.4 %collective-permute-start.3 = (bf16[8,400,256]{2,1,0:T(8,128)(2,1)}, bf16[8,400,256]{2,1,0:T(8,128)(2,1)}, u32[]{:S(2)}, u32[]{:S(2)}) collective-permute-start(bf16[8,400,256]{2,1,0:T(8,128)(2,1)} %all-to-all-done), channel_id=1, source_target_pairs={{1,0},{2,1},{3,2},{5,4},{6,5},{7,6},{9,8},{10,9},{11,10},{13,12},{... | collective-permute-start | bytes 4915208 | tf_op jit(solution)/shard_map/ppermute | solution.py:383
  135.6 34.8 %collective-permute-start.13 = (bf16[8,400,256]{2,1,0:T(8,128)(2,1)}, bf16[8,400,256]{2,1,0:T(8,128)(2,1)}, u32[]{:S(2)}, u32[]{:S(2)}) collective-permute-start(bf16[8,400,256]{2,1,0:T(8,128)(2,1)} %collective-permute-done.3), channel_id=1, source_target_pairs={{1,0},{2,1},{5,4},{6,5},{9,8},{10,9},{13,12},{14,13},{17,16},{18,1... | collective-permute-start | bytes 4915208 | tf_op jit(solution)/shard_map/ppermute | solution.py:383
  205.0 35.8 %collective-permute-start.16 = (bf16[256,2048]{1,0:T(8,128)(2,1)}, bf16[256,2048]{1,0:T(8,128)(2,1)}, u32[]{:S(2)}, u32[]{:S(2)}) collective-permute-start(bf16[256,2048]{1,0:T(8,128)(2,1)} %bitcast.56), channel_id=1, source_target_pairs={{0,1},{1,2},{2,3},{4,5},{5,6},{6,7},{8,9},{9,10},{10,11},{12,13},{... | collective-permute-start | bytes 3145736 | tf_op jit(solution)/shard_map/ppermute | solution.py:382
  206.9 40.2 %collective-permute-start.15 = (bf16[256,2048]{1,0:T(8,128)(2,1)}, bf16[256,2048]{1,0:T(8,128)(2,1)}, u32[]{:S(2)}, u32[]{:S(2)}) collective-permute-start(bf16[256,2048]{1,0:T(8,128)(2,1)} %bitcast.56), channel_id=1, source_target_pairs={{1,0},{2,1},{3,2},{5,4},{6,5},{7,6},{9,8},{10,9},{11,10},{13,12},{... | collective-permute-start | bytes 3145736 | tf_op jit(solution)/shard_map/ppermute | solution.py:383
  366.9 162.8 %all-gather.14.cloned.1.call-start = ((), (), s32[]{:S(2)}) async-start(), calls=%async_computation.9 | async-start | bytes 9437184 | tf_op jit(solution)/shard_map/all_gather | solution.py:499
  441.0 160.5 %reduce-scatter.7.cloned.1.call-start = ((), (), s32[]{:S(2)}) async-start(), calls=%async_computation.12 | async-start | bytes 10027008 | tf_op jit(solution)/shard_map/reduce_scatter | solution.py:634
  527.5 151.4 %reduce-scatter.5.cloned.1.call-start = ((), (), s32[]{:S(2)}) async-start(), calls=%async_computation.11 | async-start | bytes 10027008 | tf_op jit(solution)/shard_map/reduce_scatter | solution.py:634
  580.8 137.3 %all-gather.18.cloned.1.call-start = ((), (), s32[]{:S(2)}) async-start(), calls=%async_computation.13 | async-start | bytes 4718592 | tf_op jit(solution)/shard_map/all_gather | solution.py:664
  639.8 125.4 %all-gather.20.cloned.1.call-start = ((), (), s32[]{:S(2)}) async-start(), calls=%async_computation.14 | async-start | bytes 4718592 | tf_op jit(solution)/shard_map/all_gather | solution.py:664
  728.3 281.5 %reduce-scatter.11.cloned.1.call-start = ((), (), s32[]{:S(2)}) async-start(), calls=%async_computation.16 | async-start | bytes 7864320 | tf_op jit(solution)/shard_map/reduce_scatter | solution.py:733
  819.4 259.1 %reduce-scatter.9.cloned.1.call-start = ((), (), s32[]{:S(2)}) async-start(), calls=%async_computation.15 | async-start | bytes 18874368 | tf_op jit(solution)/shard_map/reduce_scatter | solution.py:748
  927.8 52.9 %collective-permute-start.58 = (f32[10,2048]{1,0:T(8,128)S(1)}, f32[10,2048]{1,0:T(8,128)S(1)}, u32[]{:S(2)}, u32[]{:S(2)}) collective-permute-start(f32[10,2048]{1,0:T(8,128)S(1)} %pad_maximum_fusion.13), channel_id=1, source_target_pairs={{0,4},{4,0},{8,12},{12,8},{16,20},{20,16},{24,28},{28,24},{1,5},{5... | collective-permute-start | bytes 245768 | tf_op jit(solution)/shard_map/ppermute | solution.py:418
  954.7 43.5 %collective-permute-start.64 = (bf16[256,2048]{1,0:T(8,128)(2,1)}, bf16[256,2048]{1,0:T(8,128)(2,1)}, u32[]{:S(2)}, u32[]{:S(2)}) collective-permute-start(bf16[256,2048]{1,0:T(8,128)(2,1)} %get-tuple-element.274), channel_id=1, source_target_pairs={{0,1},{1,2},{4,5},{5,6},{8,9},{9,10},{12,13},{13,14},{16,17},{17,1... | collective-permute-start | bytes 3145736 | tf_op jit(solution)/shard_map/ppermute | solution.py:402
  959.2 39.0 %collective-permute-start.67 = (bf16[256,2048]{1,0:T(8,128)(2,1)S(1)}, bf16[256,2048]{1,0:T(8,128)(2,1)}, u32[]{:S(2)}, u32[]{:S(2)}) collective-permute-start(bf16[256,2048]{1,0:T(8,128)(2,1)S(1)} %get-tuple-element.275), channel_id=1, source_target_pairs={{2,1},{3,2},{6,5},{7,6},{10,9},{11,10},{14,13},{15,14},{18,17},{19... | collective-permute-start | bytes 3145736 | tf_op jit(solution)/shard_map/ppermute | solution.py:403
  1009.8 36.8 %all-to-all-start.1 = ((bf16[8,384,256]{2,1,0:T(8,128)(2,1)}), bf16[8,384,256]{2,1,0:T(8,128)(2,1)S(1)}, u32[]{:S(2)}, u32[]{:S(2)}) async-start(bf16[8,384,256]{2,1,0:T(8,128)(2,1)} %bitcast.580), calls=%async_computation.5 | async-start | bytes 3145728 | tf_op jit(solution)/shard_map/all_to_all | solution.py:760
  1082.8 35.2 %collective-permute-start.45 = (bf16[64,2048]{1,0:T(8,128)(2,1)}, bf16[64,2048]{1,0:T(8,128)(2,1)}, u32[]{:S(2)}, u32[]{:S(2)}) collective-permute-start(bf16[64,2048]{1,0:T(8,128)(2,1)} %get-tuple-element.290), channel_id=1, source_target_pairs={{0,2},{1,3},{2,0},{3,1},{4,6},{5,7},{6,4},{7,5},{8,10},{9,11},{10,... | collective-permute-start | bytes 786440 | tf_op jit(solution)/shard_map/ppermute | solution.py:365
  1084.2 34.6 %collective-permute-start.44 = (bf16[64,2048]{1,0:T(8,128)(2,1)}, bf16[64,2048]{1,0:T(8,128)(2,1)}, u32[]{:S(2)}, u32[]{:S(2)}) collective-permute-start(bf16[64,2048]{1,0:T(8,128)(2,1)} %get-tuple-element.291), channel_id=1, source_target_pairs={{0,3},{1,0},{2,1},{3,2},{4,7},{5,4},{6,5},{7,6},{8,11},{9,8},{10,9... | collective-permute-start | bytes 786440 | tf_op jit(solution)/shard_map/ppermute | solution.py:365
  1090.9 37.0 %collective-permute-start.48 = (bf16[64,2048]{1,0:T(8,128)(2,1)}, bf16[64,2048]{1,0:T(8,128)(2,1)S(1)}, u32[]{:S(2)}, u32[]{:S(2)}) collective-permute-start(bf16[64,2048]{1,0:T(8,128)(2,1)} %get-tuple-element.286), channel_id=1, source_target_pairs={{0,2},{1,3},{2,0},{3,1},{4,6},{5,7},{6,4},{7,5},{8,10},{9,11},{10,... | collective-permute-start | bytes 786440 | tf_op jit(solution)/shard_map/ppermute | solution.py:365
  (185 other events, 4532.2 us)
Sparse Core Ops, SparseCore 0:
  9.9 68.7 all-gather.7
  81.1 58.7 all-gather.9
  142.4 54.3 all-gather.11
  367.1 75.6 all-gather.15
  445.0 54.3 all-gather.13
  527.6 73.8 reduce-scatter.6
  605.1 73.7 reduce-scatter.4
  681.4 36.6 all-gather.17
  728.4 36.7 all-gather.19
  819.5 110.7 reduce-scatter.10
  933.9 144.5 reduce-scatter.8

commit v5 on v4

--- a/solution.py
+++ b/solution.py
@@ -389,21 +389,21 @@
     return gathered
 
 
-def reduce_planes(parts, holds):
+def reduce_planes(parts):
     planes = len(parts)
     right, left = None, None
+    arrivals = []
     for t in range(1, planes):
         send_right, send_left = parts[planes - t], parts[t]
         if right is not None:
             send_right = (send_right.astype(F32) + right.astype(F32)).astype(BF16)
             send_left = (send_left.astype(F32) + left.astype(F32)).astype(BF16)
-        if t in holds:
-            send_right, send_left = after(send_right, *holds[t]), after(send_left, *holds[t])
         right = lax.ppermute(send_right, "expert", [(i, i + 1) for i in range(0, t)])
         left = lax.ppermute(
             send_left, "expert", [(i, i - 1) for i in range(planes - t, planes)]
         )
-    return parts[0].astype(F32) + right.astype(F32) + left.astype(F32)
+        arrivals.append((right, left))
+    return parts[0].astype(F32) + right.astype(F32) + left.astype(F32), arrivals
 
 
 def swap_dp(value, mask):
@@ -420,7 +420,7 @@
     return value
 
 
-def reduce_rows(left, matmul, me, hold=None):
+def reduce_rows(left, matmul, me, holds=()):
     size = lax.axis_size("dp")
     blocks = left.reshape(size // 2, 2, left.shape[0] // size, left.shape[1])
     core, chip = me % 2, me // 2
@@ -433,7 +433,7 @@
     mine = half(core) + arrived.astype(F32)
     low = mine.astype(BF16)
     total = lax.dynamic_index_in_dim(low, chip, axis=0, keepdims=False)
-    total = (total if hold is None else after(total, hold)).astype(F32)
+    total = after(total, *holds).astype(F32)
     for other in range(1, size // 2):
         send = lax.dynamic_index_in_dim(low, chip ^ other, axis=0, keepdims=False)
         total = total + swap_dp(send, 2 * other).astype(F32)
@@ -544,12 +544,6 @@
     router_wide = jnp.pad(router_two_low, ((0, 0), (0, 128 - experts)))
 
     hidden_units = down_maps.shape[1]
-    padding = ((0, -hidden_units % 128), (0, 0))
-    gate_up_local = jnp.concatenate(
-        [jnp.pad(gate_up[0, :, 0], padding), jnp.pad(gate_up[0, :, 1], padding)], axis=0
-    )
-    down_local = jnp.pad(down_maps[0], padding)
-    hidden_padded = down_local.shape[0]
     place = plane.astype(jnp.int32)[None]
 
     cosine, sine_table = rope_tables(jnp.arange(length, dtype=jnp.int32), HEAD_WIDTH // 2)
@@ -595,11 +589,18 @@
     output_list = after(output_maps[0], packed[1], packed[-1])
     output_list = gather_planes(output_list, plane, {1: (gated[0], cot_rows_list[0]), 2: (gated[-1], cot_rows_list[-1])})
     output_rows = jnp.concatenate(output_list, axis=0)
+    padding = ((0, -hidden_units % 128), (0, 0))
+    gate_up_now = after(gate_up, gated[-1])
+    gate_up_local = jnp.concatenate(
+        [jnp.pad(gate_up_now[0, :, 0], padding), jnp.pad(gate_up_now[0, :, 1], padding)], axis=0
+    )
+    down_local = jnp.pad(after(down_maps, gated[-1])[0], padding)
+
     b_home, inverse_two, onehot_mlp, gates_mlp, moved, sent = [], [], [], [], [], []
     for u in each:
         gated_now = after(gated[u], *sent)
         attn_sum, low = reduce_rows(
-            gated_now, lambda rows: dot_f32(rows, output_rows), my_dp, moved[-1] if moved else None
+            gated_now, lambda rows: dot_f32(rows, output_rows), my_dp, moved[-1:] + [gate_up_local, down_local] if moved else []
         )
         sent.append(low)
         states.append(inputs[u] + attn_sum)
@@ -673,10 +674,17 @@
         ],
         axis=0,
     )
-    g_list = []
+    g_list, output_part = [], 0.0
     for u in each:
         dh_now = after(dh_list[u], *(g_list[-1:] or grad_states[-1:]))
         grad_context = jnp.einsum("td,cd->tc", dh_now, output_rows, preferred_element_type=F32)
+        if u == units - 1:
+            for v in each:
+                output_part = output_part + jnp.einsum(
+                    "tc,td->cd", gated[v], after(dh_list[v], dh_now), preferred_element_type=F32
+                )
+            output_part = output_part.astype(BF16)
+            grad_context = after(grad_context, output_part)
         g_list.append(
             attn_backward(
                 routes_here[u],
@@ -689,6 +697,8 @@
             )
         )
 
+    out_rows = lax.psum_scatter(after(outs[0], g_list[0]), "dp", scatter_dimension=0, tiled=True)
+
     dla_list = []
 
     def cols_grad(c, hold):
@@ -718,7 +728,10 @@
         input_parts.append(grad_states[u] + grad_inputs)
         return low
 
-    done = g_list[-1]
+    output_grad, arrivals = reduce_planes(
+        [output_part[c * head_cols : (c + 1) * head_cols] for c in range(planes)]
+    )
+    done = after(g_list[-1], *arrivals[0])
     query_parts = []
     for e in range(planes):
         done = cols_grad((e - plane) % planes, done)
@@ -730,22 +743,13 @@
     packed_grad = jnp.concatenate(
         [jnp.stack(query_parts, axis=0)] + [part.transpose(1, 0, 2, 3) for part in kv_part], axis=2
     )
+    both_grad = after(both_grad, done)
+    gate_up_grad = weave_rows(both_grad, hidden_units)
+    down_grad = after(down_grad, done)[:hidden_units]
+
+    packed_grad = after(packed_grad, out_rows, output_grad, gate_up_grad)
     packed_grad = lax.psum_scatter(packed_grad, "expert", scatter_dimension=0, tiled=False)
-    for u in each[:-1]:
-        done = finish_inputs(u, done)
-    done = finish_inputs(units - 1, done)
-    output_part = 0.0
-    for u in each:
-        output_part = output_part + jnp.einsum(
-            "tc,td->cd", after(gated[u], done), dh_list[u], preferred_element_type=F32
-        )
-    output_part = output_part.astype(BF16)
-
-    both_grad = after(both_grad, output_part)
-    gate_up_grad = weave_rows(both_grad, hidden_units)
-    down_grad = after(down_grad, output_part)[:hidden_units]
-
-    out_rows = lax.psum_scatter(after(outs[0], dh_list[-1]), "dp", scatter_dimension=0, tiled=True)
+
     for u in each:
         out_slots = to_home(out_rows[:, u * width : (u + 1) * width])
         gated_table = jnp.sum(hits_list[u] * gates_mlp[u][None], axis=2).T
@@ -754,9 +758,9 @@
         mlp_sum = dot_f32(gated_high, out_slots) + dot_f32(gated_low, out_slots)
         mixed_parts.append((states[u] + mlp_sum).astype(BF16))
 
-    output_grad = reduce_planes(
-        [output_part[c * head_cols : (c + 1) * head_cols] for c in range(planes)], {}
-    )
+    for u in each:
+        done = after(done, *mixed_parts[: u])
+        done = finish_inputs(u, done)
     packed_grad = lax.all_to_all(packed_grad, "dp", split_axis=0, concat_axis=0, tiled=True)
     packed_grad = packed_grad.transpose(1, 0, 2).reshape(-1, width).astype(F32)
     query_grad = packed_grad[:query_rows]

time: 1150 us -> 1090 us (0.948)
  waiting for transfers between devices: 403 us -> 338 us
  starting transfers between devices: 133 us -> 145 us
    reduce_scatter x1, waiting for transfers between devices: 31.1 us -> 0.01 us  [per_device(): lax.psum_scatter(after(outs[0], g_list[0]), 'dp', scatter_dimension=0, ti...]
    ppermute x16, waiting for transfers between devices: 89.4 us -> 73.4 us  [swap_dp(): return lax.ppermute(value, 'dp', [(i, i ^ mask) for i in range(size)])]
    ppermute x5, waiting for transfers between devices: 26.2 us -> 13.2 us  [all_sum(): lax.ppermute(value, axis, [(i, i ^ mask) for i in range(size)])]
    slice x3 -> x2, local copies, waits for them, and re-layouts: 12.2 us -> 0.18 us  [the longest x1 12.1 us: per_device(): gate_up[0, :, 0]]
    ppermute x30, starting transfers between devices: 44.7 us -> 56.4 us  [shift_planes(): lax.ppermute(value, 'expert', [(i, (i + amount) % planes) for i in range(...]
  transfers between devices with their start and end apart: 82 -> 82, of which waited for: 48 -> 44; matrix products, arithmetic and copies ran while one was open for 28% -> 31% of each run, Pallas kernels for 15% -> 18%
where the time goes in v5:
time: 1090 us; the launch traced here: 1080 us
  waiting for transfers between devices  338 us (31%)
  matrix products  226 us (21%)
  Pallas kernels  194 us (18%)
  starting transfers between devices  145 us (13%)
  local copies, waits for them, and re-layouts  84.3 us (8%)
  other arithmetic  79.5 us (7%)
  between operations  16.7 us (2%)
    pallas_call x2, Pallas kernels, mlp_experts(): pl.pallas_call(mlp_kernel, grid_spec=pltpu.PrefetchScalarGridSpec(num_sca...  101 us
    ppermute x30, waiting for transfers between devices, shift_planes(): lax.ppermute(value, 'expert', [(i, (i + amount) % planes) for i in range(...  99.9 us
    ppermute x16, waiting for transfers between devices, swap_dp(): return lax.ppermute(value, 'dp', [(i, i ^ mask) for i in range(size)])  73.4 us
    ppermute x30, starting transfers between devices, shift_planes(): lax.ppermute(value, 'expert', [(i, (i + amount) % planes) for i in range(...  56.4 us
    dot_general x28, matrix products, dot_f32(): return jnp.dot(left, right, preferred_element_type=F32)  54.7 us
    ppermute x6, waiting for transfers between devices, gather_planes(): lax.ppermute(left, 'expert', [(i + 1, i) for i in range(0, planes - d)])  53.9 us
    dot_general x2, matrix products, per_device(): jnp.einsum('rf,rd->fd', after(dhid_list[u], down_grad), b_rows_list[u], p...  41.7 us
    pallas_call x2, Pallas kernels, attn_backward(): pl.pallas_call(functools.partial(attn_backward_kernel, experts=experts, h...  38.1 us
  transfers between devices with their start and end apart: 82, of which 44 were waited for; matrix products, arithmetic and copies ran while one was open for 31% of the time, Pallas kernels for 18%

profile of v5, /device:TPU:8, one launch (start us, length us, event | category | flops | bytes accessed | tf_op | source)
XLA Modules:
  0.0 1082.8 jit_solution(5180521287554158710)
XLA Ops:
  21.8 14.9 %collective-permute-done.7 = bf16[64,2048]{1,0:T(8,128)(2,1)S(1)} collective-permute-done((bf16[64,2048]{1,0:T(8,128)(2,1)S(1)}, bf16[64,2048]{1,0:T(8,128)(2,1)S(1)}, u32[]{:S(2)}, u32[]{:S(2)}) %collective-permute-start.7) | collective-permute-done | bytes 262176 | tf_op jit(solution)/shard_map/ppermute | solution.py:365
  115.1 15.9 %collective-permute-done.3 = bf16[8,400,256]{2,1,0:T(8,128)(2,1)} collective-permute-done((bf16[8,400,256]{2,1,0:T(8,128)(2,1)}, bf16[8,400,256]{2,1,0:T(8,128)(2,1)}, u32[]{:S(2)}, u32[]{:S(2)}) %collective-permute-start.3) | collective-permute-done | bytes 1638432 | tf_op jit(solution)/shard_map/ppermute | solution.py:383
  145.5 19.2 %collective-permute-done.11 = bf16[8,400,256]{2,1,0:T(8,128)(2,1)} collective-permute-done((bf16[8,400,256]{2,1,0:T(8,128)(2,1)}, bf16[8,400,256]{2,1,0:T(8,128)(2,1)}, u32[]{:S(2)}, u32[]{:S(2)}) %collective-permute-start.11) | collective-permute-done | bytes 1638432 | tf_op jit(solution)/shard_map/ppermute | solution.py:382
  181.7 21.3 %collective-permute-done.14 = bf16[8,400,256]{2,1,0:T(8,128)(2,1)S(1)} collective-permute-done((bf16[8,400,256]{2,1,0:T(8,128)(2,1)}, bf16[8,400,256]{2,1,0:T(8,128)(2,1)S(1)}, u32[]{:S(2)}, u32[]{:S(2)}) %collective-permute-start.14) | collective-permute-done | bytes 1638432 | tf_op jit(solution)/shard_map/ppermute | solution.py:383
  220.6 12.1 %shard_map.223 = (bf16[2,2,1024,128]{3,2,1,0:T(8,128)(2,1)}, bf16[2,1024,128]{2,1,0:T(8,128)(2,1)S(1)}, bf16[2,1024,128]{2,1,0:T(8,128)(2,1)S(1)}, bf16[2,2,1024,128]{3,2,1,0:T(8,128)(2,1)}, bf16[1024,1024]{1,0:T(8,128)(2,1)}) custom-call(s32[1024,2]{1,0:T(8,128)S(1)} %copy-done.2, f32[1024,2]{1,0:T(8,128)S(1)} %exponential_divide_fusion.1.refs_1_.gates_ref, ...), custom_call_target="tpu_custom_call" | custom-call | flops 4294967296 | bytes 12582912 | tf_op jit(solution)/shard_map/pallas_call | solution.py:141
  251.5 11.7 %shard_map.224 = (bf16[2,2,1024,128]{3,2,1,0:T(8,128)(2,1)}, bf16[2,1024,128]{2,1,0:T(8,128)(2,1)S(1)}, bf16[2,1024,128]{2,1,0:T(8,128)(2,1)S(1)}, bf16[2,2,1024,128]{3,2,1,0:T(8,128)(2,1)}, bf16[1024,1024]{1,0:T(8,128)(2,1)}) custom-call(s32[1024,2]{1,0:T(8,128)S(1)} %add_select_fusion.refs_0_.routes_ref, ...), custom_call_target="tpu_custom_call" | custom-call | flops 4294967296 | bytes 12582912 | tf_op jit(solution)/shard_map/pallas_call | solution.py:141
  276.0 11.8 %collective-permute-done.20 = bf16[256,2048]{1,0:T(8,128)(2,1)S(1)} collective-permute-done((bf16[256,2048]{1,0:T(8,128)(2,1)}, bf16[256,2048]{1,0:T(8,128)(2,1)S(1)}, u32[]{:S(2)}, u32[]{:S(2)}) %collective-permute-start.20) | collective-permute-done | bytes 1048608 | tf_op jit(solution)/shard_map/ppermute | solution.py:383
  325.3 12.3 %collective-permute-done.23 = bf16[128,2048]{1,0:T(8,128)(2,1)} collective-permute-done((bf16[128,2048]{1,0:T(8,128)(2,1)}, bf16[128,2048]{1,0:T(8,128)(2,1)}, u32[]{:S(2)}, u32[]{:S(2)}) %collective-permute-start.23) | collective-permute-done | bytes 524320 | tf_op jit(solution)/shard_map/ppermute | solution.py:411
  347.9 16.7 %collective-permute-done.28 = bf16[64,2048]{1,0:T(8,128)(2,1)S(1)} collective-permute-done((bf16[64,2048]{1,0:T(8,128)(2,1)S(1)}, bf16[64,2048]{1,0:T(8,128)(2,1)S(1)}, u32[]{:S(2)}, u32[]{:S(2)}) %collective-permute-start.28) | collective-permute-done | bytes 262176 | tf_op jit(solution)/shard_map/ppermute | solution.py:365
  460.5 50.3 %shard_map.225 = (bf16[2048,4096]{1,0:T(8,128)(2,1)}, bf16[2048,2176]{1,0:T(8,128)(2,1)}, bf16[2048,768]{1,0:T(8,128)(2,1)}, bf16[2048,1536]{1,0:T(8,128)(2,1)}) custom-call(s32[1]{0:T(128)} %bitcast.71.place_ref, bf16[2048,2048]{1,0:T(8,128)(2,1)} %all-gather.16.cloned.1.call-done.b_ref, bf16[2048,2048]{1,0:T(8,128)(2,1)} %all-gather.10.cloned.1.call-done.cot_ref, ...), custom_call_target="tpu_custom_call" | custom-call | flops 38654705664 | bytes 52428800 | tf_op jit(solution)/shard_map/pallas_call | solution.py:228
  513.5 50.7 %shard_map.226 = (bf16[2048,4096]{1,0:T(8,128)(2,1)}, bf16[2048,2176]{1,0:T(8,128)(2,1)}, bf16[2048,768]{1,0:T(8,128)(2,1)}, bf16[2048,1536]{1,0:T(8,128)(2,1)}) custom-call(s32[1]{0:T(128)} %bitcast.71.place_ref, bf16[2048,2048]{1,0:T(8,128)(2,1)} %all-gather.14.cloned.1.call-done.b_ref, ...), custom_call_target="tpu_custom_call", output_to_operand_aliasing={{0}: (7, {})} | custom-call | flops 38654705664 | bytes 52428800 | tf_op jit(solution)/shard_map/pallas_call | solution.py:228
  565.9 11.9 %fusion.223 = f32[768,2048]{1,0:T(8,128)} fusion(bf16[2048,768]{1,0:T(8,128)(2,1)} %get-tuple-element.108, bf16[2048,2048]{1,0:T(8,128)(2,1)} %all-gather.10.cloned.1.call-done.cot_ref), kind=kOutput, calls=%fused_computation.462 | convolution fusion | flops 6442450944 | bytes 17825792 | tf_op jit(solution)/shard_map/rf,rd->fd/dot_general | solution.py:640
  592.0 19.1 %fusion.224 = f32[1536,2048]{1,0:T(8,128)} fusion(bf16[2048,1536]{1,0:T(8,128)(2,1)} %get-tuple-element.109, bf16[2048,2048]{1,0:T(8,128)(2,1)} %all-gather.16.cloned.1.call-done.b_ref), kind=kOutput, calls=%fused_computation.463 | convolution fusion | flops 12884901888 | bytes 27262976 | tf_op jit(solution)/shard_map/rf,rd->fd/dot_general | solution.py:646
  627.6 13.8 %convolution_add_fusion.1 = f32[768,2048]{1,0:T(8,128)} fusion(f32[768,2048]{1,0:T(8,128)} %fusion.223, bf16[2048,768]{1,0:T(8,128)(2,1)} %get-tuple-element.114, bf16[2048,2048]{1,0:T(8,128)(2,1)} %all-gather.12.cloned.1.call-done.cot_ref), kind=kOutput, calls=%fused_computation.28 | convolution fusion | flops 6444023808 | bytes 24117248 | tf_op jit(solution)/shard_map/rf,rd->fd/dot_general | solution.py:640
  641.5 22.0 %reduce-scatter.7.cloned.1.call-done = bf16[256,2176]{1,0:T(8,128)(2,1)} async-done(((bf16[2048,2176]{1,0:T(8,128)(2,1)}), bf16[256,2176]{1,0:T(8,128)(2,1)}) %reduce-scatter.7.cloned.1.call-update) | async-done | bytes 1114128 | tf_op jit(solution)/shard_map/reduce_scatter | solution.py:635
  669.7 22.6 %convolution_add_fusion.first_ref.second_ref = f32[1536,2048]{1,0:T(8,128)} fusion(f32[1536,2048]{1,0:T(8,128)} %fusion.224, bf16[2048,1536]{1,0:T(8,128)(2,1)} %get-tuple-element.115, bf16[2048,2048]{1,0:T(8,128)(2,1)} %all-gather.14.cloned.1.call-done.b_ref), kind=kOutput, calls=%fused_computation.6 | convolution fusion | flops 12888047616 | bytes 39845888 | tf_op jit(solution)/shard_map/rf,rd->fd/dot_general | solution.py:646
  724.3 18.8 %shard_map.227 = bf16[1024,1664]{1,0:T(8,128)(2,1)} custom-call(s32[1024,2]{1,0:T(8,128)S(1)} %copy-done.3, f32[1024,2]{1,0:T(8,128)S(1)} %copy-done.1, s32[1024,1]{1,0:T(8,128)S(1)} %copy.519.refs_2_.seg_col_ref, s32[1,1024]{1,0:T(1,128)S(1)} %get-tuple-element.358.refs_3_.seg_row_ref, f32[1024,128]{1,0:T(8,128)S(1)} %get-tuple-element.386.refs_4_.cos_ref, ...), custom_call_target="tpu_custom_call" | custom-call | flops 10737418240 | bytes 12582912 | tf_op jit(solution)/shard_map/pallas_call | solution.py:167
  779.7 19.3 %shard_map.228 = bf16[1024,1664]{1,0:T(8,128)(2,1)} custom-call(s32[1024,2]{1,0:T(8,128)S(1)} %add_select_fusion.refs_0_.routes_ref, f32[1024,2]{1,0:T(8,128)S(1)} %exponential_divide_fusion.refs_1_.gates_ref, s32[1024,1]{1,0:T(8,128)S(1)} %copy.520.refs_2_.seg_col_ref, s32[1,1024]{1,0:T(1,128)S(1)} %get-tuple-element.359.refs_3_.seg_row_ref, ...), custom_call_target="tpu_custom_call" | custom-call | flops 10737418240 | bytes 12582912 | tf_op jit(solution)/shard_map/pallas_call | solution.py:167
  828.5 17.2 %collective-permute-done.65 = bf16[256,2048]{1,0:T(8,128)(2,1)S(1)} collective-permute-done((bf16[256,2048]{1,0:T(8,128)(2,1)S(1)}, bf16[256,2048]{1,0:T(8,128)(2,1)S(1)}, u32[]{:S(2)}, u32[]{:S(2)}) %collective-permute-start.65) | collective-permute-done | bytes 1048608 | tf_op jit(solution)/shard_map/ppermute | solution.py:401
  860.3 16.2 %shard_map.229 = f32[1,704,2,2048]{3,2,1,0:T(2,128)} custom-call(f32[1536,2048]{1,0:T(8,128)} %convolution_add_fusion.first_ref.second_ref, f32[1536,2048]{1,0:T(8,128)} %convolution_add_fusion.first_ref.second_ref), custom_call_target="tpu_custom_call" | custom-call | bytes 23068672 | tf_op jit(solution)/shard_map/pallas_call | solution.py:274
  957.7 10.9 %collective-permute-done.56 = bf16[128,2176]{1,0:T(8,128)(2,1)} collective-permute-done((bf16[128,2176]{1,0:T(8,128)(2,1)}, bf16[128,2176]{1,0:T(8,128)(2,1)}, u32[]{:S(2)}, u32[]{:S(2)}) %collective-permute-start.56) | collective-permute-done | bytes 557088 | tf_op jit(solution)/shard_map/ppermute | solution.py:411
  1010.9 11.1 %collective-permute-start.49 = (bf16[64,2048]{1,0:T(8,128)(2,1)}, bf16[64,2048]{1,0:T(8,128)(2,1)}, u32[]{:S(2)}, u32[]{:S(2)}) collective-permute-start(bf16[64,2048]{1,0:T(8,128)(2,1)} %get-tuple-element.293), channel_id=1, source_target_pairs={{0,1},{1,2},{2,3},{3,0},{4,5},{5,6},{6,7},{7,4},{8,9},{9,10},{10,1... | collective-permute-start | bytes 786440 | tf_op jit(solution)/shard_map/ppermute | solution.py:365
  1026.5 13.9 %collective-permute-done.45 = bf16[64,2048]{1,0:T(8,128)(2,1)S(1)} collective-permute-done((bf16[64,2048]{1,0:T(8,128)(2,1)S(1)}, bf16[64,2048]{1,0:T(8,128)(2,1)S(1)}, u32[]{:S(2)}, u32[]{:S(2)}) %collective-permute-start.45) | collective-permute-done | bytes 262176 | tf_op jit(solution)/shard_map/ppermute | solution.py:365
  1055.7 13.6 %all-to-all-done.1 = bf16[8,384,256]{2,1,0:T(8,128)(2,1)} async-done(((bf16[8,384,256]{2,1,0:T(8,128)(2,1)}), bf16[8,384,256]{2,1,0:T(8,128)(2,1)}, u32[]{:S(2)}, u32[]{:S(2)}) %all-to-all-start.1) | async-done | bytes 1572896 | tf_op jit(solution)/shard_map/all_to_all | solution.py:764
  (722 shorter events, 618.9 us)
Async XLA Ops:
  7.2 93.1 %all-gather.8.cloned.1.call-start = ((), (), s32[]{:S(2)}) async-start(), calls=%async_computation.6 | async-start | bytes 9437184 | tf_op jit(solution)/shard_map/all_gather | solution.py:523
  7.9 232.9 %all-gather.10.cloned.1.call-start = ((), (), s32[]{:S(2)}) async-start(), calls=%async_computation.7 | async-start | bytes 9437184 | tf_op jit(solution)/shard_map/all_gather | solution.py:499
  46.1 36.0 %all-to-all-start = ((bf16[8,400,256]{2,1,0:T(8,128)(2,1)}), bf16[8,400,256]{2,1,0:T(8,128)(2,1)}, u32[]{:S(2)}, u32[]{:S(2)}) async-start(bf16[8,400,256]{2,1,0:T(8,128)(2,1)} %pad_maximum_fusion.2), calls=%async_computation | async-start | bytes 3276800 | tf_op jit(solution)/shard_map/all_to_all | solution.py:518
  50.5 214.3 %all-gather.12.cloned.1.call-start = ((), (), s32[]{:S(2)}) async-start(), calls=%async_computation.8 | async-start | bytes 9437184 | tf_op jit(solution)/shard_map/all_gather | solution.py:499
  78.3 382.2 %all-gather.16.cloned.1.call-start = ((), (), s32[]{:S(2)}) async-start(), calls=%async_computation.10 | async-start | bytes 9437184 | tf_op jit(solution)/shard_map/all_gather | solution.py:499
  91.3 39.7 %collective-permute-start.4 = (bf16[8,400,256]{2,1,0:T(8,128)(2,1)}, bf16[8,400,256]{2,1,0:T(8,128)(2,1)}, u32[]{:S(2)}, u32[]{:S(2)}) collective-permute-start(bf16[8,400,256]{2,1,0:T(8,128)(2,1)} %all-to-all-done), channel_id=1, source_target_pairs={{0,1},{1,2},{2,3},{4,5},{5,6},{6,7},{8,9},{9,10},{10,11},{12,13},{... | collective-permute-start | bytes 4915208 | tf_op jit(solution)/shard_map/ppermute | solution.py:382
  93.2 37.8 %collective-permute-start.3 = (bf16[8,400,256]{2,1,0:T(8,128)(2,1)}, bf16[8,400,256]{2,1,0:T(8,128)(2,1)}, u32[]{:S(2)}, u32[]{:S(2)}) collective-permute-start(bf16[8,400,256]{2,1,0:T(8,128)(2,1)} %all-to-all-done), channel_id=1, source_target_pairs={{1,0},{2,1},{3,2},{5,4},{6,5},{7,6},{9,8},{10,9},{11,10},{13,12},{... | collective-permute-start | bytes 4915208 | tf_op jit(solution)/shard_map/ppermute | solution.py:383
  131.0 33.7 %collective-permute-start.11 = (bf16[8,400,256]{2,1,0:T(8,128)(2,1)}, bf16[8,400,256]{2,1,0:T(8,128)(2,1)}, u32[]{:S(2)}, u32[]{:S(2)}) collective-permute-start(bf16[8,400,256]{2,1,0:T(8,128)(2,1)} %collective-permute-done.4), channel_id=1, source_target_pairs={{1,2},{2,3},{5,6},{6,7},{9,10},{10,11},{13,14},{14,15},{17,18},{18... | collective-permute-start | bytes 4915208 | tf_op jit(solution)/shard_map/ppermute | solution.py:382
  135.2 34.8 %collective-permute-start.13 = (bf16[8,400,256]{2,1,0:T(8,128)(2,1)}, bf16[8,400,256]{2,1,0:T(8,128)(2,1)}, u32[]{:S(2)}, u32[]{:S(2)}) collective-permute-start(bf16[8,400,256]{2,1,0:T(8,128)(2,1)} %collective-permute-done.3), channel_id=1, source_target_pairs={{1,0},{2,1},{5,4},{6,5},{9,8},{10,9},{13,12},{14,13},{17,16},{18,1... | collective-permute-start | bytes 4915208 | tf_op jit(solution)/shard_map/ppermute | solution.py:383
  204.7 36.2 %collective-permute-start.16 = (bf16[256,2048]{1,0:T(8,128)(2,1)}, bf16[256,2048]{1,0:T(8,128)(2,1)}, u32[]{:S(2)}, u32[]{:S(2)}) collective-permute-start(bf16[256,2048]{1,0:T(8,128)(2,1)} %bitcast.56), channel_id=1, source_target_pairs={{0,1},{1,2},{2,3},{4,5},{5,6},{6,7},{8,9},{9,10},{10,11},{12,13},{... | collective-permute-start | bytes 3145736 | tf_op jit(solution)/shard_map/ppermute | solution.py:382
  206.6 40.6 %collective-permute-start.15 = (bf16[256,2048]{1,0:T(8,128)(2,1)}, bf16[256,2048]{1,0:T(8,128)(2,1)}, u32[]{:S(2)}, u32[]{:S(2)}) collective-permute-start(bf16[256,2048]{1,0:T(8,128)(2,1)} %bitcast.56), channel_id=1, source_target_pairs={{1,0},{2,1},{3,2},{5,4},{6,5},{7,6},{9,8},{10,9},{11,10},{13,12},{... | collective-permute-start | bytes 3145736 | tf_op jit(solution)/shard_map/ppermute | solution.py:383
  368.7 144.8 %all-gather.14.cloned.1.call-start = ((), (), s32[]{:S(2)}) async-start(), calls=%async_computation.9 | async-start | bytes 9437184 | tf_op jit(solution)/shard_map/all_gather | solution.py:499
  444.2 141.8 %reduce-scatter.5.cloned.1.call-start = ((), (), s32[]{:S(2)}) async-start(), calls=%async_computation.11 | async-start | bytes 10027008 | tf_op jit(solution)/shard_map/reduce_scatter | solution.py:635
  510.8 152.6 %reduce-scatter.7.cloned.1.call-start = ((), (), s32[]{:S(2)}) async-start(), calls=%async_computation.13 | async-start | bytes 10027008 | tf_op jit(solution)/shard_map/reduce_scatter | solution.py:635
  564.2 138.4 %all-gather.18.cloned.1.call-start = ((), (), s32[]{:S(2)}) async-start(), calls=%async_computation.12 | async-start | bytes 4718592 | tf_op jit(solution)/shard_map/all_gather | solution.py:665
  626.0 127.8 %all-gather.20.cloned.1.call-start = ((), (), s32[]{:S(2)}) async-start(), calls=%async_computation.15 | async-start | bytes 4718592 | tf_op jit(solution)/shard_map/all_gather | solution.py:665
  713.9 175.1 %reduce-scatter.9.cloned.1.call-start = ((), (), s32[]{:S(2)}) async-start(), calls=%async_computation.14 | async-start | bytes 18874368 | tf_op jit(solution)/shard_map/reduce_scatter | solution.py:700
  743.2 300.6 %reduce-scatter.11.cloned.1.call-start = ((), (), s32[]{:S(2)}) async-start(), calls=%async_computation.16 | async-start | bytes 7864320 | tf_op jit(solution)/shard_map/reduce_scatter | solution.py:751
  851.1 34.1 %collective-permute-start.66 = (bf16[256,2048]{1,0:T(8,128)(2,1)}, bf16[256,2048]{1,0:T(8,128)(2,1)}, u32[]{:S(2)}, u32[]{:S(2)}) collective-permute-start(bf16[256,2048]{1,0:T(8,128)(2,1)} %get-tuple-element.278), channel_id=1, source_target_pairs={{0,1},{1,2},{2,3},{4,5},{5,6},{6,7},{8,9},{9,10},{10,11},{12,13},{... | collective-permute-start | bytes 3145736 | tf_op jit(solution)/shard_map/ppermute | solution.py:401
  932.1 36.6 %collective-permute-start.56 = (bf16[128,2176]{1,0:T(8,128)(2,1)}, bf16[128,2176]{1,0:T(8,128)(2,1)}, u32[]{:S(2)}, u32[]{:S(2)}) collective-permute-start(bf16[128,2176]{1,0:T(8,128)(2,1)} %get-tuple-element.286), channel_id=1, source_target_pairs={{0,16},{4,20},{8,24},{12,28},{16,0},{20,4},{24,8},{28,12},{1,17},{... | collective-permute-start | bytes 1671176 | tf_op jit(solution)/shard_map/ppermute | solution.py:411
  933.7 35.0 %collective-permute-start.55 = (bf16[128,2176]{1,0:T(8,128)(2,1)}, bf16[128,2176]{1,0:T(8,128)(2,1)}, u32[]{:S(2)}, u32[]{:S(2)}) collective-permute-start(bf16[128,2176]{1,0:T(8,128)(2,1)} %get-tuple-element.287), channel_id=1, source_target_pairs={{0,8},{4,12},{8,0},{12,4},{16,24},{20,28},{24,16},{28,20},{1,9},{5... | collective-permute-start | bytes 1671176 | tf_op jit(solution)/shard_map/ppermute | solution.py:411
  1002.7 37.7 %collective-permute-start.45 = (bf16[64,2048]{1,0:T(8,128)(2,1)S(1)}, bf16[64,2048]{1,0:T(8,128)(2,1)S(1)}, u32[]{:S(2)}, u32[]{:S(2)}) collective-permute-start(bf16[64,2048]{1,0:T(8,128)(2,1)S(1)} %get-tuple-element.298), channel_id=1, source_target_pairs={{0,2},{1,3},{2,0},{3,1},{4,6},{5,7},{6,4},{7,5},{8,10},{9,11},{10,... | collective-permute-start | bytes 786440 | tf_op jit(solution)/shard_map/ppermute | solution.py:365
  1006.1 35.7 %collective-permute-start.44 = (bf16[64,2048]{1,0:T(8,128)(2,1)S(1)}, bf16[64,2048]{1,0:T(8,128)(2,1)S(1)}, u32[]{:S(2)}, u32[]{:S(2)}) collective-permute-start(bf16[64,2048]{1,0:T(8,128)(2,1)S(1)} %get-tuple-element.299), channel_id=1, source_target_pairs={{0,3},{1,0},{2,1},{3,2},{4,7},{5,4},{6,5},{7,6},{8,11},{9,8},{10,9... | collective-permute-start | bytes 786440 | tf_op jit(solution)/shard_map/ppermute | solution.py:365
  1010.9 38.2 %collective-permute-start.49 = (bf16[64,2048]{1,0:T(8,128)(2,1)}, bf16[64,2048]{1,0:T(8,128)(2,1)}, u32[]{:S(2)}, u32[]{:S(2)}) collective-permute-start(bf16[64,2048]{1,0:T(8,128)(2,1)} %get-tuple-element.293), channel_id=1, source_target_pairs={{0,1},{1,2},{2,3},{3,0},{4,5},{5,6},{6,7},{7,4},{8,9},{9,10},{10,1... | collective-permute-start | bytes 786440 | tf_op jit(solution)/shard_map/ppermute | solution.py:365
  (185 other events, 2625.9 us)
Sparse Core Ops, SparseCore 0:
  9.9 68.7 all-gather.7
  81.1 58.7 all-gather.9
  142.4 54.3 all-gather.11
  368.8 72.3 all-gather.15
  444.3 54.4 all-gather.13
  510.9 75.0 reduce-scatter.4
  589.6 73.7 reduce-scatter.6
  665.9 36.6 all-gather.17
  714.0 36.7 all-gather.19
  754.2 115.9 reduce-scatter.8
  889.1 109.3 reduce-scatter.10

commit v6 on v5

--- a/solution.py
+++ b/solution.py
@@ -743,11 +743,7 @@
     packed_grad = jnp.concatenate(
         [jnp.stack(query_parts, axis=0)] + [part.transpose(1, 0, 2, 3) for part in kv_part], axis=2
     )
-    both_grad = after(both_grad, done)
-    gate_up_grad = weave_rows(both_grad, hidden_units)
-    down_grad = after(down_grad, done)[:hidden_units]
-
-    packed_grad = after(packed_grad, out_rows, output_grad, gate_up_grad)
+    packed_grad = after(packed_grad, out_rows, output_grad)
     packed_grad = lax.psum_scatter(packed_grad, "expert", scatter_dimension=0, tiled=False)
 
     for u in each:
@@ -761,7 +757,12 @@
     for u in each:
         done = after(done, *mixed_parts[: u])
         done = finish_inputs(u, done)
+    both_grad = after(both_grad, done)
+    gate_up_grad = weave_rows(both_grad, hidden_units)
+    down_grad = after(down_grad, done)[:hidden_units]
+
     packed_grad = lax.all_to_all(packed_grad, "dp", split_axis=0, concat_axis=0, tiled=True)
+    arrived = packed_grad
     packed_grad = packed_grad.transpose(1, 0, 2).reshape(-1, width).astype(F32)
     query_grad = packed_grad[:query_rows]
     kv_grad = packed_grad[query_rows:].reshape(2, kv_rows, width).transpose(1, 0, 2)
@@ -781,7 +782,7 @@
     small_grad = jnp.concatenate(
         [gain_one_sum[None], gain_two_sum[None], router_one_grad, router_two_grad], axis=0
     )
-    small_grad = all_sum(all_sum(small_grad, "dp"), "expert")
+    small_grad = all_sum(after(all_sum(small_grad, "dp"), arrived), "expert")
     small_grad = lax.dynamic_index_in_dim(
         small_grad.reshape(-1, dp * planes, kv_rows), my_dp * planes + plane, axis=1, keepdims=False
     )

time: 1090 us -> 1090 us (level)
  waiting for transfers between devices: 338 us -> 358 us
  starting transfers between devices: 145 us -> 129 us
    ppermute x3, waiting for transfers between devices: 17.2 us -> 31.3 us  [reduce_planes(): lax.ppermute(send_right, 'expert', [(i, i + 1) for i in range(0, t)])]
    all_to_all x1, waiting for transfers between devices: 13.6 us -> 0.01 us  [per_device(): lax.all_to_all(packed_grad, 'dp', split_axis=0, concat_axis=0, tiled=True)]
    ppermute x30, waiting for transfers between devices: 99.9 us -> 113 us  [shift_planes(): lax.ppermute(value, 'expert', [(i, (i + amount) % planes) for i in range(...]
    unnamed x281 -> x285, local copies, waits for them, and re-layouts: 27.9 us -> 26.7 us
  transfers between devices with their start and end apart: 82 -> 82, of which waited for: 44 -> 45; matrix products, arithmetic and copies ran while one was open for 31% -> 31% of each run, Pallas kernels for 18% -> 18%
where the time goes in v6:
time: 1090 us; the launch traced here: 1080 us
  waiting for transfers between devices  358 us (33%)
  matrix products  222 us (20%)
  Pallas kernels  194 us (18%)
  starting transfers between devices  129 us (12%)
  local copies, waits for them, and re-layouts  79.2 us (7%)
  other arithmetic  77.6 us (7%)
  between operations  16.8 us (2%)
    ppermute x30, waiting for transfers between devices, shift_planes(): lax.ppermute(value, 'expert', [(i, (i + amount) % planes) for i in range(...  113 us
    pallas_call x2, Pallas kernels, mlp_experts(): pl.pallas_call(mlp_kernel, grid_spec=pltpu.PrefetchScalarGridSpec(num_sca...  101 us
    ppermute x16, waiting for transfers between devices, swap_dp(): return lax.ppermute(value, 'dp', [(i, i ^ mask) for i in range(size)])  80.5 us
    dot_general x28, matrix products, dot_f32(): return jnp.dot(left, right, preferred_element_type=F32)  55.4 us
    ppermute x6, waiting for transfers between devices, gather_planes(): lax.ppermute(left, 'expert', [(i + 1, i) for i in range(0, planes - d)])  53.8 us
    ppermute x30, starting transfers between devices, shift_planes(): lax.ppermute(value, 'expert', [(i, (i + amount) % planes) for i in range(...  45.7 us
    dot_general x2, matrix products, per_device(): jnp.einsum('rf,rd->fd', after(dhid_list[u], down_grad), b_rows_list[u], p...  41.7 us
    pallas_call x2, Pallas kernels, attn_backward(): pl.pallas_call(functools.partial(attn_backward_kernel, experts=experts, h...  38.2 us
  transfers between devices with their start and end apart: 82, of which 45 were waited for; matrix products, arithmetic and copies ran while one was open for 31% of the time, Pallas kernels for 18%

profile of v6, /device:TPU:8, one launch (start us, length us, event | category | flops | bytes accessed | tf_op | source)
XLA Modules:
  0.0 1076.4 jit_solution(6738748758363770306)
XLA Ops:
  21.8 14.9 %collective-permute-done.7 = bf16[64,2048]{1,0:T(8,128)(2,1)S(1)} collective-permute-done((bf16[64,2048]{1,0:T(8,128)(2,1)S(1)}, bf16[64,2048]{1,0:T(8,128)(2,1)S(1)}, u32[]{:S(2)}, u32[]{:S(2)}) %collective-permute-start.7) | collective-permute-done | bytes 262176 | tf_op jit(solution)/shard_map/ppermute | solution.py:365
  115.2 15.8 %collective-permute-done.3 = bf16[8,400,256]{2,1,0:T(8,128)(2,1)} collective-permute-done((bf16[8,400,256]{2,1,0:T(8,128)(2,1)}, bf16[8,400,256]{2,1,0:T(8,128)(2,1)}, u32[]{:S(2)}, u32[]{:S(2)}) %collective-permute-start.3) | collective-permute-done | bytes 1638432 | tf_op jit(solution)/shard_map/ppermute | solution.py:383
  145.6 19.2 %collective-permute-done.11 = bf16[8,400,256]{2,1,0:T(8,128)(2,1)} collective-permute-done((bf16[8,400,256]{2,1,0:T(8,128)(2,1)}, bf16[8,400,256]{2,1,0:T(8,128)(2,1)}, u32[]{:S(2)}, u32[]{:S(2)}) %collective-permute-start.11) | collective-permute-done | bytes 1638432 | tf_op jit(solution)/shard_map/ppermute | solution.py:382
  181.7 21.3 %collective-permute-done.14 = bf16[8,400,256]{2,1,0:T(8,128)(2,1)S(1)} collective-permute-done((bf16[8,400,256]{2,1,0:T(8,128)(2,1)}, bf16[8,400,256]{2,1,0:T(8,128)(2,1)S(1)}, u32[]{:S(2)}, u32[]{:S(2)}) %collective-permute-start.14) | collective-permute-done | bytes 1638432 | tf_op jit(solution)/shard_map/ppermute | solution.py:383
  220.7 12.1 %shard_map.223 = (bf16[2,2,1024,128]{3,2,1,0:T(8,128)(2,1)}, bf16[2,1024,128]{2,1,0:T(8,128)(2,1)S(1)}, bf16[2,1024,128]{2,1,0:T(8,128)(2,1)S(1)}, bf16[2,2,1024,128]{3,2,1,0:T(8,128)(2,1)}, bf16[1024,1024]{1,0:T(8,128)(2,1)}) custom-call(s32[1024,2]{1,0:T(8,128)S(1)} %copy-done.8, f32[1024,2]{1,0:T(8,128)S(1)} %exponential_divide_fusion.1.refs_1_.gates_ref, ...), custom_call_target="tpu_custom_call" | custom-call | flops 4294967296 | bytes 12582912 | tf_op jit(solution)/shard_map/pallas_call | solution.py:141
  251.7 11.7 %shard_map.224 = (bf16[2,2,1024,128]{3,2,1,0:T(8,128)(2,1)}, bf16[2,1024,128]{2,1,0:T(8,128)(2,1)S(1)}, bf16[2,1024,128]{2,1,0:T(8,128)(2,1)S(1)}, bf16[2,2,1024,128]{3,2,1,0:T(8,128)(2,1)}, bf16[1024,1024]{1,0:T(8,128)(2,1)}) custom-call(s32[1024,2]{1,0:T(8,128)S(1)} %add_select_fusion.refs_0_.routes_ref, ...), custom_call_target="tpu_custom_call" | custom-call | flops 4294967296 | bytes 12582912 | tf_op jit(solution)/shard_map/pallas_call | solution.py:141
  276.1 11.7 %collective-permute-done.20 = bf16[256,2048]{1,0:T(8,128)(2,1)S(1)} collective-permute-done((bf16[256,2048]{1,0:T(8,128)(2,1)}, bf16[256,2048]{1,0:T(8,128)(2,1)S(1)}, u32[]{:S(2)}, u32[]{:S(2)}) %collective-permute-start.20) | collective-permute-done | bytes 1048608 | tf_op jit(solution)/shard_map/ppermute | solution.py:383
  324.8 12.3 %collective-permute-done.23 = bf16[128,2048]{1,0:T(8,128)(2,1)S(1)} collective-permute-done((bf16[128,2048]{1,0:T(8,128)(2,1)}, bf16[128,2048]{1,0:T(8,128)(2,1)S(1)}, u32[]{:S(2)}, u32[]{:S(2)}) %collective-permute-start.23) | collective-permute-done | bytes 524320 | tf_op jit(solution)/shard_map/ppermute | solution.py:411
  347.0 16.7 %collective-permute-done.28 = bf16[64,2048]{1,0:T(8,128)(2,1)S(1)} collective-permute-done((bf16[64,2048]{1,0:T(8,128)(2,1)S(1)}, bf16[64,2048]{1,0:T(8,128)(2,1)S(1)}, u32[]{:S(2)}, u32[]{:S(2)}) %collective-permute-start.28) | collective-permute-done | bytes 262176 | tf_op jit(solution)/shard_map/ppermute | solution.py:365
  423.1 15.4 %collective-permute-done.34 = bf16[64,2048]{1,0:T(8,128)(2,1)S(1)} collective-permute-done((bf16[64,2048]{1,0:T(8,128)(2,1)S(1)}, bf16[64,2048]{1,0:T(8,128)(2,1)S(1)}, u32[]{:S(2)}, u32[]{:S(2)}) %collective-permute-start.34) | collective-permute-done | bytes 262176 | tf_op jit(solution)/shard_map/ppermute | solution.py:365
  458.5 50.3 %shard_map.225 = (bf16[2048,4096]{1,0:T(8,128)(2,1)}, bf16[2048,2176]{1,0:T(8,128)(2,1)}, bf16[2048,768]{1,0:T(8,128)(2,1)}, bf16[2048,1536]{1,0:T(8,128)(2,1)}) custom-call(s32[1]{0:T(128)} %bitcast.71.place_ref, bf16[2048,2048]{1,0:T(8,128)(2,1)} %all-gather.16.cloned.1.call-done.b_ref, bf16[2048,2048]{1,0:T(8,128)(2,1)} %all-gather.10.cloned.1.call-done.cot_ref, ...), custom_call_target="tpu_custom_call" | custom-call | flops 38654705664 | bytes 52428800 | tf_op jit(solution)/shard_map/pallas_call | solution.py:228
  511.4 50.5 %shard_map.226 = (bf16[2048,4096]{1,0:T(8,128)(2,1)}, bf16[2048,2176]{1,0:T(8,128)(2,1)}, bf16[2048,768]{1,0:T(8,128)(2,1)}, bf16[2048,1536]{1,0:T(8,128)(2,1)}) custom-call(s32[1]{0:T(128)} %bitcast.71.place_ref, bf16[2048,2048]{1,0:T(8,128)(2,1)} %all-gather.14.cloned.1.call-done.b_ref, ...), custom_call_target="tpu_custom_call", output_to_operand_aliasing={{0}: (7, {})} | custom-call | flops 38654705664 | bytes 52428800 | tf_op jit(solution)/shard_map/pallas_call | solution.py:228
  563.5 11.9 %fusion.223 = f32[768,2048]{1,0:T(8,128)} fusion(bf16[2048,768]{1,0:T(8,128)(2,1)} %get-tuple-element.109, bf16[2048,2048]{1,0:T(8,128)(2,1)} %all-gather.10.cloned.1.call-done.cot_ref), kind=kOutput, calls=%fused_computation.462 | convolution fusion | flops 6442450944 | bytes 17825792 | tf_op jit(solution)/shard_map/rf,rd->fd/dot_general | solution.py:640
  591.2 19.1 %fusion.224 = f32[1536,2048]{1,0:T(8,128)} fusion(bf16[2048,1536]{1,0:T(8,128)(2,1)} %get-tuple-element.110, bf16[2048,2048]{1,0:T(8,128)(2,1)} %all-gather.16.cloned.1.call-done.b_ref), kind=kOutput, calls=%fused_computation.463 | convolution fusion | flops 12884901888 | bytes 27262976 | tf_op jit(solution)/shard_map/rf,rd->fd/dot_general | solution.py:646
  625.0 13.8 %convolution_add_fusion.1 = f32[768,2048]{1,0:T(8,128)} fusion(f32[768,2048]{1,0:T(8,128)} %fusion.223, bf16[2048,768]{1,0:T(8,128)(2,1)} %get-tuple-element.115, bf16[2048,2048]{1,0:T(8,128)(2,1)} %all-gather.12.cloned.1.call-done.cot_ref), kind=kOutput, calls=%fused_computation.28 | convolution fusion | flops 6444023808 | bytes 24117248 | tf_op jit(solution)/shard_map/rf,rd->fd/dot_general | solution.py:640
  638.8 23.8 %reduce-scatter.7.cloned.1.call-done = bf16[256,2176]{1,0:T(8,128)(2,1)} async-done(((bf16[2048,2176]{1,0:T(8,128)(2,1)}), bf16[256,2176]{1,0:T(8,128)(2,1)}) %reduce-scatter.7.cloned.1.call-update) | async-done | bytes 1114128 | tf_op jit(solution)/shard_map/reduce_scatter | solution.py:635
  668.8 22.6 %convolution_add_fusion.first_ref.second_ref = f32[1536,2048]{1,0:T(8,128)} fusion(f32[1536,2048]{1,0:T(8,128)} %fusion.224, bf16[2048,1536]{1,0:T(8,128)(2,1)} %get-tuple-element.116, bf16[2048,2048]{1,0:T(8,128)(2,1)} %all-gather.14.cloned.1.call-done.b_ref), kind=kOutput, calls=%fused_computation.6 | convolution fusion | flops 12888047616 | bytes 39845888 | tf_op jit(solution)/shard_map/rf,rd->fd/dot_general | solution.py:646
  723.0 18.8 %shard_map.227 = bf16[1024,1664]{1,0:T(8,128)(2,1)} custom-call(s32[1024,2]{1,0:T(8,128)S(1)} %copy-done.9, f32[1024,2]{1,0:T(8,128)S(1)} %copy-done.1, s32[1024,1]{1,0:T(8,128)S(1)} %copy.519.refs_2_.seg_col_ref, s32[1,1024]{1,0:T(1,128)S(1)} %get-tuple-element.360.refs_3_.seg_row_ref, f32[1024,128]{1,0:T(8,128)S(1)} %copy-done.3, ...), custom_call_target="tpu_custom_call" | custom-call | flops 10737418240 | bytes 12582912 | tf_op jit(solution)/shard_map/pallas_call | solution.py:167
  777.8 19.4 %shard_map.228 = bf16[1024,1664]{1,0:T(8,128)(2,1)} custom-call(s32[1024,2]{1,0:T(8,128)S(1)} %add_select_fusion.refs_0_.routes_ref, f32[1024,2]{1,0:T(8,128)S(1)} %exponential_divide_fusion.refs_1_.gates_ref, s32[1024,1]{1,0:T(8,128)S(1)} %copy-done.7, s32[1,1024]{1,0:T(1,128)S(1)} %get-tuple-element.361.refs_3_.seg_row_ref, f32[1024,128]{1,0:T(8,128)S(1)} %copy-done.3, ...), custom_call_target="tpu_custom_call" | custom-call | flops 10737418240 | bytes 12582912 | tf_op jit(solution)/shard_map/pallas_call | solution.py:167
  823.5 18.1 %collective-permute-done.63 = bf16[256,2048]{1,0:T(8,128)(2,1)S(1)} collective-permute-done((bf16[256,2048]{1,0:T(8,128)(2,1)S(1)}, bf16[256,2048]{1,0:T(8,128)(2,1)S(1)}, u32[]{:S(2)}, u32[]{:S(2)}) %collective-permute-start.63) | collective-permute-done | bytes 1048608 | tf_op jit(solution)/shard_map/ppermute | solution.py:401
  860.4 13.2 %collective-permute-done.64 = bf16[256,2048]{1,0:T(8,128)(2,1)S(1)} collective-permute-done((bf16[256,2048]{1,0:T(8,128)(2,1)}, bf16[256,2048]{1,0:T(8,128)(2,1)S(1)}, u32[]{:S(2)}, u32[]{:S(2)}) %collective-permute-start.64) | collective-permute-done | bytes 1048608 | tf_op jit(solution)/shard_map/ppermute | solution.py:401
  910.4 12.3 %collective-permute-done.53 = bf16[128,2176]{1,0:T(8,128)(2,1)S(1)} collective-permute-done((bf16[128,2176]{1,0:T(8,128)(2,1)S(1)}, bf16[128,2176]{1,0:T(8,128)(2,1)S(1)}, u32[]{:S(2)}, u32[]{:S(2)}) %collective-permute-start.53) | collective-permute-done | bytes 557088 | tf_op jit(solution)/shard_map/ppermute | solution.py:411
  944.1 16.2 %shard_map.229 = f32[1,704,2,2048]{3,2,1,0:T(2,128)} custom-call(f32[1536,2048]{1,0:T(8,128)} %convolution_add_fusion.first_ref.second_ref, f32[1536,2048]{1,0:T(8,128)} %convolution_add_fusion.first_ref.second_ref), custom_call_target="tpu_custom_call" | custom-call | bytes 23068672 | tf_op jit(solution)/shard_map/pallas_call | solution.py:274
  1020.9 18.7 %collective-permute-done.45 = bf16[64,2048]{1,0:T(8,128)(2,1)} collective-permute-done((bf16[64,2048]{1,0:T(8,128)(2,1)}, bf16[64,2048]{1,0:T(8,128)(2,1)}, u32[]{:S(2)}, u32[]{:S(2)}) %collective-permute-start.45) | collective-permute-done | bytes 262176 | tf_op jit(solution)/shard_map/ppermute | solution.py:365
  (726 shorter events, 599.5 us)
Async XLA Ops:
  7.2 93.2 %all-gather.8.cloned.1.call-start = ((), (), s32[]{:S(2)}) async-start(), calls=%async_computation.6 | async-start | bytes 9437184 | tf_op jit(solution)/shard_map/all_gather | solution.py:523
  7.9 233.1 %all-gather.10.cloned.1.call-start = ((), (), s32[]{:S(2)}) async-start(), calls=%async_computation.7 | async-start | bytes 9437184 | tf_op jit(solution)/shard_map/all_gather | solution.py:499
  46.1 36.0 %all-to-all-start = ((bf16[8,400,256]{2,1,0:T(8,128)(2,1)}), bf16[8,400,256]{2,1,0:T(8,128)(2,1)}, u32[]{:S(2)}, u32[]{:S(2)}) async-start(bf16[8,400,256]{2,1,0:T(8,128)(2,1)} %pad_maximum_fusion.2), calls=%async_computation | async-start | bytes 3276800 | tf_op jit(solution)/shard_map/all_to_all | solution.py:518
  50.5 214.5 %all-gather.12.cloned.1.call-start = ((), (), s32[]{:S(2)}) async-start(), calls=%async_computation.8 | async-start | bytes 9437184 | tf_op jit(solution)/shard_map/all_gather | solution.py:499
  78.3 380.2 %all-gather.16.cloned.1.call-start = ((), (), s32[]{:S(2)}) async-start(), calls=%async_computation.10 | async-start | bytes 9437184 | tf_op jit(solution)/shard_map/all_gather | solution.py:499
  91.3 39.7 %collective-permute-start.4 = (bf16[8,400,256]{2,1,0:T(8,128)(2,1)}, bf16[8,400,256]{2,1,0:T(8,128)(2,1)}, u32[]{:S(2)}, u32[]{:S(2)}) collective-permute-start(bf16[8,400,256]{2,1,0:T(8,128)(2,1)} %all-to-all-done), channel_id=1, source_target_pairs={{0,1},{1,2},{2,3},{4,5},{5,6},{6,7},{8,9},{9,10},{10,11},{12,13},{... | collective-permute-start | bytes 4915208 | tf_op jit(solution)/shard_map/ppermute | solution.py:382
  93.3 37.8 %collective-permute-start.3 = (bf16[8,400,256]{2,1,0:T(8,128)(2,1)}, bf16[8,400,256]{2,1,0:T(8,128)(2,1)}, u32[]{:S(2)}, u32[]{:S(2)}) collective-permute-start(bf16[8,400,256]{2,1,0:T(8,128)(2,1)} %all-to-all-done), channel_id=1, source_target_pairs={{1,0},{2,1},{3,2},{5,4},{6,5},{7,6},{9,8},{10,9},{11,10},{13,12},{... | collective-permute-start | bytes 4915208 | tf_op jit(solution)/shard_map/ppermute | solution.py:383
  131.0 33.7 %collective-permute-start.11 = (bf16[8,400,256]{2,1,0:T(8,128)(2,1)}, bf16[8,400,256]{2,1,0:T(8,128)(2,1)}, u32[]{:S(2)}, u32[]{:S(2)}) collective-permute-start(bf16[8,400,256]{2,1,0:T(8,128)(2,1)} %collective-permute-done.4), channel_id=1, source_target_pairs={{1,2},{2,3},{5,6},{6,7},{9,10},{10,11},{13,14},{14,15},{17,18},{18... | collective-permute-start | bytes 4915208 | tf_op jit(solution)/shard_map/ppermute | solution.py:382
  135.3 34.8 %collective-permute-start.13 = (bf16[8,400,256]{2,1,0:T(8,128)(2,1)}, bf16[8,400,256]{2,1,0:T(8,128)(2,1)}, u32[]{:S(2)}, u32[]{:S(2)}) collective-permute-start(bf16[8,400,256]{2,1,0:T(8,128)(2,1)} %collective-permute-done.3), channel_id=1, source_target_pairs={{1,0},{2,1},{5,4},{6,5},{9,8},{10,9},{13,12},{14,13},{17,16},{18,1... | collective-permute-start | bytes 4915208 | tf_op jit(solution)/shard_map/ppermute | solution.py:383
  204.7 36.3 %collective-permute-start.16 = (bf16[256,2048]{1,0:T(8,128)(2,1)}, bf16[256,2048]{1,0:T(8,128)(2,1)}, u32[]{:S(2)}, u32[]{:S(2)}) collective-permute-start(bf16[256,2048]{1,0:T(8,128)(2,1)} %bitcast.56), channel_id=1, source_target_pairs={{0,1},{1,2},{2,3},{4,5},{5,6},{6,7},{8,9},{9,10},{10,11},{12,13},{... | collective-permute-start | bytes 3145736 | tf_op jit(solution)/shard_map/ppermute | solution.py:382
  206.7 40.7 %collective-permute-start.15 = (bf16[256,2048]{1,0:T(8,128)(2,1)}, bf16[256,2048]{1,0:T(8,128)(2,1)}, u32[]{:S(2)}, u32[]{:S(2)}) collective-permute-start(bf16[256,2048]{1,0:T(8,128)(2,1)} %bitcast.56), channel_id=1, source_target_pairs={{1,0},{2,1},{3,2},{5,4},{6,5},{7,6},{9,8},{10,9},{11,10},{13,12},{... | collective-permute-start | bytes 3145736 | tf_op jit(solution)/shard_map/ppermute | solution.py:383
  368.0 143.5 %all-gather.14.cloned.1.call-start = ((), (), s32[]{:S(2)}) async-start(), calls=%async_computation.9 | async-start | bytes 9437184 | tf_op jit(solution)/shard_map/all_gather | solution.py:499
  444.1 141.0 %reduce-scatter.5.cloned.1.call-start = ((), (), s32[]{:S(2)}) async-start(), calls=%async_computation.11 | async-start | bytes 10027008 | tf_op jit(solution)/shard_map/reduce_scatter | solution.py:635
  508.7 153.8 %reduce-scatter.7.cloned.1.call-start = ((), (), s32[]{:S(2)}) async-start(), calls=%async_computation.13 | async-start | bytes 10027008 | tf_op jit(solution)/shard_map/reduce_scatter | solution.py:635
  562.0 139.8 %all-gather.18.cloned.1.call-start = ((), (), s32[]{:S(2)}) async-start(), calls=%async_computation.12 | async-start | bytes 4718592 | tf_op jit(solution)/shard_map/all_gather | solution.py:665
  623.4 128.3 %all-gather.20.cloned.1.call-start = ((), (), s32[]{:S(2)}) async-start(), calls=%async_computation.15 | async-start | bytes 4718592 | tf_op jit(solution)/shard_map/all_gather | solution.py:665
  712.5 166.4 %reduce-scatter.9.cloned.1.call-start = ((), (), s32[]{:S(2)}) async-start(), calls=%async_computation.14 | async-start | bytes 18874368 | tf_op jit(solution)/shard_map/reduce_scatter | solution.py:700
  741.8 272.9 %reduce-scatter.11.cloned.1.call-start = ((), (), s32[]{:S(2)}) async-start(), calls=%async_computation.16 | async-start | bytes 7864320 | tf_op jit(solution)/shard_map/reduce_scatter | solution.py:747
  897.9 36.4 %collective-permute-start.54 = (bf16[4,128,2176]{2,1,0:T(8,128)(2,1)}, bf16[4,128,2176]{2,1,0:T(8,128)(2,1)}, u32[]{:S(2)}, u32[]{:S(2)}) collective-permute-start(bf16[4,128,2176]{2,1,0:T(8,128)(2,1)} %convolution_convert_fusion), channel_id=1, source_target_pairs={{0,4},{4,0},{8,12},{12,8},{16,20},{20,16},{24,28},{28,24},{1,5},{5... | collective-permute-start | bytes 6684680 | tf_op jit(solution)/shard_map/ppermute | solution.py:411
  1004.6 35.0 %collective-permute-start.45 = (bf16[64,2048]{1,0:T(8,128)(2,1)}, bf16[64,2048]{1,0:T(8,128)(2,1)}, u32[]{:S(2)}, u32[]{:S(2)}) collective-permute-start(bf16[64,2048]{1,0:T(8,128)(2,1)} %get-tuple-element.300), channel_id=1, source_target_pairs={{0,2},{1,3},{2,0},{3,1},{4,6},{5,7},{6,4},{7,5},{8,10},{9,11},{10,... | collective-permute-start | bytes 786440 | tf_op jit(solution)/shard_map/ppermute | solution.py:365
  1008.8 33.9 %collective-permute-start.44 = (bf16[64,2048]{1,0:T(8,128)(2,1)}, bf16[64,2048]{1,0:T(8,128)(2,1)}, u32[]{:S(2)}, u32[]{:S(2)}) collective-permute-start(bf16[64,2048]{1,0:T(8,128)(2,1)} %get-tuple-element.301), channel_id=1, source_target_pairs={{0,3},{1,0},{2,1},{3,2},{4,7},{5,4},{6,5},{7,6},{8,11},{9,8},{10,9... | collective-permute-start | bytes 786440 | tf_op jit(solution)/shard_map/ppermute | solution.py:365
  1010.9 34.5 %collective-permute-start.49 = (bf16[64,2048]{1,0:T(8,128)(2,1)}, bf16[64,2048]{1,0:T(8,128)(2,1)}, u32[]{:S(2)}, u32[]{:S(2)}) collective-permute-start(bf16[64,2048]{1,0:T(8,128)(2,1)} %get-tuple-element.295), channel_id=1, source_target_pairs={{0,1},{1,2},{2,3},{3,0},{4,5},{5,6},{6,7},{7,4},{8,9},{9,10},{10,1... | collective-permute-start | bytes 786440 | tf_op jit(solution)/shard_map/ppermute | solution.py:365
  1012.9 36.4 %collective-permute-start.48 = (bf16[64,2048]{1,0:T(8,128)(2,1)}, bf16[64,2048]{1,0:T(8,128)(2,1)}, u32[]{:S(2)}, u32[]{:S(2)}) collective-permute-start(bf16[64,2048]{1,0:T(8,128)(2,1)} %get-tuple-element.296), channel_id=1, source_target_pairs={{0,2},{1,3},{2,0},{3,1},{4,6},{5,7},{6,4},{7,5},{8,10},{9,11},{10,... | collective-permute-start | bytes 786440 | tf_op jit(solution)/shard_map/ppermute | solution.py:365
  1014.7 39.8 %all-to-all-start.1 = ((bf16[8,384,256]{2,1,0:T(8,128)(2,1)}), bf16[8,384,256]{2,1,0:T(8,128)(2,1)S(1)}, u32[]{:S(2)}, u32[]{:S(2)}) async-start(bf16[8,384,256]{2,1,0:T(8,128)(2,1)} %bitcast.576), calls=%async_computation.5 | async-start | bytes 3145728 | tf_op jit(solution)/shard_map/all_to_all | solution.py:764
  (187 other events, 3505.0 us)
Sparse Core Ops, SparseCore 0:
  9.9 68.7 all-gather.7
  81.1 58.7 all-gather.9
  142.4 54.3 all-gather.11
  368.1 70.5 all-gather.15
  444.2 55.4 all-gather.13
  508.9 76.2 reduce-scatter.4
  588.7 73.7 reduce-scatter.6
  665.0 36.6 all-gather.17
  712.6 36.7 all-gather.19
  752.8 115.9 reduce-scatter.8
  879.1 109.6 reduce-scatter.10

commit v7 on v6

--- a/solution.py
+++ b/solution.py
@@ -762,7 +762,6 @@
     down_grad = after(down_grad, done)[:hidden_units]
 
     packed_grad = lax.all_to_all(packed_grad, "dp", split_axis=0, concat_axis=0, tiled=True)
-    arrived = packed_grad
     packed_grad = packed_grad.transpose(1, 0, 2).reshape(-1, width).astype(F32)
     query_grad = packed_grad[:query_rows]
     kv_grad = packed_grad[query_rows:].reshape(2, kv_rows, width).transpose(1, 0, 2)
@@ -782,7 +781,7 @@
     small_grad = jnp.concatenate(
         [gain_one_sum[None], gain_two_sum[None], router_one_grad, router_two_grad], axis=0
     )
-    small_grad = all_sum(after(all_sum(small_grad, "dp"), arrived), "expert")
+    small_grad = all_sum(all_sum(small_grad, "dp"), "expert")
     small_grad = lax.dynamic_index_in_dim(
         small_grad.reshape(-1, dp * planes, kv_rows), my_dp * planes + plane, axis=1, keepdims=False
     )

time: 1090 us -> 1100 us (level)
  starting transfers between devices: 129 us -> 146 us
    all_to_all x1, waiting for transfers between devices: 0.01 us -> 13.6 us  [per_device(): lax.all_to_all(packed_grad, 'dp', split_axis=0, concat_axis=0, tiled=True)]
    ppermute x30, waiting for transfers between devices: 113 us -> 100 us  [shift_planes(): lax.ppermute(value, 'expert', [(i, (i + amount) % planes) for i in range(...]
    ppermute x30, starting transfers between devices: 45.7 us -> 58.1 us  [shift_planes(): lax.ppermute(value, 'expert', [(i, (i + amount) % planes) for i in range(...]
    unnamed x285 -> x275, local copies, waits for them, and re-layouts: 26.7 us -> 27.6 us
  transfers between devices with their start and end apart: 82 -> 82, of which waited for: 45 -> 45; matrix products, arithmetic and copies ran while one was open for 31% -> 30% of each run, Pallas kernels for 18% -> 18%
where the time goes in v7:
time: 1100 us; the launch traced here: 1090 us
  waiting for transfers between devices  352 us (32%)
  matrix products  220 us (20%)
  Pallas kernels  194 us (18%)
  starting transfers between devices  146 us (13%)
  local copies, waits for them, and re-layouts  81.7 us (7%)
  other arithmetic  79.6 us (7%)
  between operations  16.8 us (2%)
    pallas_call x2, Pallas kernels, mlp_experts(): pl.pallas_call(mlp_kernel, grid_spec=pltpu.PrefetchScalarGridSpec(num_sca...  101 us
    ppermute x30, waiting for transfers between devices, shift_planes(): lax.ppermute(value, 'expert', [(i, (i + amount) % planes) for i in range(...  100 us
    ppermute x16, waiting for transfers between devices, swap_dp(): return lax.ppermute(value, 'dp', [(i, i ^ mask) for i in range(size)])  72.7 us
    ppermute x30, starting transfers between devices, shift_planes(): lax.ppermute(value, 'expert', [(i, (i + amount) % planes) for i in range(...  58.1 us
    dot_general x28, matrix products, dot_f32(): return jnp.dot(left, right, preferred_element_type=F32)  55.3 us
    ppermute x6, waiting for transfers between devices, gather_planes(): lax.ppermute(left, 'expert', [(i + 1, i) for i in range(0, planes - d)])  53.9 us
    dot_general x2, matrix products, per_device(): jnp.einsum('rf,rd->fd', after(dhid_list[u], down_grad), b_rows_list[u], p...  41.6 us
    pallas_call x2, Pallas kernels, attn_backward(): pl.pallas_call(functools.partial(attn_backward_kernel, experts=experts, h...  38.2 us
  transfers between devices with their start and end apart: 82, of which 45 were waited for; matrix products, arithmetic and copies ran while one was open for 30% of the time, Pallas kernels for 18%

profile of v7, /device:TPU:8, one launch (start us, length us, event | category | flops | bytes accessed | tf_op | source)
XLA Modules:
  0.0 1090.1 jit_solution(5069324440802943324)
XLA Ops:
  21.8 14.9 %collective-permute-done.7 = bf16[64,2048]{1,0:T(8,128)(2,1)S(1)} collective-permute-done((bf16[64,2048]{1,0:T(8,128)(2,1)S(1)}, bf16[64,2048]{1,0:T(8,128)(2,1)S(1)}, u32[]{:S(2)}, u32[]{:S(2)}) %collective-permute-start.7) | collective-permute-done | bytes 262176 | tf_op jit(solution)/shard_map/ppermute | solution.py:365
  115.1 15.9 %collective-permute-done.3 = bf16[8,400,256]{2,1,0:T(8,128)(2,1)} collective-permute-done((bf16[8,400,256]{2,1,0:T(8,128)(2,1)}, bf16[8,400,256]{2,1,0:T(8,128)(2,1)}, u32[]{:S(2)}, u32[]{:S(2)}) %collective-permute-start.3) | collective-permute-done | bytes 1638432 | tf_op jit(solution)/shard_map/ppermute | solution.py:383
  145.5 19.2 %collective-permute-done.11 = bf16[8,400,256]{2,1,0:T(8,128)(2,1)} collective-permute-done((bf16[8,400,256]{2,1,0:T(8,128)(2,1)}, bf16[8,400,256]{2,1,0:T(8,128)(2,1)}, u32[]{:S(2)}, u32[]{:S(2)}) %collective-permute-start.11) | collective-permute-done | bytes 1638432 | tf_op jit(solution)/shard_map/ppermute | solution.py:382
  181.7 21.3 %collective-permute-done.14 = bf16[8,400,256]{2,1,0:T(8,128)(2,1)S(1)} collective-permute-done((bf16[8,400,256]{2,1,0:T(8,128)(2,1)}, bf16[8,400,256]{2,1,0:T(8,128)(2,1)S(1)}, u32[]{:S(2)}, u32[]{:S(2)}) %collective-permute-start.14) | collective-permute-done | bytes 1638432 | tf_op jit(solution)/shard_map/ppermute | solution.py:383
  220.6 12.1 %shard_map.223 = (bf16[2,2,1024,128]{3,2,1,0:T(8,128)(2,1)}, bf16[2,1024,128]{2,1,0:T(8,128)(2,1)S(1)}, bf16[2,1024,128]{2,1,0:T(8,128)(2,1)S(1)}, bf16[2,2,1024,128]{3,2,1,0:T(8,128)(2,1)}, bf16[1024,1024]{1,0:T(8,128)(2,1)}) custom-call(s32[1024,2]{1,0:T(8,128)S(1)} %copy-done.8, f32[1024,2]{1,0:T(8,128)S(1)} %exponential_divide_fusion.1.refs_1_.gates_ref, ...), custom_call_target="tpu_custom_call" | custom-call | flops 4294967296 | bytes 12582912 | tf_op jit(solution)/shard_map/pallas_call | solution.py:141
  251.6 11.7 %shard_map.224 = (bf16[2,2,1024,128]{3,2,1,0:T(8,128)(2,1)}, bf16[2,1024,128]{2,1,0:T(8,128)(2,1)S(1)}, bf16[2,1024,128]{2,1,0:T(8,128)(2,1)S(1)}, bf16[2,2,1024,128]{3,2,1,0:T(8,128)(2,1)}, bf16[1024,1024]{1,0:T(8,128)(2,1)}) custom-call(s32[1024,2]{1,0:T(8,128)S(1)} %add_select_fusion.refs_0_.routes_ref, ...), custom_call_target="tpu_custom_call" | custom-call | flops 4294967296 | bytes 12582912 | tf_op jit(solution)/shard_map/pallas_call | solution.py:141
  276.0 11.8 %collective-permute-done.20 = bf16[256,2048]{1,0:T(8,128)(2,1)S(1)} collective-permute-done((bf16[256,2048]{1,0:T(8,128)(2,1)}, bf16[256,2048]{1,0:T(8,128)(2,1)S(1)}, u32[]{:S(2)}, u32[]{:S(2)}) %collective-permute-start.20) | collective-permute-done | bytes 1048608 | tf_op jit(solution)/shard_map/ppermute | solution.py:383
  324.8 12.3 %collective-permute-done.23 = bf16[128,2048]{1,0:T(8,128)(2,1)S(1)} collective-permute-done((bf16[128,2048]{1,0:T(8,128)(2,1)}, bf16[128,2048]{1,0:T(8,128)(2,1)S(1)}, u32[]{:S(2)}, u32[]{:S(2)}) %collective-permute-start.23) | collective-permute-done | bytes 524320 | tf_op jit(solution)/shard_map/ppermute | solution.py:411
  346.9 16.7 %collective-permute-done.28 = bf16[64,2048]{1,0:T(8,128)(2,1)S(1)} collective-permute-done((bf16[64,2048]{1,0:T(8,128)(2,1)S(1)}, bf16[64,2048]{1,0:T(8,128)(2,1)S(1)}, u32[]{:S(2)}, u32[]{:S(2)}) %collective-permute-start.28) | collective-permute-done | bytes 262176 | tf_op jit(solution)/shard_map/ppermute | solution.py:365
  422.9 15.4 %collective-permute-done.34 = bf16[64,2048]{1,0:T(8,128)(2,1)S(1)} collective-permute-done((bf16[64,2048]{1,0:T(8,128)(2,1)S(1)}, bf16[64,2048]{1,0:T(8,128)(2,1)S(1)}, u32[]{:S(2)}, u32[]{:S(2)}) %collective-permute-start.34) | collective-permute-done | bytes 262176 | tf_op jit(solution)/shard_map/ppermute | solution.py:365
  458.4 50.3 %shard_map.225 = (bf16[2048,4096]{1,0:T(8,128)(2,1)}, bf16[2048,2176]{1,0:T(8,128)(2,1)}, bf16[2048,768]{1,0:T(8,128)(2,1)}, bf16[2048,1536]{1,0:T(8,128)(2,1)}) custom-call(s32[1]{0:T(128)} %bitcast.71.place_ref, bf16[2048,2048]{1,0:T(8,128)(2,1)} %all-gather.16.cloned.1.call-done.b_ref, bf16[2048,2048]{1,0:T(8,128)(2,1)} %all-gather.10.cloned.1.call-done.cot_ref, ...), custom_call_target="tpu_custom_call" | custom-call | flops 38654705664 | bytes 52428800 | tf_op jit(solution)/shard_map/pallas_call | solution.py:228
  511.4 50.4 %shard_map.226 = (bf16[2048,4096]{1,0:T(8,128)(2,1)}, bf16[2048,2176]{1,0:T(8,128)(2,1)}, bf16[2048,768]{1,0:T(8,128)(2,1)}, bf16[2048,1536]{1,0:T(8,128)(2,1)}) custom-call(s32[1]{0:T(128)} %bitcast.71.place_ref, bf16[2048,2048]{1,0:T(8,128)(2,1)} %all-gather.14.cloned.1.call-done.b_ref, ...), custom_call_target="tpu_custom_call", output_to_operand_aliasing={{0}: (7, {})} | custom-call | flops 38654705664 | bytes 52428800 | tf_op jit(solution)/shard_map/pallas_call | solution.py:228
  563.3 11.8 %fusion.223 = f32[768,2048]{1,0:T(8,128)} fusion(bf16[2048,768]{1,0:T(8,128)(2,1)} %get-tuple-element.108, bf16[2048,2048]{1,0:T(8,128)(2,1)} %all-gather.10.cloned.1.call-done.cot_ref), kind=kOutput, calls=%fused_computation.462 | convolution fusion | flops 6442450944 | bytes 17825792 | tf_op jit(solution)/shard_map/rf,rd->fd/dot_general | solution.py:640
  591.0 19.1 %fusion.224 = f32[1536,2048]{1,0:T(8,128)} fusion(bf16[2048,1536]{1,0:T(8,128)(2,1)} %get-tuple-element.109, bf16[2048,2048]{1,0:T(8,128)(2,1)} %all-gather.16.cloned.1.call-done.b_ref), kind=kOutput, calls=%fused_computation.463 | convolution fusion | flops 12884901888 | bytes 27262976 | tf_op jit(solution)/shard_map/rf,rd->fd/dot_general | solution.py:646
  624.9 13.8 %convolution_add_fusion.1 = f32[768,2048]{1,0:T(8,128)} fusion(f32[768,2048]{1,0:T(8,128)} %fusion.223, bf16[2048,768]{1,0:T(8,128)(2,1)} %get-tuple-element.114, bf16[2048,2048]{1,0:T(8,128)(2,1)} %all-gather.12.cloned.1.call-done.cot_ref), kind=kOutput, calls=%fused_computation.28 | convolution fusion | flops 6444023808 | bytes 24117248 | tf_op jit(solution)/shard_map/rf,rd->fd/dot_general | solution.py:640
  638.7 23.7 %reduce-scatter.7.cloned.1.call-done = bf16[256,2176]{1,0:T(8,128)(2,1)} async-done(((bf16[2048,2176]{1,0:T(8,128)(2,1)}), bf16[256,2176]{1,0:T(8,128)(2,1)}) %reduce-scatter.7.cloned.1.call-update) | async-done | bytes 1114128 | tf_op jit(solution)/shard_map/reduce_scatter | solution.py:635
  668.7 22.5 %convolution_add_fusion.first_ref.second_ref = f32[1536,2048]{1,0:T(8,128)} fusion(f32[1536,2048]{1,0:T(8,128)} %fusion.224, bf16[2048,1536]{1,0:T(8,128)(2,1)} %get-tuple-element.115, bf16[2048,2048]{1,0:T(8,128)(2,1)} %all-gather.14.cloned.1.call-done.b_ref), kind=kOutput, calls=%fused_computation.6 | convolution fusion | flops 12888047616 | bytes 39845888 | tf_op jit(solution)/shard_map/rf,rd->fd/dot_general | solution.py:646
  722.3 18.8 %shard_map.227 = bf16[1024,1664]{1,0:T(8,128)(2,1)} custom-call(s32[1024,2]{1,0:T(8,128)S(1)} %copy-done.9, f32[1024,2]{1,0:T(8,128)S(1)} %copy-done.1, s32[1024,1]{1,0:T(8,128)S(1)} %copy.519.refs_2_.seg_col_ref, s32[1,1024]{1,0:T(1,128)S(1)} %get-tuple-element.358.refs_3_.seg_row_ref, f32[1024,128]{1,0:T(8,128)S(1)} %copy-done.3, ...), custom_call_target="tpu_custom_call" | custom-call | flops 10737418240 | bytes 12582912 | tf_op jit(solution)/shard_map/pallas_call | solution.py:167
  777.0 19.5 %shard_map.228 = bf16[1024,1664]{1,0:T(8,128)(2,1)} custom-call(s32[1024,2]{1,0:T(8,128)S(1)} %add_select_fusion.refs_0_.routes_ref, f32[1024,2]{1,0:T(8,128)S(1)} %exponential_divide_fusion.refs_1_.gates_ref, s32[1024,1]{1,0:T(8,128)S(1)} %copy-done.7, s32[1,1024]{1,0:T(1,128)S(1)} %get-tuple-element.359.refs_3_.seg_row_ref, f32[1024,128]{1,0:T(8,128)S(1)} %copy-done.3, ...), custom_call_target="tpu_custom_call" | custom-call | flops 10737418240 | bytes 12582912 | tf_op jit(solution)/shard_map/pallas_call | solution.py:167
  822.8 18.1 %collective-permute-done.65 = bf16[256,2048]{1,0:T(8,128)(2,1)S(1)} collective-permute-done((bf16[256,2048]{1,0:T(8,128)(2,1)S(1)}, bf16[256,2048]{1,0:T(8,128)(2,1)S(1)}, u32[]{:S(2)}, u32[]{:S(2)}) %collective-permute-start.65) | collective-permute-done | bytes 1048608 | tf_op jit(solution)/shard_map/ppermute | solution.py:401
  859.6 13.2 %collective-permute-done.66 = bf16[256,2048]{1,0:T(8,128)(2,1)S(1)} collective-permute-done((bf16[256,2048]{1,0:T(8,128)(2,1)}, bf16[256,2048]{1,0:T(8,128)(2,1)S(1)}, u32[]{:S(2)}, u32[]{:S(2)}) %collective-permute-start.66) | collective-permute-done | bytes 1048608 | tf_op jit(solution)/shard_map/ppermute | solution.py:401
  972.5 16.2 %shard_map.229 = f32[1,704,2,2048]{3,2,1,0:T(2,128)} custom-call(f32[1536,2048]{1,0:T(8,128)} %convolution_add_fusion.first_ref.second_ref, f32[1536,2048]{1,0:T(8,128)} %convolution_add_fusion.first_ref.second_ref), custom_call_target="tpu_custom_call" | custom-call | bytes 23068672 | tf_op jit(solution)/shard_map/pallas_call | solution.py:274
  1032.2 12.9 %collective-permute-done.45 = bf16[64,2048]{1,0:T(8,128)(2,1)} collective-permute-done((bf16[64,2048]{1,0:T(8,128)(2,1)S(1)}, bf16[64,2048]{1,0:T(8,128)(2,1)}, u32[]{:S(2)}, u32[]{:S(2)}) %collective-permute-start.45) | collective-permute-done | bytes 262176 | tf_op jit(solution)/shard_map/ppermute | solution.py:365
  1061.0 13.6 %all-to-all-done.1 = bf16[8,384,256]{2,1,0:T(8,128)(2,1)} async-done(((bf16[8,384,256]{2,1,0:T(8,128)(2,1)}), bf16[8,384,256]{2,1,0:T(8,128)(2,1)}, u32[]{:S(2)}, u32[]{:S(2)}) %all-to-all-start.1) | async-done | bytes 1572896 | tf_op jit(solution)/shard_map/all_to_all | solution.py:764
  (716 shorter events, 618.3 us)
Async XLA Ops:
  7.2 93.2 %all-gather.8.cloned.1.call-start = ((), (), s32[]{:S(2)}) async-start(), calls=%async_computation.6 | async-start | bytes 9437184 | tf_op jit(solution)/shard_map/all_gather | solution.py:523
  7.9 233.0 %all-gather.10.cloned.1.call-start = ((), (), s32[]{:S(2)}) async-start(), calls=%async_computation.7 | async-start | bytes 9437184 | tf_op jit(solution)/shard_map/all_gather | solution.py:499
  46.1 36.0 %all-to-all-start = ((bf16[8,400,256]{2,1,0:T(8,128)(2,1)}), bf16[8,400,256]{2,1,0:T(8,128)(2,1)}, u32[]{:S(2)}, u32[]{:S(2)}) async-start(bf16[8,400,256]{2,1,0:T(8,128)(2,1)} %pad_maximum_fusion.2), calls=%async_computation | async-start | bytes 3276800 | tf_op jit(solution)/shard_map/all_to_all | solution.py:518
  50.5 214.4 %all-gather.12.cloned.1.call-start = ((), (), s32[]{:S(2)}) async-start(), calls=%async_computation.8 | async-start | bytes 9437184 | tf_op jit(solution)/shard_map/all_gather | solution.py:499
  78.3 380.1 %all-gather.16.cloned.1.call-start = ((), (), s32[]{:S(2)}) async-start(), calls=%async_computation.10 | async-start | bytes 9437184 | tf_op jit(solution)/shard_map/all_gather | solution.py:499
  91.3 39.7 %collective-permute-start.4 = (bf16[8,400,256]{2,1,0:T(8,128)(2,1)}, bf16[8,400,256]{2,1,0:T(8,128)(2,1)}, u32[]{:S(2)}, u32[]{:S(2)}) collective-permute-start(bf16[8,400,256]{2,1,0:T(8,128)(2,1)} %all-to-all-done), channel_id=1, source_target_pairs={{0,1},{1,2},{2,3},{4,5},{5,6},{6,7},{8,9},{9,10},{10,11},{12,13},{... | collective-permute-start | bytes 4915208 | tf_op jit(solution)/shard_map/ppermute | solution.py:382
  93.2 37.7 %collective-permute-start.3 = (bf16[8,400,256]{2,1,0:T(8,128)(2,1)}, bf16[8,400,256]{2,1,0:T(8,128)(2,1)}, u32[]{:S(2)}, u32[]{:S(2)}) collective-permute-start(bf16[8,400,256]{2,1,0:T(8,128)(2,1)} %all-to-all-done), channel_id=1, source_target_pairs={{1,0},{2,1},{3,2},{5,4},{6,5},{7,6},{9,8},{10,9},{11,10},{13,12},{... | collective-permute-start | bytes 4915208 | tf_op jit(solution)/shard_map/ppermute | solution.py:383
  131.0 33.7 %collective-permute-start.11 = (bf16[8,400,256]{2,1,0:T(8,128)(2,1)}, bf16[8,400,256]{2,1,0:T(8,128)(2,1)}, u32[]{:S(2)}, u32[]{:S(2)}) collective-permute-start(bf16[8,400,256]{2,1,0:T(8,128)(2,1)} %collective-permute-done.4), channel_id=1, source_target_pairs={{1,2},{2,3},{5,6},{6,7},{9,10},{10,11},{13,14},{14,15},{17,18},{18... | collective-permute-start | bytes 4915208 | tf_op jit(solution)/shard_map/ppermute | solution.py:382
  135.3 34.8 %collective-permute-start.13 = (bf16[8,400,256]{2,1,0:T(8,128)(2,1)}, bf16[8,400,256]{2,1,0:T(8,128)(2,1)}, u32[]{:S(2)}, u32[]{:S(2)}) collective-permute-start(bf16[8,400,256]{2,1,0:T(8,128)(2,1)} %collective-permute-done.3), channel_id=1, source_target_pairs={{1,0},{2,1},{5,4},{6,5},{9,8},{10,9},{13,12},{14,13},{17,16},{18,1... | collective-permute-start | bytes 4915208 | tf_op jit(solution)/shard_map/ppermute | solution.py:383
  170.1 32.9 %collective-permute-start.14 = (bf16[8,400,256]{2,1,0:T(8,128)(2,1)}, bf16[8,400,256]{2,1,0:T(8,128)(2,1)S(1)}, u32[]{:S(2)}, u32[]{:S(2)}) collective-permute-start(bf16[8,400,256]{2,1,0:T(8,128)(2,1)} %collective-permute-done.13), channel_id=1, source_target_pairs={{1,0},{5,4},{9,8},{13,12},{17,16},{21,20},{25,24},{29,28}} | collective-permute-start | bytes 4915208 | tf_op jit(solution)/shard_map/ppermute | solution.py:383
  204.7 36.3 %collective-permute-start.16 = (bf16[256,2048]{1,0:T(8,128)(2,1)}, bf16[256,2048]{1,0:T(8,128)(2,1)}, u32[]{:S(2)}, u32[]{:S(2)}) collective-permute-start(bf16[256,2048]{1,0:T(8,128)(2,1)} %bitcast.56), channel_id=1, source_target_pairs={{0,1},{1,2},{2,3},{4,5},{5,6},{6,7},{8,9},{9,10},{10,11},{12,13},{... | collective-permute-start | bytes 3145736 | tf_op jit(solution)/shard_map/ppermute | solution.py:382
  206.6 40.7 %collective-permute-start.15 = (bf16[256,2048]{1,0:T(8,128)(2,1)}, bf16[256,2048]{1,0:T(8,128)(2,1)}, u32[]{:S(2)}, u32[]{:S(2)}) collective-permute-start(bf16[256,2048]{1,0:T(8,128)(2,1)} %bitcast.56), channel_id=1, source_target_pairs={{1,0},{2,1},{3,2},{5,4},{6,5},{7,6},{9,8},{10,9},{11,10},{13,12},{... | collective-permute-start | bytes 3145736 | tf_op jit(solution)/shard_map/ppermute | solution.py:383
  367.9 143.5 %all-gather.14.cloned.1.call-start = ((), (), s32[]{:S(2)}) async-start(), calls=%async_computation.9 | async-start | bytes 9437184 | tf_op jit(solution)/shard_map/all_gather | solution.py:499
  444.1 140.9 %reduce-scatter.5.cloned.1.call-start = ((), (), s32[]{:S(2)}) async-start(), calls=%async_computation.11 | async-start | bytes 10027008 | tf_op jit(solution)/shard_map/reduce_scatter | solution.py:635
  508.7 153.7 %reduce-scatter.7.cloned.1.call-start = ((), (), s32[]{:S(2)}) async-start(), calls=%async_computation.13 | async-start | bytes 10027008 | tf_op jit(solution)/shard_map/reduce_scatter | solution.py:635
  561.8 139.8 %all-gather.18.cloned.1.call-start = ((), (), s32[]{:S(2)}) async-start(), calls=%async_computation.12 | async-start | bytes 4718592 | tf_op jit(solution)/shard_map/all_gather | solution.py:665
  623.3 127.6 %all-gather.20.cloned.1.call-start = ((), (), s32[]{:S(2)}) async-start(), calls=%async_computation.15 | async-start | bytes 4718592 | tf_op jit(solution)/shard_map/all_gather | solution.py:665
  711.8 166.2 %reduce-scatter.9.cloned.1.call-start = ((), (), s32[]{:S(2)}) async-start(), calls=%async_computation.14 | async-start | bytes 18874368 | tf_op jit(solution)/shard_map/reduce_scatter | solution.py:700
  741.1 307.8 %reduce-scatter.11.cloned.1.call-start = ((), (), s32[]{:S(2)}) async-start(), calls=%async_computation.16 | async-start | bytes 7864320 | tf_op jit(solution)/shard_map/reduce_scatter | solution.py:747
  921.2 36.5 %collective-permute-start.56 = (bf16[128,2176]{1,0:T(8,128)(2,1)}, bf16[128,2176]{1,0:T(8,128)(2,1)}, u32[]{:S(2)}, u32[]{:S(2)}) collective-permute-start(bf16[128,2176]{1,0:T(8,128)(2,1)} %get-tuple-element.286), channel_id=1, source_target_pairs={{0,16},{4,20},{8,24},{12,28},{16,0},{20,4},{24,8},{28,12},{1,17},{... | collective-permute-start | bytes 1671176 | tf_op jit(solution)/shard_map/ppermute | solution.py:411
  922.8 34.9 %collective-permute-start.55 = (bf16[128,2176]{1,0:T(8,128)(2,1)}, bf16[128,2176]{1,0:T(8,128)(2,1)}, u32[]{:S(2)}, u32[]{:S(2)}) collective-permute-start(bf16[128,2176]{1,0:T(8,128)(2,1)} %get-tuple-element.287), channel_id=1, source_target_pairs={{0,8},{4,12},{8,0},{12,4},{16,24},{20,28},{24,16},{28,20},{1,9},{5... | collective-permute-start | bytes 1671176 | tf_op jit(solution)/shard_map/ppermute | solution.py:411
  1009.9 35.2 %collective-permute-start.45 = (bf16[64,2048]{1,0:T(8,128)(2,1)S(1)}, bf16[64,2048]{1,0:T(8,128)(2,1)}, u32[]{:S(2)}, u32[]{:S(2)}) collective-permute-start(bf16[64,2048]{1,0:T(8,128)(2,1)S(1)} %get-tuple-element.298), channel_id=1, source_target_pairs={{0,2},{1,3},{2,0},{3,1},{4,6},{5,7},{6,4},{7,5},{8,10},{9,11},{10,... | collective-permute-start | bytes 786440 | tf_op jit(solution)/shard_map/ppermute | solution.py:365
  1010.8 36.8 %collective-permute-start.44 = (bf16[64,2048]{1,0:T(8,128)(2,1)S(1)}, bf16[64,2048]{1,0:T(8,128)(2,1)}, u32[]{:S(2)}, u32[]{:S(2)}) collective-permute-start(bf16[64,2048]{1,0:T(8,128)(2,1)S(1)} %get-tuple-element.299), channel_id=1, source_target_pairs={{0,3},{1,0},{2,1},{3,2},{4,7},{5,4},{6,5},{7,6},{8,11},{9,8},{10,9... | collective-permute-start | bytes 786440 | tf_op jit(solution)/shard_map/ppermute | solution.py:365
  1016.6 37.6 %collective-permute-start.49 = (bf16[64,2048]{1,0:T(8,128)(2,1)}, bf16[64,2048]{1,0:T(8,128)(2,1)}, u32[]{:S(2)}, u32[]{:S(2)}) collective-permute-start(bf16[64,2048]{1,0:T(8,128)(2,1)} %get-tuple-element.293), channel_id=1, source_target_pairs={{0,1},{1,2},{2,3},{3,0},{4,5},{5,6},{6,7},{7,4},{8,9},{9,10},{10,1... | collective-permute-start | bytes 786440 | tf_op jit(solution)/shard_map/ppermute | solution.py:365
  (182 other events, 3564.4 us)
Sparse Core Ops, SparseCore 0:
  9.9 68.7 all-gather.7
  81.1 58.7 all-gather.9
  142.4 54.3 all-gather.11
  368.0 70.5 all-gather.15
  444.2 55.3 all-gather.13
  508.8 76.1 reduce-scatter.4
  588.6 73.7 reduce-scatter.6
  664.9 36.6 all-gather.17
  711.9 36.7 all-gather.19
  752.1 115.9 reduce-scatter.8
  878.2 109.7 reduce-scatter.10
